TPU v7x, 256 devices: a whole 4x4x8 slice. The times are simulated.
256 devices in a mesh: dom: 256 (over y, z, x, core).
Axes of the slice: x: 4, y: 4, z: 8, core: 2. Of those that a mesh axis runs over, the one named last changes fastest.
Arguments:
- thickness: float32 [80, 425984], P(None, 'dom'), may hold values from 0.5 to 2
- tracer: float32 [80, 425984], P(None, 'dom'), may hold values from -6 to 6
- velocity: float32 [80, 1277952], P(None, 'dom'), may hold values from -6 to 6
- active_levels: int32 [425984], P('dom'), may hold values from 1 to 80
- gradient_tiles: bfloat16 [9984, 2, 128, 128], P('dom'), may hold values from -0.375 to 0.375
- average_tiles: bfloat16 [9984, 2, 128, 128], P('dom'), may hold values from -0.375 to 0.375
- edge_sources: int32 [9984, 2], P('dom'), may hold values from 0 to 3327, as said below
- divergence_tiles: bfloat16 [3328, 6, 128, 128], P('dom'), may hold values from -0.21875 to 0.21875
- cell_sources: int32 [3328, 6], P('dom'), may hold values from 0 to 9983, as said below
Outputs:
- new_thickness: float32 [80, 425984], P(None, 'dom')
- new_tracer: float32 [80, 425984], P(None, 'dom')
- new_velocity: float32 [80, 1277952], P(None, 'dom')
Inputs may be any that keep to these rules, and one draw needn't show every extreme that they name: `edge_sources`: entry 0 of the row of edge block e is e // 3; every other entry is e // 3 - 1 or e // 3 + 1 modulo 3328. `cell_sources`: entries 0, 1, 2 of the row of cell block b are 3b, 3b+1, 3b+2; every other entry is 3c, 3c+1 or 3c+2 with c = b - 1 or b + 1 modulo 3328.
All inputs are finite; a program needn't handle non-finite values.
Results may differ from a plain program's by a relative error of at most 0.0009.
Values may be sent and summed in bfloat16 or wider, within the bound.
No kernel may reach another device: no remote copies, remote signals or barrier semaphores. Data moves between devices by JAX's collectives and lax.ppermute only.
A program may use at most 128 MiB of HBM per device.

v0:
```python
import jax
import jax.numpy as jnp
from jax import lax
from jax.sharding import PartitionSpec as P

buoyancy = 0.2
drag_rate = 0.5
time_step = 0.25


def with_halo(array, sides, width):
    for axis, dim in sides:
        devices, length = (lax.axis_size(axis), array.shape[dim])
        up = [(i, (i + 1) % devices) for i in range(devices)]
        down = [(j, i) for i, j in up]
        last = lax.slice_in_dim(array, length - width, length, axis=dim)
        initial = lax.slice_in_dim(array, 0, width, axis=dim)
        before = lax.ppermute(last, axis, up)
        after = lax.ppermute(initial, axis, down)
        array = jnp.concatenate([before, array, after], axis=dim)
    return array


def block_apply(values, tiles, local_sources):
    height = values.shape[0]
    tile_size = tiles.shape[-1]
    blocks = values.reshape(height, -1, tile_size)
    picked = blocks[:, local_sources, :]
    result = jnp.einsum("rokc,okcf->rof", picked, tiles, preferred_element_type=jnp.float32)
    return result.reshape(height, tiles.shape[0] * tile_size)


def cell_mask(active, levels):
    return (jnp.arange(levels, dtype=jnp.int32)[:, None] < active[None, :]).astype(jnp.float32)


def edge_mask(mask, tile_size):
    levels = mask.shape[0]
    per_cell = mask.reshape(levels, -1, 1, tile_size)
    return jnp.broadcast_to(per_cell, (levels, per_cell.shape[1], 3, tile_size)).reshape(levels, -1)


def pressure(thickness_now, tracer_now, mask):
    weight = thickness_now * (1.0 - buoyancy * tracer_now) * mask
    return (jnp.cumsum(weight, axis=0) - 0.5 * weight) / weight.shape[0]


def advance(anchor, current, slope, keep_share):
    return keep_share * anchor + (1.0 - keep_share) * (current + time_step * slope)


def local(
    thickness,
    tracer,
    velocity,
    active_levels,
    gradient_tiles,
    average_tiles,
    edge_sources,
    divergence_tiles,
    cell_sources,
):
    levels = thickness.shape[0]
    tile_size = gradient_tiles.shape[-1]
    own_blocks = cell_sources.shape[0]
    devices = lax.axis_size("dom")
    position = lax.axis_index("dom")
    total_blocks = own_blocks * devices
    first_block = position * own_blocks
    depth_rim = 1
    wide_levels = with_halo(active_levels, (("dom", 0),), depth_rim * tile_size)
    wide_mask = cell_mask(wide_levels, levels)
    own_mask = wide_mask[:, depth_rim * tile_size : (depth_rim + own_blocks) * tile_size]
    own_edge_mask = edge_mask(own_mask, tile_size)
    divergence_local = jnp.mod(cell_sources - 3 * (first_block - 1), 3 * total_blocks)
    gradient_local = jnp.mod(edge_sources - (first_block - 1), total_blocks)
    anchor = (thickness, tracer, velocity)
    keep_shares = (0.0, 0.75, 1.0 / 3.0)
    current = anchor
    for section_index in range(3):
        velocity_now = current[2]
        stacked = jnp.concatenate([current[0], current[1]], axis=0)
        wide_state = with_halo(stacked.astype(jnp.bfloat16), (("dom", 1),), tile_size).astype(
            stacked.dtype
        )
        pressures = pressure(wide_state[:levels], wide_state[levels:], wide_mask).astype(
            jnp.bfloat16
        )
        gradient = block_apply(pressures, gradient_tiles, gradient_local)
        edge_values = block_apply(wide_state.astype(jnp.bfloat16), average_tiles, gradient_local)
        d_velocity = (-gradient - drag_rate * velocity_now) * own_edge_mask
        moving = velocity_now * own_edge_mask
        fluxes = jnp.concatenate(
            [edge_values[:levels] * moving, edge_values[levels:] * moving], axis=0
        ).astype(jnp.bfloat16)
        tendencies_wide_flux = with_halo(fluxes, (("dom", 1),), 3 * tile_size)
        spread = block_apply(tendencies_wide_flux, divergence_tiles, divergence_local)
        d_thickness = -spread[:levels] * own_mask
        d_tracer = -spread[levels:] * own_mask
        slopes = (d_thickness, d_tracer, d_velocity)
        current = tuple(
            (
                advance(anchor[field], current[field], slopes[field], keep_shares[section_index])
                for field in range(3)
            )
        )
    return (current[0], current[1], current[2])


def solution(mesh):
    return jax.shard_map(
        local,
        mesh=mesh,
        in_specs=(
            P(None, "dom"),
            P(None, "dom"),
            P(None, "dom"),
            P("dom"),
            P("dom", None, None, None),
            P("dom", None, None, None),
            P("dom", None),
            P("dom", None, None, None),
            P("dom", None),
        ),
        out_specs=(P(None, "dom"), P(None, "dom"), P(None, "dom")),
        check_vma=False,
    )
```

profile of v0, /device:TPU:0, one launch (start us, length us, event | category | flops | bytes accessed | tf_op | source)
XLA Modules:
  0.0 171.9 jit_solution(13639085919402614739)
XLA Ops:
  3.1 8.3 %collective-permute-start.3 = (bf16[160,128]{1,0:T(8,128)(2,1)S(1)}, bf16[160,128]{1,0:T(8,128)(2,1)S(1)}, u32[]{:S(2)}, u32[]{:S(2)}) collective-permute-start(bf16[160,128]{1,0:T(8,128)(2,1)S(1)} %get-tuple-element.39), channel_id=1, source_target_pairs={{1,0},{2,1},{3,2},{4,3},{5,4},{6,5},{7,6},{8,7},{9,8},{10,9},{11,1... | collective-permute-start | bytes 122888 | tf_op jit(solution)/shard_map/ppermute | solution.py:19
  11.4 7.2 %collective-permute-start.1 = (s32[128]{0:T(128)S(1)}, s32[128]{0:T(128)S(1)}, u32[]{:S(2)}, u32[]{:S(2)}) collective-permute-start(s32[128]{0:T(128)S(1)} %get-tuple-element.49), channel_id=1, source_target_pairs={{1,0},{2,1},{3,2},{4,3},{5,4},{6,5},{7,6},{8,7},{9,8},{10,9},{11,1... | collective-permute-start | bytes 1544 | tf_op jit(solution)/shard_map/ppermute | solution.py:19
  25.6 3.7 %reshape.70 = f32[80,4992]{1,0:T(8,128)} reshape(f32[80,13,3,128]{3,2,1,0:T(4,128)} %broadcast_in_dim.28) | data formatting | bytes 3194880 | tf_op jit(solution)/shard_map/reshape | solution.py:40
  30.6 2.9 %gather_fusion = bf16[78,160,128]{2,1,0:T(8,128)(2,1)} fusion(bf16[160,15,128]{2,0,1:T(8,128)(2,1)S(1)} %bitcast.326, s32[1024]{0:T(1024)S(1)} %pad_clamp_fusion.1), kind=kCustom, calls=%fused_computation | custom fusion | bytes 6390072 | tf_op jit(solution)/shard_map/gather | solution.py:28
  33.4 2.9 %convolution_bitcast_fusion.2 = f32[160,39,128]{2,0,1:T(8,128)S(1)} fusion(bf16[160,39,2,128]{3,0,2,1:T(8,128)(2,1)} %bitcast.332, bf16[39,2,128,128]{3,2,1,0:T(8,128)(2,1)S(1)} %copy-done), kind=kOutput, calls=%fused_computation.11 | convolution fusion | flops 408944640 | bytes 8945664 | tf_op jit(solution)/shard_map/rokc,okcf->rof/dot_general | solution.py:29
  40.2 7.2 %collective-permute-start.5 = (bf16[160,384]{1,0:T(8,128)(2,1)S(1)}, bf16[160,384]{1,0:T(8,128)(2,1)}, u32[]{:S(2)}, u32[]{:S(2)}) collective-permute-start(bf16[160,384]{1,0:T(8,128)(2,1)S(1)} %get-tuple-element.21), channel_id=1, source_target_pairs={{1,0},{2,1},{3,2},{4,3},{5,4},{6,5},{7,6},{8,7},{9,8},{10,9},{11,1... | collective-permute-start | bytes 368648 | tf_op jit(solution)/shard_map/ppermute | solution.py:19
  52.6 3.0 %copy_bitcast_fusion.2 = bf16[160,45,128]{2,0,1:T(8,128)(2,1)} fusion(bf16[160,384]{1,0:T(8,128)(2,1)} %collective-permute-done.5, bf16[80,4992]{1,0:T(8,128)(2,1)} %copy-done.24, bf16[80,4992]{1,0:T(8,128)(2,1)} %copy-done.23, bf16[160,384]{1,0:T(8,128)(2,1)} %collective-permute-done.4), kind=kLoop, calls=%fused_computation.14 | loop fusion | flops 7372800 | bytes 3686400 | tf_op jit(solution)/shard_map/reshape | solution.py:27
  55.6 4.4 %gather_fusion.1 = bf16[78,160,128]{2,1,0:T(8,128)(2,1)} fusion(bf16[160,45,128]{2,0,1:T(8,128)(2,1)} %copy_bitcast_fusion.2, s32[1024]{0:T(1024)S(1)} %pad_clamp_fusion), kind=kCustom, calls=%fused_computation.1 | custom fusion | bytes 6390072 | tf_op jit(solution)/shard_map/gather | solution.py:28
  59.9 3.7 %convolution_bitcast_fusion.5 = f32[160,13,128]{2,0,1:T(8,128)S(1)} fusion(bf16[160,13,6,128]{3,0,2,1:T(8,128)(2,1)} %bitcast.330, bf16[13,6,128,128]{3,2,1,0:T(8,128)(2,1)} %param.16), kind=kOutput, calls=%fused_computation.62 | convolution fusion | flops 408944640 | bytes 6815744 | tf_op jit(solution)/shard_map/rokc,okcf->rof/dot_general | solution.py:29
  65.6 7.2 %collective-permute-start.7 = (bf16[160,128]{1,0:T(8,128)(2,1)S(1)}, bf16[160,128]{1,0:T(8,128)(2,1)S(1)}, u32[]{:S(2)}, u32[]{:S(2)}) collective-permute-start(bf16[160,128]{1,0:T(8,128)(2,1)S(1)} %get-tuple-element.37), channel_id=1, source_target_pairs={{1,0},{2,1},{3,2},{4,3},{5,4},{6,5},{7,6},{8,7},{9,8},{10,9},{11,1... | collective-permute-start | bytes 122888 | tf_op jit(solution)/shard_map/ppermute | solution.py:19
  75.9 2.9 %gather_fusion.2 = bf16[78,160,128]{2,1,0:T(8,128)(2,1)} fusion(bf16[160,15,128]{2,0,1:T(8,128)(2,1)S(1)} %bitcast.327, s32[1024]{0:T(1024)S(1)} %pad_clamp_fusion.1), kind=kCustom, calls=%fused_computation.2 | custom fusion | bytes 6390072 | tf_op jit(solution)/shard_map/gather | solution.py:28
  78.8 2.9 %convolution_bitcast_fusion.1 = f32[160,39,128]{2,0,1:T(8,128)S(1)} fusion(bf16[160,39,2,128]{3,0,2,1:T(8,128)(2,1)} %bitcast.333, bf16[39,2,128,128]{3,2,1,0:T(8,128)(2,1)S(1)} %copy-done), kind=kOutput, calls=%fused_computation.10 | convolution fusion | flops 408944640 | bytes 8945664 | tf_op jit(solution)/shard_map/rokc,okcf->rof/dot_general | solution.py:29
  84.9 7.3 %collective-permute-start.9 = (bf16[160,384]{1,0:T(8,128)(2,1)S(1)}, bf16[160,384]{1,0:T(8,128)(2,1)S(1)}, u32[]{:S(2)}, u32[]{:S(2)}) collective-permute-start(bf16[160,384]{1,0:T(8,128)(2,1)S(1)} %get-tuple-element.19), channel_id=1, source_target_pairs={{1,0},{2,1},{3,2},{4,3},{5,4},{6,5},{7,6},{8,7},{9,8},{10,9},{11,1... | collective-permute-start | bytes 368648 | tf_op jit(solution)/shard_map/ppermute | solution.py:19
  96.3 4.4 %gather_fusion.4 = bf16[78,160,128]{2,1,0:T(8,128)(2,1)} fusion(bf16[160,45,128]{2,0,1:T(8,128)(2,1)} %copy_bitcast_fusion.1, s32[1024]{0:T(1024)S(1)} %pad_clamp_fusion), kind=kCustom, calls=%fused_computation.4 | custom fusion | bytes 6390072 | tf_op jit(solution)/shard_map/gather | solution.py:28
  100.6 3.7 %convolution_bitcast_fusion.4 = f32[160,13,128]{2,0,1:T(8,128)S(1)} fusion(bf16[160,13,6,128]{3,0,2,1:T(8,128)(2,1)} %bitcast.331, bf16[13,6,128,128]{3,2,1,0:T(8,128)(2,1)} %param.16), kind=kOutput, calls=%fused_computation.61 | convolution fusion | flops 408944640 | bytes 6815744 | tf_op jit(solution)/shard_map/rokc,okcf->rof/dot_general | solution.py:29
  106.8 7.4 %collective-permute-start.11 = (bf16[160,128]{1,0:T(8,128)(2,1)S(1)}, bf16[160,128]{1,0:T(8,128)(2,1)S(1)}, u32[]{:S(2)}, u32[]{:S(2)}) collective-permute-start(bf16[160,128]{1,0:T(8,128)(2,1)S(1)} %get-tuple-element.35), channel_id=1, source_target_pairs={{1,0},{2,1},{3,2},{4,3},{5,4},{6,5},{7,6},{8,7},{9,8},{10,9},{11,1... | collective-permute-start | bytes 122888 | tf_op jit(solution)/shard_map/ppermute | solution.py:19
  117.3 2.9 %gather_fusion.5 = bf16[78,160,128]{2,1,0:T(8,128)(2,1)} fusion(bf16[160,15,128]{2,0,1:T(8,128)(2,1)S(1)} %bitcast.328, s32[1024]{0:T(1024)S(1)} %pad_clamp_fusion.1), kind=kCustom, calls=%fused_computation.5 | custom fusion | bytes 6390072 | tf_op jit(solution)/shard_map/gather | solution.py:28
  120.1 2.9 %convolution_bitcast_fusion = f32[160,39,128]{2,0,1:T(8,128)S(1)} fusion(bf16[160,39,2,128]{3,0,2,1:T(8,128)(2,1)} %bitcast.334, bf16[39,2,128,128]{3,2,1,0:T(8,128)(2,1)S(1)} %copy-done), kind=kOutput, calls=%fused_computation.9 | convolution fusion | flops 408944640 | bytes 8945664 | tf_op jit(solution)/shard_map/rokc,okcf->rof/dot_general | solution.py:29
  135.2 4.1 %fusion.21 = f32[39,10,8,128]{3,2,1,0:T(8,128)} fusion(bf16[80,39,2,128]{3,0,2,1:T(8,128)(2,1)} %bitcast.339, bf16[39,2,128,128]{3,2,1,0:T(8,128)(2,1)} %param.13), kind=kOutput, calls=%fused_computation.56 | convolution fusion | flops 204871680 | bytes 5750784 | tf_op jit(solution)/shard_map/rokc,okcf->rof/dot_general | solution.py:29
  141.3 3.0 %fusion.20 = f32[39,10,8,128]{3,2,1,0:T(8,128)S(1)} fusion(bf16[80,39,2,128]{3,0,2,1:T(8,128)(2,1)} %bitcast.338, bf16[39,2,128,128]{3,2,1,0:T(8,128)(2,1)} %param.13), kind=kOutput, calls=%fused_computation.54 | convolution fusion | flops 204871680 | bytes 5750784 | tf_op jit(solution)/shard_map/rokc,okcf->rof/dot_general | solution.py:29
  145.0 4.0 %fusion.4 = (f32[80,4992]{1,0:T(8,128)}, bf16[80,4992]{1,0:T(8,128)(2,1)S(1)}, bf16[80,4992]{1,0:T(8,128)(2,1)S(1)}) fusion(f32[80,4992]{1,0:T(8,128)S(1)} %copy-done.3, f32[39,10,8,128]{3,2,1,0:T(8,128)S(1)} %fusion.20, f32[80,4992]{1,0:T(8,128)S(1)} %copy-done.7, f32[39,10,8,128]{3,2,1,0:T(8,128)} %fusion.21, f32[39,10,8,128]{3,2,1,0:T(8,128)S(1)} %copy-done.9, ...), kind=kLoop, calls=%fused_computation.23 | loop fusion | flops 11182080 | bytes 14376960 | tf_op jit(solution)/shard_map/add | solution.py:49
  149.1 7.5 %collective-permute-start.13 = (bf16[160,384]{1,0:T(8,128)(2,1)S(1)}, bf16[160,384]{1,0:T(8,128)(2,1)S(1)}, u32[]{:S(2)}, u32[]{:S(2)}) collective-permute-start(bf16[160,384]{1,0:T(8,128)(2,1)S(1)} %get-tuple-element.17), channel_id=1, source_target_pairs={{1,0},{2,1},{3,2},{4,3},{5,4},{6,5},{7,6},{8,7},{9,8},{10,9},{11,1... | collective-permute-start | bytes 368648 | tf_op jit(solution)/shard_map/ppermute | solution.py:19
  160.7 4.4 %gather_fusion.7 = bf16[78,160,128]{2,1,0:T(8,128)(2,1)} fusion(bf16[160,45,128]{2,0,1:T(8,128)(2,1)} %copy_bitcast_fusion, s32[1024]{0:T(1024)S(1)} %pad_clamp_fusion), kind=kCustom, calls=%fused_computation.7 | custom fusion | bytes 6390072 | tf_op jit(solution)/shard_map/gather | solution.py:28
  165.0 3.8 %convolution_bitcast_fusion.3 = f32[160,13,128]{2,0,1:T(8,128)S(1)} fusion(bf16[160,13,6,128]{3,0,2,1:T(8,128)(2,1)} %bitcast.329, bf16[13,6,128,128]{3,2,1,0:T(8,128)(2,1)} %param.16), kind=kOutput, calls=%fused_computation.60 | convolution fusion | flops 408944640 | bytes 6815744 | tf_op jit(solution)/shard_map/rokc,okcf->rof/dot_general | solution.py:29
  (147 shorter events, 59.6 us)
Async XLA Ops:
  0.6 32.8 %copy-start = (bf16[39,2,128,128]{3,2,1,0:T(8,128)(2,1)S(1)}, bf16[39,2,128,128]{3,2,1,0:T(8,128)(2,1)}, u32[]{:S(2)}) copy-start(bf16[39,2,128,128]{3,2,1,0:T(8,128)(2,1)} %param.14) | copy-start | bytes 7667716
  0.6 10.7 %copy-start.33 = (s32[1664]{0:T(1024)S(1)}, s32[1664]{0:T(1024)}, u32[]{:S(2)}) copy-start(s32[1664]{0:T(1024)} %param.12) | copy-start | bytes 19972
  0.7 17.9 %copy-start.35 = (s32[39,2]{0,1:T(2,128)S(1)}, s32[39,2]{0,1:T(2,128)}, u32[]{:S(2)}) copy-start(s32[39,2]{0,1:T(2,128)} %param.15) | copy-start | bytes 940
  0.7 18.1 %copy-start.34 = (s32[13,6]{0,1:T(8,128)S(1)}, s32[13,6]{0,1:T(8,128)}, u32[]{:S(2)}) copy-start(s32[13,6]{0,1:T(8,128)} %param.17) | copy-start | bytes 940
  3.0 26.2 %collective-permute-start.2 = (bf16[160,128]{1,0:T(8,128)(2,1)S(1)}, bf16[160,128]{1,0:T(8,128)(2,1)S(1)}, u32[]{:S(2)}, u32[]{:S(2)}) collective-permute-start(bf16[160,128]{1,0:T(8,128)(2,1)S(1)} %get-tuple-element.38), channel_id=1, source_target_pairs={{0,1},{1,2},{2,3},{3,4},{4,5},{5,6},{6,7},{7,8},{8,9},{9,10},{10,1... | collective-permute-start | bytes 122888 | tf_op jit(solution)/shard_map/ppermute | solution.py:18
  3.1 26.1 %collective-permute-start.3 = (bf16[160,128]{1,0:T(8,128)(2,1)S(1)}, bf16[160,128]{1,0:T(8,128)(2,1)S(1)}, u32[]{:S(2)}, u32[]{:S(2)}) collective-permute-start(bf16[160,128]{1,0:T(8,128)(2,1)S(1)} %get-tuple-element.39), channel_id=1, source_target_pairs={{1,0},{2,1},{3,2},{4,3},{5,4},{6,5},{7,6},{8,7},{9,8},{10,9},{11,1... | collective-permute-start | bytes 122888 | tf_op jit(solution)/shard_map/ppermute | solution.py:19
  11.4 8.4 %collective-permute-start = (s32[128]{0:T(128)S(1)}, s32[128]{0:T(128)S(1)}, u32[]{:S(2)}, u32[]{:S(2)}) collective-permute-start(s32[128]{0:T(128)S(1)} %get-tuple-element.48), channel_id=1, source_target_pairs={{0,1},{1,2},{2,3},{3,4},{4,5},{5,6},{6,7},{7,8},{8,9},{9,10},{10,1... | collective-permute-start | bytes 1544 | tf_op jit(solution)/shard_map/ppermute | solution.py:18
  11.4 8.5 %collective-permute-start.1 = (s32[128]{0:T(128)S(1)}, s32[128]{0:T(128)S(1)}, u32[]{:S(2)}, u32[]{:S(2)}) collective-permute-start(s32[128]{0:T(128)S(1)} %get-tuple-element.49), channel_id=1, source_target_pairs={{1,0},{2,1},{3,2},{4,3},{5,4},{6,5},{7,6},{8,7},{9,8},{10,9},{11,1... | collective-permute-start | bytes 1544 | tf_op jit(solution)/shard_map/ppermute | solution.py:19
  38.7 8.7 %copy-start.10 = (f32[160,1920]{1,0:T(8,128)S(1)}, f32[160,1920]{1,0:T(8,128)}, u32[]{:S(2)}) copy-start(f32[160,1920]{1,0:T(8,128)} %get-tuple-element.32) | copy-start | bytes 3686404
  40.2 12.3 %collective-permute-start.4 = (bf16[160,384]{1,0:T(8,128)(2,1)}, bf16[160,384]{1,0:T(8,128)(2,1)}, u32[]{:S(2)}, u32[]{:S(2)}) collective-permute-start(bf16[160,384]{1,0:T(8,128)(2,1)} %get-tuple-element.20), channel_id=1, source_target_pairs={{0,1},{1,2},{2,3},{3,4},{4,5},{5,6},{6,7},{7,8},{8,9},{9,10},{10,1... | collective-permute-start | bytes 368648 | tf_op jit(solution)/shard_map/ppermute | solution.py:18
  40.2 12.3 %collective-permute-start.5 = (bf16[160,384]{1,0:T(8,128)(2,1)S(1)}, bf16[160,384]{1,0:T(8,128)(2,1)}, u32[]{:S(2)}, u32[]{:S(2)}) collective-permute-start(bf16[160,384]{1,0:T(8,128)(2,1)S(1)} %get-tuple-element.21), channel_id=1, source_target_pairs={{1,0},{2,1},{3,2},{4,3},{5,4},{6,5},{7,6},{8,7},{9,8},{10,9},{11,1... | collective-permute-start | bytes 368648 | tf_op jit(solution)/shard_map/ppermute | solution.py:19
  63.6 9.1 %copy-start.25 = (bf16[78,80,128]{2,1,0:T(8,128)(2,1)S(1)}, bf16[78,80,128]{2,1,0:T(8,128)(2,1)}, u32[]{:S(2)}) copy-start(bf16[78,80,128]{2,1,0:T(8,128)(2,1)} %gather_fusion.3) | copy-start | bytes 4792324
  65.2 7.6 %copy-start.4 = (bf16[39,2,128,128]{3,2,1,0:T(8,128)(2,1)S(1)}, bf16[39,2,128,128]{3,2,1,0:T(8,128)(2,1)}, u32[]{:S(2)}) copy-start(bf16[39,2,128,128]{3,2,1,0:T(8,128)(2,1)} %param.13) | copy-start | bytes 7667716
  65.5 9.1 %collective-permute-start.6 = (bf16[160,128]{1,0:T(8,128)(2,1)S(1)}, bf16[160,128]{1,0:T(8,128)(2,1)S(1)}, u32[]{:S(2)}, u32[]{:S(2)}) collective-permute-start(bf16[160,128]{1,0:T(8,128)(2,1)S(1)} %get-tuple-element.36), channel_id=1, source_target_pairs={{0,1},{1,2},{2,3},{3,4},{4,5},{5,6},{6,7},{7,8},{8,9},{9,10},{10,1... | collective-permute-start | bytes 122888 | tf_op jit(solution)/shard_map/ppermute | solution.py:18
  65.6 9.0 %collective-permute-start.7 = (bf16[160,128]{1,0:T(8,128)(2,1)S(1)}, bf16[160,128]{1,0:T(8,128)(2,1)S(1)}, u32[]{:S(2)}, u32[]{:S(2)}) collective-permute-start(bf16[160,128]{1,0:T(8,128)(2,1)S(1)} %get-tuple-element.37), channel_id=1, source_target_pairs={{1,0},{2,1},{3,2},{4,3},{5,4},{6,5},{7,6},{8,7},{9,8},{10,9},{11,1... | collective-permute-start | bytes 122888 | tf_op jit(solution)/shard_map/ppermute | solution.py:19
  84.8 9.8 %collective-permute-start.8 = (bf16[160,384]{1,0:T(8,128)(2,1)S(1)}, bf16[160,384]{1,0:T(8,128)(2,1)S(1)}, u32[]{:S(2)}, u32[]{:S(2)}) collective-permute-start(bf16[160,384]{1,0:T(8,128)(2,1)S(1)} %get-tuple-element.18), channel_id=1, source_target_pairs={{0,1},{1,2},{2,3},{3,4},{4,5},{5,6},{6,7},{7,8},{8,9},{9,10},{10,1... | collective-permute-start | bytes 368648 | tf_op jit(solution)/shard_map/ppermute | solution.py:18
  84.9 9.8 %collective-permute-start.9 = (bf16[160,384]{1,0:T(8,128)(2,1)S(1)}, bf16[160,384]{1,0:T(8,128)(2,1)S(1)}, u32[]{:S(2)}, u32[]{:S(2)}) collective-permute-start(bf16[160,384]{1,0:T(8,128)(2,1)S(1)} %get-tuple-element.19), channel_id=1, source_target_pairs={{1,0},{2,1},{3,2},{4,3},{5,4},{6,5},{7,6},{8,7},{9,8},{10,9},{11,1... | collective-permute-start | bytes 368648 | tf_op jit(solution)/shard_map/ppermute | solution.py:19
  106.7 9.1 %collective-permute-start.10 = (bf16[160,128]{1,0:T(8,128)(2,1)S(1)}, bf16[160,128]{1,0:T(8,128)(2,1)S(1)}, u32[]{:S(2)}, u32[]{:S(2)}) collective-permute-start(bf16[160,128]{1,0:T(8,128)(2,1)S(1)} %get-tuple-element.34), channel_id=1, source_target_pairs={{0,1},{1,2},{2,3},{3,4},{4,5},{5,6},{6,7},{7,8},{8,9},{9,10},{10,1... | collective-permute-start | bytes 122888 | tf_op jit(solution)/shard_map/ppermute | solution.py:18
  106.8 9.0 %collective-permute-start.11 = (bf16[160,128]{1,0:T(8,128)(2,1)S(1)}, bf16[160,128]{1,0:T(8,128)(2,1)S(1)}, u32[]{:S(2)}, u32[]{:S(2)}) collective-permute-start(bf16[160,128]{1,0:T(8,128)(2,1)S(1)} %get-tuple-element.35), channel_id=1, source_target_pairs={{1,0},{2,1},{3,2},{4,3},{5,4},{6,5},{7,6},{8,7},{9,8},{10,9},{11,1... | collective-permute-start | bytes 122888 | tf_op jit(solution)/shard_map/ppermute | solution.py:19
  135.2 4.1 %copy-start.32 = (bf16[10,15,8,128]{3,2,1,0:T(8,128)(2,1)S(1)}, bf16[10,15,8,128]{3,2,1,0:T(8,128)(2,1)}, u32[]{:S(2)}) copy-start(bf16[10,15,8,128]{3,2,1,0:T(8,128)(2,1)} %get-tuple-element.51) | copy-start | bytes 921604
  149.0 9.8 %collective-permute-start.12 = (bf16[160,384]{1,0:T(8,128)(2,1)S(1)}, bf16[160,384]{1,0:T(8,128)(2,1)S(1)}, u32[]{:S(2)}, u32[]{:S(2)}) collective-permute-start(bf16[160,384]{1,0:T(8,128)(2,1)S(1)} %get-tuple-element.16), channel_id=1, source_target_pairs={{0,1},{1,2},{2,3},{3,4},{4,5},{5,6},{6,7},{7,8},{8,9},{9,10},{10,1... | collective-permute-start | bytes 368648 | tf_op jit(solution)/shard_map/ppermute | solution.py:18
  149.1 10.0 %collective-permute-start.13 = (bf16[160,384]{1,0:T(8,128)(2,1)S(1)}, bf16[160,384]{1,0:T(8,128)(2,1)S(1)}, u32[]{:S(2)}, u32[]{:S(2)}) collective-permute-start(bf16[160,384]{1,0:T(8,128)(2,1)S(1)} %get-tuple-element.17), channel_id=1, source_target_pairs={{1,0},{2,1},{3,2},{4,3},{5,4},{6,5},{7,6},{8,7},{9,8},{10,9},{11,1... | collective-permute-start | bytes 368648 | tf_op jit(solution)/shard_map/ppermute | solution.py:19
  165.0 3.9 %copy-start.29 = (f32[13,10,8,128]{3,2,1,0:T(8,128)S(1)}, f32[13,10,8,128]{3,2,1,0:T(8,128)}, u32[]{:S(2)}) copy-start(f32[13,10,8,128]{3,2,1,0:T(8,128)} %copy-done.28) | copy-start | bytes 1597444
  165.0 3.9 %copy-start.31 = (f32[13,10,8,128]{3,2,1,0:T(8,128)S(1)}, f32[13,10,8,128]{3,2,1,0:T(8,128)}, u32[]{:S(2)}) copy-start(f32[13,10,8,128]{3,2,1,0:T(8,128)} %copy-done.30) | copy-start | bytes 1597444
  (26 other events, 48.1 us)
where the time goes:
time: 173 us; the launch traced here: 172 us
  starting transfers between devices  52.4 us (30%)
  local copies, waits for them, and re-layouts  50.4 us (29%)
  other arithmetic  32 us (18%)
  matrix products  28.6 us (17%)
  waiting for transfers between devices  7.39 us (4%)
    ppermute x7, starting transfers between devices, with_halo(): after = lax.ppermute(initial, axis, down)  52 us
    dot_general x9, matrix products, block_apply(): jnp.einsum('rokc,okcf->rof', picked, tiles, preferred_element_type=jnp.fl...  28.6 us
    gather x9, local copies, waits for them, and re-layouts, block_apply(): picked = blocks[:, local_sources, :]  27.8 us
    unnamed x75, local copies, waits for them, and re-layouts  13.3 us
    reshape x4, other arithmetic, block_apply(): blocks = values.reshape(height, -1, tile_size)  7.91 us
    ppermute x7, waiting for transfers between devices, with_halo(): before = lax.ppermute(last, axis, up)  6.97 us
    add x2, other arithmetic, advance(): keep_share * anchor + (1.0 - keep_share) * (current + time_step * slope)  5.62 us
    another operation x3, other arithmetic, pressure(): return (jnp.cumsum(weight, axis=0) - 0.5 * weight) / weight.shape[0]  5.17 us
  transfers between devices with their start and end apart: 14, of which 7 were waited for; matrix products, arithmetic and copies ran while one was open for 10% of the time, Pallas kernels for 0%

commit v1 on v0

v1 whole, which is shorter than its diff:
```python
import jax
import jax.numpy as jnp
from jax import lax
from jax.experimental import pallas as pl
from jax.experimental.pallas import tpu as pltpu
from jax.sharding import PartitionSpec as P

buoyancy = 0.2
drag_rate = 0.5
time_step = 0.25
keep_shares = (0.0, 0.75, 1.0 / 3.0)

F32 = jnp.float32
BF16 = jnp.bfloat16
LEV = 80
TILE = 128
NEAR = 3 * LEV
NEXT = NEAR + 2 * LEV
MOVE = NEXT + 3 * LEV
SIDE = MOVE + 16


def lanes(block):
    return slice(block * TILE, (block + 1) * TILE)


def advance(anchor, current, slope, keep_share):
    if keep_share == 0.0:
        return current + time_step * slope
    return keep_share * anchor + (1.0 - keep_share) * (current + time_step * slope)


def block_mask(levels_ref, block):
    depth = lax.broadcasted_iota(jnp.int32, (LEV, TILE), 0)
    return (depth < levels_ref[0:1, lanes(block)]).astype(F32)


def above_weights():
    row = lax.broadcasted_iota(jnp.int32, (LEV, 3 * LEV), 0)
    column = lax.broadcasted_iota(jnp.int32, (LEV, 3 * LEV), 1)
    column = jnp.where(column >= 2 * LEV, column - 2 * LEV, jnp.where(column >= LEV, column - LEV, column))
    return jnp.where(column < row, 1.0, jnp.where(column == row, 0.5, 0.0)).astype(BF16)


def coded_block(thickness, tracer, mask, above):
    weight = thickness * (1.0 - buoyancy * tracer) * mask
    high = weight.astype(BF16)
    rest = weight - high.astype(F32)
    middle = rest.astype(BF16)
    low = (rest - middle.astype(F32)).astype(BF16)
    parts = jnp.concatenate([high, middle, low], axis=0)
    pressure = jnp.dot(above, parts, preferred_element_type=F32) * (1.0 / LEV)
    return jnp.concatenate([pressure.astype(BF16), thickness.astype(BF16), tracer.astype(BF16)], axis=0)


def near(offset, own, whole):
    return jnp.where(offset > own, offset - whole, jnp.where(offset < -(whole - own), offset + whole, offset))


def edge_step(levels_mask, first, second, gradient, average, velocity, anchor, keep_share):
    slope = jnp.dot(
        jnp.concatenate([first[:LEV], second[:LEV]], axis=1), gradient, preferred_element_type=F32
    )
    carried = jnp.dot(
        jnp.concatenate([first[LEV:], second[LEV:]], axis=1), average, preferred_element_type=F32
    )
    moving = velocity * levels_mask
    flux = jnp.concatenate([carried[:LEV] * moving, carried[LEV:] * moving], axis=0).astype(BF16)
    change = (-slope - drag_rate * velocity) * levels_mask
    return flux, advance(anchor, velocity, change, keep_share)


def cell_step(block, fluxes_ref, sources_ref, first_block, own, whole, tiles_ref):
    picked = []
    for t in range(6):
        offset = sources_ref[block, t] - 3 * first_block
        offset = jnp.where(offset > 3 * own + 2, offset - 3 * whole, jnp.where(offset < -3, offset + 3 * whole, offset))
        picked.append(fluxes_ref[offset + 3])
    return -jnp.dot(jnp.concatenate(picked, axis=1), tiles_ref[block], preferred_element_type=F32)


def other_block(sources_ref, edge, first_block, own, whole):
    offset = sources_ref[edge, 1] - first_block
    return jnp.where(offset > own, offset - whole, jnp.where(offset < -1, offset + whole, offset))


def start_kernel(own, thickness, tracer, velocity, levels, average, edge_sources, coded, inner, outer, staged):
    above = above_weights()
    position = lax.axis_index("dom")
    whole = own * lax.axis_size("dom")
    for block in range(own):
        mask = block_mask(levels, block)
        coded[block] = coded_block(thickness[:, lanes(block)], tracer[:, lanes(block)], mask, above)
    for side, block, after in ((0, 0, 1), (1, own - 1, own - 2)):
        mask = block_mask(levels, block)
        staged[side, 0:NEAR, :] = coded[block]
        staged[side, NEAR:NEXT, :] = coded[after, LEV:, :]
        for j in range(3):
            edge = 3 * block + j
            staged[side, NEXT + j * LEV : NEXT + (j + 1) * LEV, :] = (velocity[:, lanes(edge)] * mask).astype(BF16)
            staged[side, SIDE + j * 256 : SIDE + (j + 1) * 256, :] = average[edge]
        row = lax.broadcasted_iota(jnp.int32, (16, TILE), 0)
        signs = jnp.zeros((16, TILE), F32)
        for j in range(3):
            other = other_block(edge_sources, 3 * block + j, position * own, own, whole)
            signs = jnp.where(row == j, (other - block).astype(F32), signs)
        staged[side, MOVE:SIDE, :] = signs.astype(BF16)
    inner_side = 1 - lax.rem(position, 2)
    inner[...] = staged[inner_side]
    outer[...] = staged[1 - inner_side]


def inside_kernel(
    own, keep_share,
    coded, thickness, tracer, velocity, thickness0, tracer0, velocity0, levels,
    gradient, average, edge_sources, divergence, cell_sources,
    fluxes, new_coded, new_thickness, new_tracer, new_velocity,
):
    above = above_weights()
    position = lax.axis_index("dom")
    whole = own * lax.axis_size("dom")
    first_block = position * own

    for block in range(1, own - 1):
        mask = block_mask(levels, block)
        for edge in range(3 * block, 3 * block + 3):
            other = other_block(edge_sources, edge, first_block, own, whole)
            flux, updated = edge_step(
                mask, coded[block], coded[other], gradient[edge], average[edge],
                velocity[:, lanes(edge)], velocity0[:, lanes(edge)], keep_share,
            )
            fluxes[edge + 3] = flux
            new_velocity[:, lanes(edge)] = updated
    for block in range(2, own - 2):
        finish_cell(
            block, own, keep_share, above, first_block, whole,
            thickness, tracer, thickness0, tracer0, levels, divergence, cell_sources,
            fluxes, new_coded, new_thickness, new_tracer,
        )


def finish_cell(
    block, own, keep_share, above, first_block, whole,
    thickness, tracer, thickness0, tracer0, levels, divergence, cell_sources,
    fluxes, new_coded, new_thickness, new_tracer,
):
    at = lanes(block)
    mask = block_mask(levels, block)
    change = cell_step(block, fluxes, cell_sources, first_block, own, whole, divergence)
    h = advance(thickness0[:, at], thickness[:, at], change[:LEV] * mask, keep_share)
    s = advance(tracer0[:, at], tracer[:, at], change[LEV:] * mask, keep_share)
    new_thickness[:, at] = h
    new_tracer[:, at] = s
    if new_coded is not None:
        new_coded[block] = coded_block(h, s, mask, above)


def rim_kernel(
    own, keep_share, last,
    inner_in, outer_in, tiles_inner, tiles_outer,
    coded, thickness, tracer, velocity, thickness0, tracer0, velocity0, levels,
    gradient, average, edge_sources, divergence, cell_sources,
    fluxes_in, new_coded_in, new_thickness_in, new_tracer_in, new_velocity_in,
    fluxes, new_coded, new_thickness, new_tracer, new_velocity,
    *rest,
):
    if last:
        halo, halo_tiles = rest
    else:
        inner, outer, halo, halo_tiles, staged = rest
    above = above_weights()
    position = lax.axis_index("dom")
    whole = own * lax.axis_size("dom")
    first_block = position * own
    inner_side = 1 - lax.rem(position, 2)
    halo[inner_side] = inner_in[0:MOVE, :]
    halo[1 - inner_side] = outer_in[0:MOVE, :]
    halo_tiles[inner_side] = tiles_inner[MOVE:, :]
    halo_tiles[1 - inner_side] = tiles_outer[MOVE:, :]

    for side, block, after in ((0, 0, 1), (1, own - 1, own - 2)):
        mask = block_mask(levels, block)
        outward = 2 * side - 1
        beyond = -1 if side == 0 else own
        signs = halo_tiles[side, 0:16, :].astype(F32)
        for j in range(3):
            edge = 3 * block + j
            other = other_block(edge_sources, edge, first_block, own, whole)
            away = jnp.full((3 * LEV, TILE), (other == beyond).astype(F32))
            second = jnp.where(away > 0.5, halo[side, 0:NEAR, :].astype(F32), coded[after].astype(F32)).astype(BF16)
            flux, updated = edge_step(
                mask, coded[block], second, gradient[edge], average[edge],
                velocity[:, lanes(edge)], velocity0[:, lanes(edge)], keep_share,
            )
            fluxes[edge + 3] = flux
            new_velocity[:, lanes(edge)] = updated
            toward = signs[j : j + 1, :] * outward
            second = jnp.where(
                jnp.broadcast_to(toward, (2 * LEV, TILE)) > 0.0,
                halo[side, NEAR:NEXT, :].astype(F32),
                coded[block, LEV:, :].astype(F32),
            ).astype(BF16)
            carried = jnp.dot(
                jnp.concatenate([halo[side, LEV:NEAR, :], second], axis=1),
                halo_tiles[side, 16 + j * 256 : 16 + (j + 1) * 256, :],
                preferred_element_type=F32,
            )
            moving = halo[side, NEXT + j * LEV : NEXT + (j + 1) * LEV, :].astype(F32)
            fluxes[3 * beyond + 3 + j] = jnp.concatenate(
                [carried[:LEV] * moving, carried[LEV:] * moving], axis=0
            ).astype(BF16)
    for block in (0, 1, own - 2, own - 1):
        finish_cell(
            block, own, keep_share, above, first_block, whole,
            thickness, tracer, thickness0, tracer0, levels, divergence, cell_sources,
            fluxes, None if last else new_coded, new_thickness, new_tracer,
        )
    if not last:
        for side, block, after in ((0, 0, 1), (1, own - 1, own - 2)):
            mask = block_mask(levels, block)
            staged[side, 0:NEAR, :] = new_coded[block]
            staged[side, NEAR:NEXT, :] = new_coded[after, LEV:, :]
            for j in range(3):
                edge = 3 * block + j
                staged[side, NEXT + j * LEV : NEXT + (j + 1) * LEV, :] = (new_velocity[:, lanes(edge)] * mask).astype(BF16)
        inner[...] = staged[inner_side]
        outer[...] = staged[1 - inner_side]


def in_vmem(array):
    return pltpu.with_memory_space_constraint(array, pltpu.VMEM)


def local(
    thickness,
    tracer,
    velocity,
    active_levels,
    gradient_tiles,
    average_tiles,
    edge_sources,
    divergence_tiles,
    cell_sources,
):
    own = cell_sources.shape[0]
    devices = lax.axis_size("dom")
    within = [(i, i ^ 1) for i in range(devices)]
    across = [(i, (i + 1) % devices if i % 2 else (i - 1) % devices) for i in range(devices)]
    cells, edges = thickness.shape[1], velocity.shape[1]
    vmem = pl.BlockSpec(memory_space=pltpu.VMEM)
    smem = pl.BlockSpec(memory_space=pltpu.SMEM)
    params = pltpu.CompilerParams(vmem_limit_bytes=16 * 1024 * 1024)

    gradient = in_vmem(gradient_tiles.reshape(3 * own, 2 * TILE, TILE))
    average = in_vmem(average_tiles.reshape(3 * own, 2 * TILE, TILE))
    divergence = in_vmem(divergence_tiles.reshape(own, 6 * TILE, TILE))
    levels = in_vmem(active_levels.reshape(1, cells))
    thickness0, tracer0, velocity0 = in_vmem(thickness), in_vmem(tracer), in_vmem(velocity)
    first_rows = SIDE + 6 * TILE

    def message(rows):
        return pltpu.VMEM((rows, TILE), BF16)

    coded, inner, outer = pl.pallas_call(
        lambda *refs: start_kernel(own, *refs),
        out_shape=(pltpu.VMEM((own, NEAR, TILE), BF16), message(first_rows), message(first_rows)),
        in_specs=[vmem] * 5 + [smem],
        out_specs=[vmem] * 3,
        scratch_shapes=[pltpu.VMEM((2, first_rows, TILE), BF16)],
        compiler_params=params,
        name="start",
    )(thickness0, tracer0, velocity0, levels, average, edge_sources)

    state = (thickness0, tracer0, velocity0)
    tiles_inner = tiles_outer = None
    for section in range(3):
        last = section == 2
        keep_share = keep_shares[section]
        inner_in = lax.ppermute(inner, "dom", within)
        outer_in = lax.ppermute(outer, "dom", across)
        if section == 0:
            tiles_inner, tiles_outer = inner_in, outer_in
        common = (coded, *state, thickness0, tracer0, velocity0, levels, gradient, average, edge_sources, divergence, cell_sources)
        common_specs = [vmem] * 10 + [smem, vmem, smem]
        kind = pltpu.VMEM
        built_shapes = (
            pltpu.VMEM((3 * own + 6, 2 * LEV, TILE), BF16),
            pltpu.VMEM((own, NEAR, TILE), BF16),
            kind((LEV, cells), F32),
            kind((LEV, cells), F32),
            kind((LEV, edges), F32),
        )
        built = pl.pallas_call(
            lambda *refs, keep_share=keep_share: inside_kernel(own, keep_share, *refs),
            out_shape=built_shapes,
            in_specs=common_specs,
            out_specs=[vmem] * 5,
            compiler_params=params,
            name="inside",
        )(*common)
        built = pl.pallas_call(
            lambda *refs, keep_share=keep_share, last=last: rim_kernel(own, keep_share, last, *refs),
            out_shape=built_shapes + (() if last else (message(MOVE), message(MOVE))),
            in_specs=[vmem] * 4 + common_specs + [vmem] * 5,
            out_specs=[vmem] * (5 if last else 7),
            scratch_shapes=[pltpu.VMEM((2, MOVE, TILE), BF16), pltpu.VMEM((2, 16 + 6 * TILE, TILE), BF16)]
            + ([] if last else [pltpu.VMEM((2, MOVE, TILE), BF16)]),
            input_output_aliases={4 + len(common) + i: i for i in range(5)},
            compiler_params=params,
            name="rim",
        )(inner_in, outer_in, tiles_inner, tiles_outer, *common, *built)
        coded = built[1]
        state = built[2:5]
        if not last:
            inner, outer = built[5], built[6]
    return state


def solution(mesh):
    return jax.shard_map(
        local,
        mesh=mesh,
        in_specs=(
            P(None, "dom"),
            P(None, "dom"),
            P(None, "dom"),
            P("dom"),
            P("dom", None, None, None),
            P("dom", None, None, None),
            P("dom", None),
            P("dom", None, None, None),
            P("dom", None),
        ),
        out_specs=(P(None, "dom"), P(None, "dom"), P(None, "dom")),
        check_vma=False,
    )
```

time: 173 us -> 62.4 us (0.36)
  starting transfers between devices: 52.4 us -> 12.6 us
  local copies, waits for them, and re-layouts: 50.4 us -> 16.7 us
  other arithmetic: 32 us -> 0 us
  matrix products: 28.6 us -> 0 us
  Pallas kernels: 0 us -> 24.4 us
    ppermute x14 -> x6, starting transfers between devices: 52.4 us -> 12.6 us  [the longest x3 12.3 us: local(): outer_in = lax.ppermute(outer, 'dom', across)]
    dot_general x9 -> x0, matrix products: 28.6 us -> none  [block_apply(): jnp.einsum('rokc,okcf->rof', picked, tiles, preferred_element_type=jnp.fl...]
    gather x9 -> x0, local copies, waits for them, and re-layouts: 27.8 us -> none  [block_apply(): picked = blocks[:, local_sources, :]]
    pallas_call x0 -> x7, Pallas kernels: none -> 24.4 us  [the longest x3 14.4 us: local(): pl.pallas_call(lambda *refs, keep_share=keep_share: inside_kernel(own, ke...]
    another operation x9 -> x0, other arithmetic: 9.3 us -> none  [the longest x3 5.17 us: pressure(): return (jnp.cumsum(weight, axis=0) - 0.5 * weight) / weight.shape[0]]
    reshape x4 -> x0, other arithmetic: 7.91 us -> none  [block_apply(): blocks = values.reshape(height, -1, tile_size)]
    add x2 -> x0, other arithmetic: 5.62 us -> none  [advance(): keep_share * anchor + (1.0 - keep_share) * (current + time_step * slope)]
    broadcast_in_dim x4 -> x0, local copies, waits for them, and re-layouts: 4.97 us -> none  [the longest x2 4.77 us: edge_mask(): jnp.broadcast_to(per_cell, (levels, per_cell.shape[1], 3, tile_size))]
  transfers between devices with their start and end apart: 14 -> 6, of which waited for: 7 -> 2; matrix products, arithmetic and copies ran while one was open for 10% -> 0% of each run, Pallas kernels for 0% -> 23%
where the time goes in v1:
time: 62.4 us; the launch traced here: 62 us
  Pallas kernels  24.4 us (39%)
  local copies, waits for them, and re-layouts  16.7 us (27%)
  starting transfers between devices  12.6 us (20%)
  waiting for transfers between devices  7.4 us (12%)
  between operations  0.76 us (1%)
    unnamed x35, local copies, waits for them, and re-layouts  16 us
    pallas_call x3, Pallas kernels, local(): pl.pallas_call(lambda *refs, keep_share=keep_share: inside_kernel(own, ke...  14.4 us
    ppermute x3, starting transfers between devices, local(): outer_in = lax.ppermute(outer, 'dom', across)  12.3 us
    pallas_call x3, Pallas kernels, local(): pl.pallas_call(lambda *refs, keep_share=keep_share, last=last: rim_kernel...  7.77 us
    ppermute x3, waiting for transfers between devices, local(): outer_in = lax.ppermute(outer, 'dom', across)  7.39 us
    pallas_call x1, Pallas kernels, local(): pl.pallas_call(lambda *refs: start_kernel(own, *refs), out_shape=(pltpu.V...  2.26 us
  transfers between devices with their start and end apart: 6, of which 2 were waited for; matrix products, arithmetic and copies ran while one was open for 0% of the time, Pallas kernels for 23%

profile of v1, /device:TPU:0, one launch (start us, length us, event | category | flops | bytes accessed | tf_op | source)
XLA Modules:
  0.0 62.0 jit_solution(11499682148861549728)
XLA Ops:
  2.1 1.4 %copy-done = f32[80,4992]{1,0:T(8,128)S(1)} copy-done((f32[80,4992]{1,0:T(8,128)S(1)}, f32[80,4992]{1,0:T(8,128)}, u32[]{:S(2)}) %copy-start) | copy-done | bytes 1597464
  3.5 1.7 %copy-done.2 = bf16[39,2,128,128]{3,2,1,0:T(8,128)(2,1)S(1)} copy-done((bf16[39,2,128,128]{3,2,1,0:T(8,128)(2,1)S(1)}, bf16[39,2,128,128]{3,2,1,0:T(8,128)(2,1)}, u32[]{:S(2)}) %copy-start.2) | copy-done | bytes 2555928
  5.2 1.0 %copy-done.8 = f32[80,1664]{1,0:T(8,128)S(1)} copy-done((f32[80,1664]{1,0:T(8,128)S(1)}, f32[80,1664]{1,0:T(8,128)}, u32[]{:S(2)}) %copy-start.8) | copy-done | bytes 532504
  6.3 1.0 %copy-done.10 = f32[80,1664]{1,0:T(8,128)S(1)} copy-done((f32[80,1664]{1,0:T(8,128)S(1)}, f32[80,1664]{1,0:T(8,128)}, u32[]{:S(2)}) %copy-start.10) | copy-done | bytes 532504
  7.3 2.3 %start.1 = (bf16[13,240,128]{2,1,0:T(8,128)(2,1)S(1)}, bf16[1424,128]{1,0:T(8,128)(2,1)}, bf16[1424,128]{1,0:T(8,128)(2,1)}) custom-call(f32[80,1664]{1,0:T(8,128)S(1)} %copy-done.8, f32[80,1664]{1,0:T(8,128)S(1)} %copy-done.10, f32[80,4992]{1,0:T(8,128)S(1)} %copy-done, s32[1,1664]{1,0:T(1,128)S(1)} %reshape.18.refs_3_.refs_7_.refs_11_, ...), custom_call_target="tpu_custom_call" | custom-call | tf_op jit(solution)/shard_map/start/pallas_call | solution.py:264
  9.6 0.9 %copy-done.12 = bf16[13,240,128]{2,1,0:T(8,128)(2,1)} copy-done((bf16[13,240,128]{2,1,0:T(8,128)(2,1)}, bf16[13,240,128]{2,1,0:T(8,128)(2,1)S(1)}, u32[]{:S(2)}) %copy-start.12) | copy-done | bytes 798744
  10.5 8.9 %collective-permute-start.1 = (bf16[1424,128]{1,0:T(8,128)(2,1)}, bf16[1424,128]{1,0:T(8,128)(2,1)S(1)}, u32[]{:S(2)}, u32[]{:S(2)}) collective-permute-start(bf16[1424,128]{1,0:T(8,128)(2,1)} %get-tuple-element.37), channel_id=1, source_target_pairs={{0,255},{1,2},{2,1},{3,4},{4,3},{5,6},{6,5},{7,8},{8,7},{9,10},{10... | collective-permute-start | bytes 1093640 | tf_op jit(solution)/shard_map/ppermute | solution.py:280
  19.5 1.7 %copy-done.3 = bf16[39,2,128,128]{3,2,1,0:T(8,128)(2,1)S(1)} copy-done((bf16[39,2,128,128]{3,2,1,0:T(8,128)(2,1)S(1)}, bf16[39,2,128,128]{3,2,1,0:T(8,128)(2,1)}, u32[]{:S(2)}) %copy-start.3) | copy-done | bytes 2555928
  21.2 1.7 %copy-done.4 = bf16[39,2,128,128]{3,2,1,0:T(8,128)(2,1)S(1)} copy-done((bf16[39,2,128,128]{3,2,1,0:T(8,128)(2,1)S(1)}, bf16[39,2,128,128]{3,2,1,0:T(8,128)(2,1)}, u32[]{:S(2)}) %copy-start.4) | copy-done | bytes 2555928
  22.9 1.7 %copy-done.6 = bf16[13,6,128,128]{3,2,1,0:T(8,128)(2,1)S(1)} copy-done((bf16[13,6,128,128]{3,2,1,0:T(8,128)(2,1)S(1)}, bf16[13,6,128,128]{3,2,1,0:T(8,128)(2,1)}, u32[]{:S(2)}) %copy-start.6) | copy-done | bytes 2555928
  24.6 1.1 %copy-done.13 = bf16[13,240,128]{2,1,0:T(8,128)(2,1)S(1)} copy-done((bf16[13,240,128]{2,1,0:T(8,128)(2,1)S(1)}, bf16[13,240,128]{2,1,0:T(8,128)(2,1)}, u32[]{:S(2)}) %copy-start.13) | copy-done | bytes 798744
  25.8 4.7 %inside.3 = (bf16[45,160,128]{2,1,0:T(8,128)(2,1)S(1)}, bf16[13,240,128]{2,1,0:T(8,128)(2,1)S(1)}, f32[80,1664]{1,0:T(8,128)S(1)}, f32[80,1664]{1,0:T(8,128)S(1)}, f32[80,4992]{1,0:T(8,128)S(1)}) custom-call(bf16[13,240,128]{2,1,0:T(8,128)(2,1)S(1)} %copy-done.13, f32[80,1664]{1,0:T(8,128)S(1)} %copy-done.9, f32[80,1664]{1,0:T(8,128)S(1)} %copy-done.11, ...), custom_call_target="tpu_custom_call" | custom-call | tf_op jit(solution)/shard_map/inside/pallas_call | solution.py:293
  30.5 2.9 %rim.3 = (bf16[45,160,128]{2,1,0:T(8,128)(2,1)S(1)}, bf16[13,240,128]{2,1,0:T(8,128)(2,1)S(1)}, f32[80,1664]{1,0:T(8,128)S(1)}, f32[80,1664]{1,0:T(8,128)S(1)}, ...) custom-call(bf16[1424,128]{1,0:T(8,128)(2,1)S(1)} %collective-permut, ...), custom_call_target="tpu_custom_call", output_to_operand_aliasing={{0}: (17, {}), {1}: (18, {}), {2}: (19, {}), {3}: (20, {}),... | custom-call | tf_op jit(solution)/shard_map/rim/pallas_call | solution.py:301
  33.5 1.4 %collective-permute-start.3 = (bf16[640,128]{1,0:T(8,128)(2,1)S(1)}, bf16[640,128]{1,0:T(8,128)(2,1)S(1)}, u32[]{:S(2)}, u32[]{:S(2)}) collective-permute-start(bf16[640,128]{1,0:T(8,128)(2,1)S(1)} %get-tuple-element.45), channel_id=1, source_target_pairs={{0,255},{1,2},{2,1},{3,4},{4,3},{5,6},{6,5},{7,8},{8,7},{9,10},{10... | collective-permute-start | bytes 491528 | tf_op jit(solution)/shard_map/ppermute | solution.py:280
  34.9 4.8 %inside.4 = (bf16[45,160,128]{2,1,0:T(8,128)(2,1)S(1)}, bf16[13,240,128]{2,1,0:T(8,128)(2,1)S(1)}, f32[80,1664]{1,0:T(8,128)S(1)}, f32[80,1664]{1,0:T(8,128)S(1)}, f32[80,4992]{1,0:T(8,128)S(1)}) custom-call(bf16[13,240,128]{2,1,0:T(8,128)(2,1)S(1)} %get-tuple-element.46.refs_0_.refs_4_, f32[80,1664]{1,0:T(8,128)S(1)} %get-tuple-element.47.refs_1_.refs_5_, ...), custom_call_target="tpu_custom_call" | custom-call | tf_op jit(solution)/shard_map/inside/pallas_call | solution.py:293
  39.8 4.0 %collective-permute-done.3.refs_1_ = bf16[640,128]{1,0:T(8,128)(2,1)S(1)} collective-permute-done((bf16[640,128]{1,0:T(8,128)(2,1)S(1)}, bf16[640,128]{1,0:T(8,128)(2,1)S(1)}, u32[]{:S(2)}, u32[]{:S(2)}) %collective-permute-start.3) | collective-permute-done | bytes 163872 | tf_op jit(solution)/shard_map/ppermute | solution.py:280
  43.8 2.9 %rim.4 = (bf16[45,160,128]{2,1,0:T(8,128)(2,1)S(1)}, bf16[13,240,128]{2,1,0:T(8,128)(2,1)S(1)}, f32[80,1664]{1,0:T(8,128)S(1)}, f32[80,1664]{1,0:T(8,128)S(1)}, ...) custom-call(bf16[640,128]{1,0:T(8,128)(2,1)S(1)} %collective-permute, ...), custom_call_target="tpu_custom_call", output_to_operand_aliasing={{0}: (17, {}), {1}: (18, {}), {2}: (19, {}), {3}: (20, {}),... | custom-call | tf_op jit(solution)/shard_map/rim/pallas_call | solution.py:301
  47.0 2.0 %collective-permute-start.5 = (bf16[640,128]{1,0:T(8,128)(2,1)S(1)}, bf16[640,128]{1,0:T(8,128)(2,1)S(1)}, u32[]{:S(2)}, u32[]{:S(2)}) collective-permute-start(bf16[640,128]{1,0:T(8,128)(2,1)S(1)} %get-tuple-element.56), channel_id=1, source_target_pairs={{0,255},{1,2},{2,1},{3,4},{4,3},{5,6},{6,5},{7,8},{8,7},{9,10},{10... | collective-permute-start | bytes 491528 | tf_op jit(solution)/shard_map/ppermute | solution.py:280
  48.9 4.9 %inside.5 = (bf16[45,160,128]{2,1,0:T(8,128)(2,1)S(1)}, bf16[13,240,128]{2,1,0:T(8,128)(2,1)S(1)}, f32[80,1664]{1,0:T(8,128)S(1)}, f32[80,1664]{1,0:T(8,128)S(1)}, f32[80,4992]{1,0:T(8,128)S(1)}) custom-call(bf16[13,240,128]{2,1,0:T(8,128)(2,1)S(1)} %get-tuple-element.57.refs_0_.refs_4_, f32[80,1664]{1,0:T(8,128)S(1)} %get-tuple-element.58.refs_1_.refs_5_, ...), custom_call_target="tpu_custom_call" | custom-call | tf_op jit(solution)/shard_map/inside/pallas_call | solution.py:293
  53.8 3.4 %collective-permute-done.5.refs_1_ = bf16[640,128]{1,0:T(8,128)(2,1)S(1)} collective-permute-done((bf16[640,128]{1,0:T(8,128)(2,1)S(1)}, bf16[640,128]{1,0:T(8,128)(2,1)S(1)}, u32[]{:S(2)}, u32[]{:S(2)}) %collective-permute-start.5) | collective-permute-done | bytes 163872 | tf_op jit(solution)/shard_map/ppermute | solution.py:280
  57.2 2.0 %rim.5 = (bf16[45,160,128]{2,1,0:T(8,128)(2,1)S(1)}, bf16[13,240,128]{2,1,0:T(8,128)(2,1)S(1)}, f32[80,1664]{1,0:T(8,128)S(1)}, f32[80,1664]{1,0:T(8,128)S(1)}, f32[80,4992]{1,0:T(8,128)S(1)}) custom-call(bf16[640,128]{1,0:T(8,128)(2,1)S(1)} %collective-permute-done.4.refs_0_, ...), custom_call_target="tpu_custom_call", output_to_operand_aliasing={{0}: (17, {}), {1}: (18, {}), {2}: (19, {}), {3}: (20, {}),... | custom-call | tf_op jit(solution)/shard_map/rim/pallas_call | solution.py:301
  59.2 0.8 %copy.55 = f32[80,1664]{1,0:T(8,128)} copy(f32[80,1664]{1,0:T(8,128)S(1)} %get-tuple-element.69) | data formatting | bytes 1064960
  60.0 0.8 %copy.56 = f32[80,1664]{1,0:T(8,128)} copy(f32[80,1664]{1,0:T(8,128)S(1)} %get-tuple-element.70) | data formatting | bytes 1064960
  60.8 1.1 %copy.57 = f32[80,4992]{1,0:T(8,128)} copy(f32[80,4992]{1,0:T(8,128)S(1)} %get-tuple-element.71) | data formatting | bytes 3194880
  (31 shorter events, 2.0 us)
Async XLA Ops:
  2.1 1.4 %copy-start = (f32[80,4992]{1,0:T(8,128)S(1)}, f32[80,4992]{1,0:T(8,128)}, u32[]{:S(2)}) copy-start(f32[80,4992]{1,0:T(8,128)} %refs_10_.8) | copy-start | bytes 4792324
  3.5 1.7 %copy-start.2 = (bf16[39,2,128,128]{3,2,1,0:T(8,128)(2,1)S(1)}, bf16[39,2,128,128]{3,2,1,0:T(8,128)(2,1)}, u32[]{:S(2)}) copy-start(bf16[39,2,128,128]{3,2,1,0:T(8,128)(2,1)} %param.14) | copy-start | bytes 7667716
  5.2 1.0 %copy-start.8 = (f32[80,1664]{1,0:T(8,128)S(1)}, f32[80,1664]{1,0:T(8,128)}, u32[]{:S(2)}) copy-start(f32[80,1664]{1,0:T(8,128)} %refs_8_.5) | copy-start | bytes 1597444
  6.3 1.0 %copy-start.10 = (f32[80,1664]{1,0:T(8,128)S(1)}, f32[80,1664]{1,0:T(8,128)}, u32[]{:S(2)}) copy-start(f32[80,1664]{1,0:T(8,128)} %refs_9_.5) | copy-start | bytes 1597444
  7.3 12.0 %copy-start.14 = (s32[13,6]{0,1:T(8,128)S(1)}, s32[13,6]{0,1:T(8,128)}, u32[]{:S(2)}) copy-start(s32[13,6]{0,1:T(8,128)} %param.17) | copy-start | bytes 940
  7.3 12.1 %copy-start.1 = (f32[80,4992]{1,0:T(8,128)S(1)}, f32[80,4992]{1,0:T(8,128)}, u32[]{:S(2)}) copy-start(f32[80,4992]{1,0:T(8,128)} %refs_10_.8) | copy-start | bytes 4792324
  7.3 12.1 %copy-start.9 = (f32[80,1664]{1,0:T(8,128)S(1)}, f32[80,1664]{1,0:T(8,128)}, u32[]{:S(2)}) copy-start(f32[80,1664]{1,0:T(8,128)} %refs_8_.5) | copy-start | bytes 1597444
  7.3 12.1 %copy-start.11 = (f32[80,1664]{1,0:T(8,128)S(1)}, f32[80,1664]{1,0:T(8,128)}, u32[]{:S(2)}) copy-start(f32[80,1664]{1,0:T(8,128)} %refs_9_.5) | copy-start | bytes 1597444
  9.6 0.9 %copy-start.12 = (bf16[13,240,128]{2,1,0:T(8,128)(2,1)}, bf16[13,240,128]{2,1,0:T(8,128)(2,1)S(1)}, u32[]{:S(2)}) copy-start(bf16[13,240,128]{2,1,0:T(8,128)(2,1)S(1)} %get-tuple-element.38.refs_0_.refs_4_) | copy-start | bytes 2396164
  10.5 20.0 %collective-permute-start = (bf16[1424,128]{1,0:T(8,128)(2,1)}, bf16[1424,128]{1,0:T(8,128)(2,1)S(1)}, u32[]{:S(2)}, u32[]{:S(2)}) collective-permute-start(bf16[1424,128]{1,0:T(8,128)(2,1)} %get-tuple-element.36), channel_id=1, source_target_pairs={{0,1},{1,0},{2,3},{3,2},{4,5},{5,4},{6,7},{7,6},{8,9},{9,8},{10,11... | collective-permute-start | bytes 1093640 | tf_op jit(solution)/shard_map/ppermute | solution.py:279
  10.5 20.0 %collective-permute-start.1 = (bf16[1424,128]{1,0:T(8,128)(2,1)}, bf16[1424,128]{1,0:T(8,128)(2,1)S(1)}, u32[]{:S(2)}, u32[]{:S(2)}) collective-permute-start(bf16[1424,128]{1,0:T(8,128)(2,1)} %get-tuple-element.37), channel_id=1, source_target_pairs={{0,255},{1,2},{2,1},{3,4},{4,3},{5,6},{6,5},{7,8},{8,7},{9,10},{10... | collective-permute-start | bytes 1093640 | tf_op jit(solution)/shard_map/ppermute | solution.py:280
  19.5 1.7 %copy-start.3 = (bf16[39,2,128,128]{3,2,1,0:T(8,128)(2,1)S(1)}, bf16[39,2,128,128]{3,2,1,0:T(8,128)(2,1)}, u32[]{:S(2)}) copy-start(bf16[39,2,128,128]{3,2,1,0:T(8,128)(2,1)} %param.14) | copy-start | bytes 7667716
  21.2 1.7 %copy-start.4 = (bf16[39,2,128,128]{3,2,1,0:T(8,128)(2,1)S(1)}, bf16[39,2,128,128]{3,2,1,0:T(8,128)(2,1)}, u32[]{:S(2)}) copy-start(bf16[39,2,128,128]{3,2,1,0:T(8,128)(2,1)} %param.13) | copy-start | bytes 7667716
  22.9 1.7 %copy-start.6 = (bf16[13,6,128,128]{3,2,1,0:T(8,128)(2,1)S(1)}, bf16[13,6,128,128]{3,2,1,0:T(8,128)(2,1)}, u32[]{:S(2)}) copy-start(bf16[13,6,128,128]{3,2,1,0:T(8,128)(2,1)} %param.16) | copy-start | bytes 7667716
  24.6 1.1 %copy-start.13 = (bf16[13,240,128]{2,1,0:T(8,128)(2,1)S(1)}, bf16[13,240,128]{2,1,0:T(8,128)(2,1)}, u32[]{:S(2)}) copy-start(bf16[13,240,128]{2,1,0:T(8,128)(2,1)} %copy-done.12) | copy-start | bytes 2396164
  30.5 4.4 %copy-start.5 = (bf16[39,2,128,128]{3,2,1,0:T(8,128)(2,1)S(1)}, bf16[39,2,128,128]{3,2,1,0:T(8,128)(2,1)}, u32[]{:S(2)}) copy-start(bf16[39,2,128,128]{3,2,1,0:T(8,128)(2,1)} %param.13) | copy-start | bytes 7667716
  30.5 4.4 %copy-start.7 = (bf16[13,6,128,128]{3,2,1,0:T(8,128)(2,1)S(1)}, bf16[13,6,128,128]{3,2,1,0:T(8,128)(2,1)}, u32[]{:S(2)}) copy-start(bf16[13,6,128,128]{3,2,1,0:T(8,128)(2,1)} %param.16) | copy-start | bytes 7667716
  33.4 6.4 %collective-permute-start.2 = (bf16[640,128]{1,0:T(8,128)(2,1)S(1)}, bf16[640,128]{1,0:T(8,128)(2,1)S(1)}, u32[]{:S(2)}, u32[]{:S(2)}) collective-permute-start(bf16[640,128]{1,0:T(8,128)(2,1)S(1)} %get-tuple-element.44), channel_id=1, source_target_pairs={{0,1},{1,0},{2,3},{3,2},{4,5},{5,4},{6,7},{7,6},{8,9},{9,8},{10,11... | collective-permute-start | bytes 491528 | tf_op jit(solution)/shard_map/ppermute | solution.py:279
  33.5 10.3 %collective-permute-start.3 = (bf16[640,128]{1,0:T(8,128)(2,1)S(1)}, bf16[640,128]{1,0:T(8,128)(2,1)S(1)}, u32[]{:S(2)}, u32[]{:S(2)}) collective-permute-start(bf16[640,128]{1,0:T(8,128)(2,1)S(1)} %get-tuple-element.45), channel_id=1, source_target_pairs={{0,255},{1,2},{2,1},{3,4},{4,3},{5,6},{6,5},{7,8},{8,7},{9,10},{10... | collective-permute-start | bytes 491528 | tf_op jit(solution)/shard_map/ppermute | solution.py:280
  46.7 7.1 %collective-permute-start.4 = (bf16[640,128]{1,0:T(8,128)(2,1)S(1)}, bf16[640,128]{1,0:T(8,128)(2,1)S(1)}, u32[]{:S(2)}, u32[]{:S(2)}) collective-permute-start(bf16[640,128]{1,0:T(8,128)(2,1)S(1)} %get-tuple-element.55), channel_id=1, source_target_pairs={{0,1},{1,0},{2,3},{3,2},{4,5},{5,4},{6,7},{7,6},{8,9},{9,8},{10,11... | collective-permute-start | bytes 491528 | tf_op jit(solution)/shard_map/ppermute | solution.py:279
  47.0 10.3 %collective-permute-start.5 = (bf16[640,128]{1,0:T(8,128)(2,1)S(1)}, bf16[640,128]{1,0:T(8,128)(2,1)S(1)}, u32[]{:S(2)}, u32[]{:S(2)}) collective-permute-start(bf16[640,128]{1,0:T(8,128)(2,1)S(1)} %get-tuple-element.56), channel_id=1, source_target_pairs={{0,255},{1,2},{2,1},{3,4},{4,3},{5,6},{6,5},{7,8},{8,7},{9,10},{10... | collective-permute-start | bytes 491528 | tf_op jit(solution)/shard_map/ppermute | solution.py:280

commit v2 on v1

v2 whole, which is shorter than its diff:
```python
import jax
import jax.numpy as jnp
from jax import lax
from jax.experimental import pallas as pl
from jax.experimental.pallas import tpu as pltpu
from jax.sharding import PartitionSpec as P

buoyancy = 0.2
drag_rate = 0.5
time_step = 0.25
keep_shares = (0.0, 0.75, 1.0 / 3.0)

F32 = jnp.float32
BF16 = jnp.bfloat16
LEV = 80
TILE = 128
NEAR = 3 * LEV
NEXT = NEAR + 2 * LEV
MOVE = NEXT + 3 * LEV
SIDE = MOVE + 16


def lanes(block):
    return slice(block * TILE, (block + 1) * TILE)


def advance(anchor, current, slope, keep_share):
    if keep_share == 0.0:
        return current + time_step * slope
    return keep_share * anchor + (1.0 - keep_share) * (current + time_step * slope)


def block_mask(levels_ref, block):
    depth = lax.broadcasted_iota(jnp.int32, (LEV, TILE), 0)
    return (depth < levels_ref[block : block + 1, :]).astype(F32)


def above_weights():
    row = lax.broadcasted_iota(jnp.int32, (LEV, 3 * LEV), 0)
    column = lax.broadcasted_iota(jnp.int32, (LEV, 3 * LEV), 1)
    column = jnp.where(column >= 2 * LEV, column - 2 * LEV, jnp.where(column >= LEV, column - LEV, column))
    return jnp.where(column < row, 1.0, jnp.where(column == row, 0.5, 0.0)).astype(BF16)


def pressure_of(done, above):
    highs, middles, lows = [], [], []
    for thickness, tracer, mask in done:
        weight = thickness * (1.0 - buoyancy * tracer) * mask
        high = weight.astype(BF16)
        rest = weight - high.astype(F32)
        middle = rest.astype(BF16)
        highs.append(high)
        middles.append(middle)
        lows.append((rest - middle.astype(F32)).astype(BF16))
    parts = jnp.concatenate([jnp.concatenate(p, axis=1) for p in (highs, middles, lows)], axis=0)
    return jnp.dot(above, parts, preferred_element_type=F32) * (1.0 / LEV)


def code_blocks(coded, blocks, done, above):
    pressures = pressure_of(done, above)
    for i, (block, (thickness, tracer, mask)) in enumerate(zip(blocks, done)):
        coded[block, 0:LEV, :] = pressures[:, lanes(i)].astype(BF16)
        coded[block, LEV : 2 * LEV, :] = thickness.astype(BF16)
        coded[block, 2 * LEV : NEAR, :] = tracer.astype(BF16)


def edge_step(levels_mask, first, second, gradient, average, velocity, anchor, keep_share):
    slope = jnp.dot(
        jnp.concatenate([first[:LEV], second[:LEV]], axis=1), gradient, preferred_element_type=F32
    )
    carried = jnp.dot(
        jnp.concatenate([first[LEV:], second[LEV:]], axis=1), average, preferred_element_type=F32
    )
    moving = velocity * levels_mask
    flux = jnp.concatenate([carried[:LEV] * moving, carried[LEV:] * moving], axis=0).astype(BF16)
    change = (-slope - drag_rate * velocity) * levels_mask
    return flux, advance(anchor, velocity, change, keep_share)


def cell_step(block, fluxes_ref, sources_ref, first_block, own, whole, tiles_ref):
    picked = []
    for t in range(6):
        offset = sources_ref[t, block] - 3 * first_block
        offset = jnp.where(offset > 3 * own + 2, offset - 3 * whole, jnp.where(offset < -3, offset + 3 * whole, offset))
        picked.append(fluxes_ref[offset + 3])
    return -jnp.dot(jnp.concatenate(picked, axis=1), tiles_ref[block], preferred_element_type=F32)


def other_block(sources_ref, edge, first_block, own, whole):
    offset = sources_ref[1, edge] - first_block
    return jnp.where(offset > own, offset - whole, jnp.where(offset < -1, offset + whole, offset))


def start_kernel(
    own, thickness, tracer, velocity, levels, average, edge_sources, cell_sources,
    inner, outer, levels_out, edge_sources_out, cell_sources_out,
    h, s, v, flat, sems,
):
    position = lax.axis_index("dom")
    whole = own * lax.axis_size("dom")
    inner_side = 1 - lax.rem(position, 2)
    ends = []
    for p, side in ((0, inner_side), (1, 1 - inner_side)):
        block = side * (own - 1)
        ends.append((p, side, block, block + 1 - 2 * side))

    def columns(block, wide):
        return pl.ds(pl.multiple_of(block * TILE, TILE), wide)

    small = [
        pltpu.make_async_copy(levels, flat, sems.at[0]),
        pltpu.make_async_copy(edge_sources, edge_sources_out, sems.at[1]),
        pltpu.make_async_copy(cell_sources, cell_sources_out, sems.at[2]),
    ]
    fields, tiles = [], []
    for p, side, block, after in ends:
        for k, b in ((0, block), (1, after)):
            fields.append(pltpu.make_async_copy(thickness.at[:, columns(b, TILE)], h.at[p, k], sems.at[3 + 4 * p + 2 * k]))
            fields.append(pltpu.make_async_copy(tracer.at[:, columns(b, TILE)], s.at[p, k], sems.at[4 + 4 * p + 2 * k]))
        fields.append(pltpu.make_async_copy(velocity.at[:, columns(3 * block, 3 * TILE)], v.at[p], sems.at[11 + p]))
        message = (inner, outer)[p]
        rows = pl.ds(pl.multiple_of(block * 6 * TILE, 6 * TILE), 6 * TILE)
        tiles.append(pltpu.make_async_copy(average.at[rows, :], message.at[pl.ds(SIDE, 6 * TILE), :], sems.at[13 + p]))
    for copy in small + fields + tiles:
        copy.start()
    above = above_weights()
    for copy in small:
        copy.wait()
    for block in range(own):
        levels_out[block] = flat[lanes(block)]
    for copy in fields:
        copy.wait()
    done = []
    for p, side, block, after in ends:
        depth = lax.broadcasted_iota(jnp.int32, (LEV, TILE), 0)
        done.append((h[p, 0], s[p, 0], (depth < levels_out[pl.ds(block, 1), :]).astype(F32)))
    pressures = pressure_of(done, above)
    for p, side, block, after in ends:
        message = (inner, outer)[p]
        mask = done[p][2]
        message[0:LEV, :] = pressures[:, lanes(p)].astype(BF16)
        message[LEV : 2 * LEV, :] = h[p, 0].astype(BF16)
        message[2 * LEV : NEAR, :] = s[p, 0].astype(BF16)
        message[NEAR : NEAR + LEV, :] = h[p, 1].astype(BF16)
        message[NEAR + LEV : NEXT, :] = s[p, 1].astype(BF16)
        row = lax.broadcasted_iota(jnp.int32, (16, TILE), 0)
        signs = jnp.zeros((16, TILE), F32)
        for j in range(3):
            message[NEXT + j * LEV : NEXT + (j + 1) * LEV, :] = (v[p, :, lanes(j)] * mask).astype(BF16)
            low = other_block(edge_sources_out, j, position * own, own, whole)
            high = other_block(edge_sources_out, 3 * (own - 1) + j, position * own, own, whole) - (own - 1)
            signs = jnp.where(row == j, jnp.where(side == 0, low, high).astype(F32), signs)
        message[MOVE:SIDE, :] = signs.astype(BF16)
    for copy in tiles:
        copy.wait()


def load_kernel(own, keep_share, *refs):
    far = refs[:6]
    levels, edge_sources, cell_sources = refs[6:9]
    fluxes, new_coded, new_thickness, new_tracer, new_velocity, coded = refs[9:15]
    here = refs[15:21]
    sems = refs[21]
    h0, s0, v0, gradient, average, divergence = here
    cuts = ((0, 3), (3, 6), (6, 9), (9, own))

    def copies(which, cut):
        lo, hi = cut
        n = hi - lo
        if which < 2:
            at = (slice(None), pl.ds(lo * TILE, n * TILE))
        elif which == 2:
            at = (slice(None), pl.ds(3 * lo * TILE, 3 * n * TILE))
        elif which < 5:
            at = (pl.ds(3 * lo, 3 * n),)
        else:
            at = (pl.ds(lo, n),)
        return pltpu.make_async_copy(far[which].at[at], here[which].at[at], sems.at[which, cuts.index(cut)])

    for which in (0, 1):
        for cut in cuts:
            copies(which, cut).start()
    for cut in cuts:
        for which in (2, 3, 4):
            copies(which, cut).start()
    for cut in cuts:
        copies(5, cut).start()
    for which in (0, 1):
        for cut in cuts:
            copies(which, cut).wait()
    above = above_weights()
    done = [(h0[:, lanes(b)], s0[:, lanes(b)], block_mask(levels, b)) for b in range(own)]
    code_blocks(coded, range(own), done, above)

    def wait_edges(block):
        for cut in cuts:
            if block == max(cut[0], 1):
                for which in (2, 3, 4):
                    copies(which, cut).wait()

    def wait_cells(block):
        for cut in cuts:
            if block == max(cut[0], 2):
                copies(5, cut).wait()

    inside_kernel(
        own, keep_share, coded, h0, s0, v0, h0, s0, v0, levels,
        gradient, average, edge_sources, divergence, cell_sources,
        fluxes, new_coded, new_thickness, new_tracer, new_velocity,
        wait_edges=wait_edges, wait_cells=wait_cells,
    )


def last_inside_kernel(own, keep_share, *refs):
    common = refs[:13]
    fluxes, far_h, far_s, far_v, h, s, v, sems = refs[13:]
    sent = []

    def after_edges():
        at = (slice(None), pl.ds(3 * TILE, 3 * (own - 2) * TILE))
        copy = pltpu.make_async_copy(v.at[at], far_v.at[at], sems.at[0])
        copy.start()
        sent.append(copy)

    inside_kernel(own, keep_share, *common, fluxes, None, h, s, v, after_edges=after_edges)
    at = (slice(None), pl.ds(2 * TILE, (own - 4) * TILE))
    for i, (a, b) in enumerate(((h, far_h), (s, far_s))):
        copy = pltpu.make_async_copy(a.at[at], b.at[at], sems.at[1 + i])
        copy.start()
        sent.append(copy)
    for copy in sent:
        copy.wait()


def inside_kernel(
    own, keep_share,
    coded, thickness, tracer, velocity, thickness0, tracer0, velocity0, levels,
    gradient, average, edge_sources, divergence, cell_sources,
    fluxes, new_coded, new_thickness, new_tracer, new_velocity,
    wait_edges=None, wait_cells=None, after_edges=None,
):
    above = above_weights()
    position = lax.axis_index("dom")
    whole = own * lax.axis_size("dom")
    first_block = position * own

    for block in range(1, own - 1):
        if wait_edges is not None:
            wait_edges(block)
        mask = block_mask(levels, block)
        for edge in range(3 * block, 3 * block + 3):
            other = other_block(edge_sources, edge, first_block, own, whole)
            flux, updated = edge_step(
                mask, coded[block], coded[other], gradient[edge], average[edge],
                velocity[:, lanes(edge)], velocity0[:, lanes(edge)], keep_share,
            )
            fluxes[edge + 3] = flux
            new_velocity[:, lanes(edge)] = updated
    if after_edges is not None:
        after_edges()
    done = []
    for block in range(2, own - 2):
        if wait_cells is not None:
            wait_cells(block)
        done.append(
            finish_cell(
                block, own, keep_share, first_block, whole,
                thickness, tracer, thickness0, tracer0, levels, divergence, cell_sources,
                fluxes, new_thickness, new_tracer,
            )
        )
    if new_coded is not None:
        code_blocks(new_coded, range(2, own - 2), done, above)


def finish_cell(
    block, own, keep_share, first_block, whole,
    thickness, tracer, thickness0, tracer0, levels, divergence, cell_sources,
    fluxes, new_thickness, new_tracer,
):
    at = lanes(block)
    mask = block_mask(levels, block)
    change = cell_step(block, fluxes, cell_sources, first_block, own, whole, divergence)
    h = advance(thickness0[:, at], thickness[:, at], change[:LEV] * mask, keep_share)
    s = advance(tracer0[:, at], tracer[:, at], change[LEV:] * mask, keep_share)
    new_thickness[:, at] = h
    new_tracer[:, at] = s
    return h, s, mask


def rim_kernel(
    own, keep_share, last,
    inner_in, outer_in, tiles_inner, tiles_outer,
    coded, thickness, tracer, velocity, thickness0, tracer0, velocity0, levels,
    gradient, average, edge_sources, divergence, cell_sources,
    *rest,
):
    if last:
        fluxes, far_h, far_s, far_v, halo, halo_tiles, pair, new_thickness, new_tracer, new_velocity, sems = rest[4:]
    else:
        fluxes, new_coded, new_thickness, new_tracer, new_velocity = rest[5:10]
        inner, outer, halo, halo_tiles, pair, staged = rest[10:]
    above = above_weights()
    position = lax.axis_index("dom")
    whole = own * lax.axis_size("dom")
    first_block = position * own
    inner_side = 1 - lax.rem(position, 2)
    sent = []

    def send(here, far, lo, wide, sem):
        at = (slice(None), pl.ds(lo * TILE, wide * TILE))
        copy = pltpu.make_async_copy(here.at[at], far.at[at], sems.at[sem])
        copy.start()
        sent.append(copy)

    halo[inner_side] = inner_in[0:MOVE, :]
    halo[1 - inner_side] = outer_in[0:MOVE, :]
    halo_tiles[inner_side] = tiles_inner[MOVE:, :]
    halo_tiles[1 - inner_side] = tiles_outer[MOVE:, :]

    for side, block, after in ((0, 0, 1), (1, own - 1, own - 2)):
        mask = block_mask(levels, block)
        outward = 2 * side - 1
        beyond = -1 if side == 0 else own
        pair[side, 0] = halo[side, 0:NEAR, :]
        pair[side, 1] = coded[after]
        signs = halo_tiles[side, 0:16, :].astype(F32)
        for j in range(3):
            edge = 3 * block + j
            other = other_block(edge_sources, edge, first_block, own, whole)
            flux, updated = edge_step(
                mask, coded[block], pair[side, (other == after).astype(jnp.int32)], gradient[edge], average[edge],
                velocity[:, lanes(edge)], velocity0[:, lanes(edge)], keep_share,
            )
            fluxes[edge + 3] = flux
            new_velocity[:, lanes(edge)] = updated
            toward = signs[j : j + 1, :] * outward
            second = jnp.where(
                jnp.broadcast_to(toward, (2 * LEV, TILE)) > 0.0,
                halo[side, NEAR:NEXT, :].astype(F32),
                coded[block, LEV:, :].astype(F32),
            ).astype(BF16)
            carried = jnp.dot(
                jnp.concatenate([halo[side, LEV:NEAR, :], second], axis=1),
                halo_tiles[side, 16 + j * 256 : 16 + (j + 1) * 256, :],
                preferred_element_type=F32,
            )
            moving = halo[side, NEXT + j * LEV : NEXT + (j + 1) * LEV, :].astype(F32)
            fluxes[3 * beyond + 3 + j] = jnp.concatenate(
                [carried[:LEV] * moving, carried[LEV:] * moving], axis=0
            ).astype(BF16)
        if last:
            send(new_velocity, far_v, 3 * block, 3, side)
    rim = (0, 1, own - 2, own - 1)
    done = []
    for block in rim:
        done.append(
            finish_cell(
                block, own, keep_share, first_block, whole,
                thickness, tracer, thickness0, tracer0, levels, divergence, cell_sources,
                fluxes, new_thickness, new_tracer,
            )
        )
        if last and block in (1, own - 1):
            send(new_thickness, far_h, block - 1, 2, 2 if block == 1 else 3)
            send(new_tracer, far_s, block - 1, 2, 4 if block == 1 else 5)
    if last:
        for copy in sent:
            copy.wait()
    else:
        code_blocks(new_coded, rim, done, above)
        for side, block, after in ((0, 0, 1), (1, own - 1, own - 2)):
            mask = block_mask(levels, block)
            staged[side, 0:NEAR, :] = new_coded[block]
            staged[side, NEAR:NEXT, :] = new_coded[after, LEV:, :]
            for j in range(3):
                edge = 3 * block + j
                staged[side, NEXT + j * LEV : NEXT + (j + 1) * LEV, :] = (new_velocity[:, lanes(edge)] * mask).astype(BF16)
        inner[...] = staged[inner_side]
        outer[...] = staged[1 - inner_side]


def in_hbm(array):
    return pltpu.with_memory_space_constraint(array, pltpu.HBM)


def local(
    thickness,
    tracer,
    velocity,
    active_levels,
    gradient_tiles,
    average_tiles,
    edge_sources,
    divergence_tiles,
    cell_sources,
):
    own = cell_sources.shape[0]
    devices = lax.axis_size("dom")
    within = [(i, i ^ 1) for i in range(devices)]
    across = [(i, (i + 1) % devices if i % 2 else (i - 1) % devices) for i in range(devices)]
    cells, edges = thickness.shape[1], velocity.shape[1]
    vmem = pl.BlockSpec(memory_space=pltpu.VMEM)
    hbm = pl.BlockSpec(memory_space=pltpu.HBM)
    params = pltpu.CompilerParams(vmem_limit_bytes=16 * 1024 * 1024)

    gradient = in_hbm(gradient_tiles.reshape(3 * own, 2 * TILE, TILE))
    average = in_hbm(average_tiles.reshape(3 * own, 2 * TILE, TILE))
    average_rows = in_hbm(average_tiles.reshape(3 * own * 2 * TILE, TILE))
    divergence = in_hbm(divergence_tiles.reshape(own, 6 * TILE, TILE))
    thickness, tracer, velocity = in_hbm(thickness), in_hbm(tracer), in_hbm(velocity)
    first_rows = SIDE + 6 * TILE

    def message(rows):
        return pltpu.VMEM((rows, TILE), BF16)

    inner, outer, levels, edge_sources, cell_sources = pl.pallas_call(
        lambda *refs: start_kernel(own, *refs),
        out_shape=(
            message(first_rows),
            message(first_rows),
            pltpu.VMEM((own, TILE), jnp.int32),
            pltpu.VMEM((2, 3 * own), jnp.int32),
            pltpu.VMEM((6, own), jnp.int32),
        ),
        in_specs=[hbm] * 7,
        out_specs=[vmem] * 5,
        scratch_shapes=[
            pltpu.VMEM((2, 2, LEV, TILE), F32),
            pltpu.VMEM((2, 2, LEV, TILE), F32),
            pltpu.VMEM((2, LEV, 3 * TILE), F32),
            pltpu.VMEM((cells,), jnp.int32),
            pltpu.SemaphoreType.DMA((15,)),
        ],
        compiler_params=params,
        name="start",
    )(thickness, tracer, velocity, in_hbm(active_levels), average_rows, in_hbm(edge_sources.T), in_hbm(cell_sources.T))

    tiles_inner = tiles_outer = None
    state = ()
    for section in range(3):
        last = section == 2
        keep_share = keep_shares[section]
        inner_in = lax.ppermute(inner, "dom", within)
        outer_in = lax.ppermute(outer, "dom", across)
        coded_shape = pltpu.VMEM((own, NEAR, TILE), BF16)
        field_shapes = (
            pltpu.VMEM((LEV, cells), F32),
            pltpu.VMEM((LEV, cells), F32),
            pltpu.VMEM((LEV, edges), F32),
        )
        built_shapes = (pltpu.VMEM((3 * own + 6, 2 * LEV, TILE), BF16), coded_shape) + field_shapes
        if section == 0:
            tiles_inner, tiles_outer = inner_in, outer_in
            loaded = pl.pallas_call(
                lambda *refs, keep_share=keep_share: load_kernel(own, keep_share, *refs),
                out_shape=built_shapes
                + (coded_shape,)
                + field_shapes
                + (
                    pltpu.VMEM((3 * own, 2 * TILE, TILE), BF16),
                    pltpu.VMEM((3 * own, 2 * TILE, TILE), BF16),
                    pltpu.VMEM((own, 6 * TILE, TILE), BF16),
                ),
                in_specs=[hbm] * 6 + [vmem] * 3,
                out_specs=[vmem] * 12,
                scratch_shapes=[pltpu.SemaphoreType.DMA((6, 4))],
                compiler_params=params,
                name="inside",
            )(thickness, tracer, velocity, gradient, average, divergence, levels, edge_sources, cell_sources)
            built = loaded[:5]
            coded = loaded[5]
            anchor = loaded[6:9]
            gradient, average, divergence = loaded[9:]
            state = anchor
        common = (coded, *state, *anchor, levels, gradient, average, edge_sources, divergence, cell_sources)
        if last:
            built_shapes = built_shapes[:1] + (
                pltpu.HBM((LEV, cells), F32),
                pltpu.HBM((LEV, cells), F32),
                pltpu.HBM((LEV, edges), F32),
            )
        built_specs = [vmem] + [hbm] * 3 if last else [vmem] * 5
        field_scratch = list(field_shapes)
        if section > 0:
            body = last_inside_kernel if last else inside_kernel
            built = pl.pallas_call(
                lambda *refs, keep_share=keep_share, body=body: body(own, keep_share, *refs),
                out_shape=built_shapes,
                in_specs=[vmem] * 13,
                out_specs=built_specs,
                scratch_shapes=field_scratch + [pltpu.SemaphoreType.DMA((3,))] if last else [],
                compiler_params=params,
                name="inside",
            )(*common)
        scratch = [
            pltpu.VMEM((2, MOVE, TILE), BF16),
            pltpu.VMEM((2, 16 + 6 * TILE, TILE), BF16),
            pltpu.VMEM((2, 2, NEAR, TILE), BF16),
        ]
        if last:
            scratch += field_scratch + [pltpu.SemaphoreType.DMA((6,))]
        else:
            scratch += [pltpu.VMEM((2, MOVE, TILE), BF16)]
        built = pl.pallas_call(
            lambda *refs, keep_share=keep_share, last=last: rim_kernel(own, keep_share, last, *refs),
            out_shape=built_shapes + (() if last else (message(MOVE), message(MOVE))),
            in_specs=[vmem] * 17 + built_specs,
            out_specs=built_specs + ([] if last else [vmem] * 2),
            scratch_shapes=scratch,
            input_output_aliases={17 + i: i for i in range(len(built_shapes))},
            compiler_params=params,
            name="rim",
        )(inner_in, outer_in, tiles_inner, tiles_outer, *common, *built)
        if last:
            return built[1:4]
        coded = built[1]
        state = built[2:5]
        inner, outer = built[5:]


def solution(mesh):
    return jax.shard_map(
        local,
        mesh=mesh,
        in_specs=(
            P(None, "dom"),
            P(None, "dom"),
            P(None, "dom"),
            P("dom"),
            P("dom", None, None, None),
            P("dom", None, None, None),
            P("dom", None),
            P("dom", None, None, None),
            P("dom", None),
        ),
        out_specs=(P(None, "dom"), P(None, "dom"), P(None, "dom")),
        check_vma=False,
    )
```

time: 62.4 us -> 42.9 us (0.69)
  local copies, waits for them, and re-layouts: 16.7 us -> 0 us
  starting transfers between devices: 12.6 us -> 21.8 us
  Pallas kernels: 24.4 us -> 18.2 us
  waiting for transfers between devices: 7.4 us -> 1.88 us
    unnamed x35 -> x0, local copies, waits for them, and re-layouts: 16 us -> none
    ppermute x3, starting transfers between devices: 12.3 us -> 21.6 us  [local(): outer_in = lax.ppermute(outer, 'dom', across)]
    ppermute x3, waiting for transfers between devices: 7.39 us -> 1.87 us  [local(): outer_in = lax.ppermute(outer, 'dom', across)]
    pallas_call x3, Pallas kernels: 7.77 us -> 4.47 us  [local(): pl.pallas_call(lambda *refs, keep_share=keep_share, last=last: rim_kernel...]
    pallas_call x4, Pallas kernels: 16.7 us -> 13.7 us  [the longest x2 6.09 us: local(): pl.pallas_call(lambda *refs, keep_share=keep_share, body=body: body(own,...]
    reshape x1 -> x0, local copies, waits for them, and re-layouts: 0.7 us -> none  [local(): levels = in_vmem(active_levels.reshape(1, cells))]
  transfers between devices with their start and end apart: 6 -> 6, of which waited for: 2 -> 2; matrix products, arithmetic and copies ran while one was open for 0% -> 0% of each run, Pallas kernels for 23% -> 28%
where the time goes in v2:
time: 42.9 us; the launch traced here: 42.8 us
  starting transfers between devices  21.8 us (51%)
  Pallas kernels  18.2 us (42%)
  waiting for transfers between devices  1.88 us (4%)
  between operations  0.88 us (2%)
    ppermute x3, starting transfers between devices, local(): outer_in = lax.ppermute(outer, 'dom', across)  21.6 us
    pallas_call x2, Pallas kernels, local(): pl.pallas_call(lambda *refs, keep_share=keep_share, body=body: body(own,...  6.09 us
    pallas_call x1, Pallas kernels, local(): pl.pallas_call(lambda *refs, keep_share=keep_share: load_kernel(own, keep...  6.08 us
    pallas_call x3, Pallas kernels, local(): pl.pallas_call(lambda *refs, keep_share=keep_share, last=last: rim_kernel...  4.47 us
    ppermute x3, waiting for transfers between devices, local(): outer_in = lax.ppermute(outer, 'dom', across)  1.87 us
    pallas_call x1, Pallas kernels, local(): pl.pallas_call(lambda *refs: start_kernel(own, *refs), out_shape=(message...  1.53 us
  transfers between devices with their start and end apart: 6, of which 2 were waited for; matrix products, arithmetic and copies ran while one was open for 0% of the time, Pallas kernels for 28%

profile of v2, /device:TPU:0, one launch (start us, length us, event | category | flops | bytes accessed | tf_op | source)
XLA Modules:
  0.0 42.8 jit_solution(5383955472283136832)
XLA Ops:
  0.6 1.5 %start.1 = (bf16[1424,128]{1,0:T(8,128)(2,1)S(1)}, bf16[1424,128]{1,0:T(8,128)(2,1)S(1)}, s32[13,128]{1,0:T(8,128)S(1)}, s32[2,39]{1,0:T(2,128)S(1)}, s32[6,13]{1,0:T(8,128)S(1)}) custom-call(f32[80,1664]{1,0:T(8,128)} %refs_0_.3, f32[80,1664]{1,0:T(8,128)} %refs_1_.3, f32[80,4992]{1,0:T(8,128)} %refs_2_.3, s32[1664]{0:T(1024)} %refs_3_.1, ...), custom_call_target="tpu_custom_call" | custom-call | tf_op jit(solution)/shard_map/start/pallas_call | solution.py:417
  2.2 0.1 collective-permute-start
  2.3 8.9 %collective-permute-start.1 = (bf16[1424,128]{1,0:T(8,128)(2,1)S(1)}, bf16[1424,128]{1,0:T(8,128)(2,1)S(1)}, u32[]{:S(2)}, u32[]{:S(2)}) collective-permute-start(bf16[1424,128]{1,0:T(8,128)(2,1)S(1)} %get-tuple-element.45), channel_id=1, source_target_pairs={{0,255},{1,2},{2,1},{3,4},{4,3},{5,6},{6,5},{7,8},{8,7},{9,10},{10... | collective-permute-start | bytes 1093640 | tf_op jit(solution)/shard_map/ppermute | solution.py:445
  11.1 6.1 %inside.3 = (bf16[45,160,128]{2,1,0:T(8,128)(2,1)S(1)}, bf16[13,240,128]{2,1,0:T(8,128)(2,1)S(1)}, f32[80,1664]{1,0:T(8,128)S(1)}, f32[80,1664]{1,0:T(8,128)S(1)...) custom-call(f32[80,1664]{1,0:T(8,128)} %refs_0_.3, ...), custom_call_target="tpu_custom_call" | custom-call | tf_op jit(solution)/shard_map/inside/pallas_call | solution.py:455
  17.2 0.0 collective-permute-done.refs_0_.refs_2_
  17.2 0.0 collective-permute-done.1.refs_1_.refs_3_
  17.2 1.4 %rim.3 = (bf16[45,160,128]{2,1,0:T(8,128)(2,1)S(1)}, bf16[13,240,128]{2,1,0:T(8,128)(2,1)S(1)}, f32[80,1664]{1,0:T(8,128)S(1)}, f32[80,1664]{1,0:T(8,128)S(1)}, ...) custom-call(bf16[1424,128]{1,0:T(8,128)(2,1)S(1)} %collective-permut, ...), custom_call_target="tpu_custom_call", output_to_operand_aliasing={{0}: (17, {}), {1}: (18, {}), {2}: (19, {}), {3}: (20, {}),... | custom-call | tf_op jit(solution)/shard_map/rim/pallas_call | solution.py:505
  18.6 0.1 collective-permute-start.2
  18.7 6.3 %collective-permute-start.3 = (bf16[640,128]{1,0:T(8,128)(2,1)S(1)}, bf16[640,128]{1,0:T(8,128)(2,1)S(1)}, u32[]{:S(2)}, u32[]{:S(2)}) collective-permute-start(bf16[640,128]{1,0:T(8,128)(2,1)S(1)} %get-tuple-element.62), channel_id=1, source_target_pairs={{0,255},{1,2},{2,1},{3,4},{4,3},{5,6},{6,5},{7,8},{8,7},{9,10},{10... | collective-permute-start | bytes 491528 | tf_op jit(solution)/shard_map/ppermute | solution.py:445
  25.0 2.6 %inside.4 = (bf16[45,160,128]{2,1,0:T(8,128)(2,1)S(1)}, bf16[13,240,128]{2,1,0:T(8,128)(2,1)S(1)}, f32[80,1664]{1,0:T(8,128)S(1)}, f32[80,1664]{1,0:T(8,128)S(1)}, f32[80,4992]{1,0:T(8,128)S(1)}) custom-call(bf16[13,240,128]{2,1,0:T(8,128)(2,1)S(1)} %get-tuple-element.63.refs_0_.refs_4_, f32[80,1664]{1,0:T(8,128)S(1)} %get-tuple-element.64.refs_1_.refs_5_, ...), custom_call_target="tpu_custom_call" | custom-call | tf_op jit(solution)/shard_map/inside/pallas_call | solution.py:487
  27.6 0.0 collective-permute-done.2.refs_0_
  27.6 1.4 %collective-permute-done.3.refs_1_ = bf16[640,128]{1,0:T(8,128)(2,1)S(1)} collective-permute-done((bf16[640,128]{1,0:T(8,128)(2,1)S(1)}, bf16[640,128]{1,0:T(8,128)(2,1)S(1)}, u32[]{:S(2)}, u32[]{:S(2)}) %collective-permute-start.3) | collective-permute-done | bytes 163872 | tf_op jit(solution)/shard_map/ppermute | solution.py:445
  29.0 1.3 %rim.4 = (bf16[45,160,128]{2,1,0:T(8,128)(2,1)S(1)}, bf16[13,240,128]{2,1,0:T(8,128)(2,1)S(1)}, f32[80,1664]{1,0:T(8,128)S(1)}, f32[80,1664]{1,0:T(8,128)S(1)}, ...) custom-call(bf16[640,128]{1,0:T(8,128)(2,1)S(1)} %collective-permute, ...), custom_call_target="tpu_custom_call", output_to_operand_aliasing={{0}: (17, {}), {1}: (18, {}), {2}: (19, {}), {3}: (20, {}),... | custom-call | tf_op jit(solution)/shard_map/rim/pallas_call | solution.py:505
  30.3 0.1 collective-permute-start.4
  30.4 6.4 %collective-permute-start.5 = (bf16[640,128]{1,0:T(8,128)(2,1)S(1)}, bf16[640,128]{1,0:T(8,128)(2,1)S(1)}, u32[]{:S(2)}, u32[]{:S(2)}) collective-permute-start(bf16[640,128]{1,0:T(8,128)(2,1)S(1)} %get-tuple-element.73), channel_id=1, source_target_pairs={{0,255},{1,2},{2,1},{3,4},{4,3},{5,6},{6,5},{7,8},{8,7},{9,10},{10... | collective-permute-start | bytes 491528 | tf_op jit(solution)/shard_map/ppermute | solution.py:445
  36.8 3.5 %inside.5 = (bf16[45,160,128]{2,1,0:T(8,128)(2,1)S(1)}, f32[80,1664]{1,0:T(8,128)}, f32[80,1664]{1,0:T(8,128)}, f32[80,4992]{1,0:T(8,128)}) custom-call(bf16[13,240,128]{2,1,0:T(8,128)(2,1)S(1)} %get-tuple-element.74.refs_0_.refs_4_, f32[80,1664]{1,0:T(8,128)S(1)} %get-tuple-element.75.refs_1_.refs_5_, f32[80,1664]{1,0:T(8,128)S(1)} %get-tuple-element.76.refs_2_.refs_6_, ...), custom_call_target="tpu_custom_call" | custom-call | tf_op jit(solution)/shard_map/inside/pallas_call | solution.py:487
  40.4 0.0 collective-permute-done.4.refs_0_
  40.4 0.5 %collective-permute-done.5.refs_1_ = bf16[640,128]{1,0:T(8,128)(2,1)S(1)} collective-permute-done((bf16[640,128]{1,0:T(8,128)(2,1)S(1)}, bf16[640,128]{1,0:T(8,128)(2,1)S(1)}, u32[]{:S(2)}, u32[]{:S(2)}) %collective-permute-start.5) | collective-permute-done | bytes 163872 | tf_op jit(solution)/shard_map/ppermute | solution.py:445
  40.8 1.8 %rim.5 = (bf16[45,160,128]{2,1,0:T(8,128)(2,1)S(1)}, f32[80,1664]{1,0:T(8,128)}, f32[80,1664]{1,0:T(8,128)}, f32[80,4992]{1,0:T(8,128)}) custom-call(bf16[640,128]{1,0:T(8,128)(2,1)S(1)} %collective-permute-done.4.refs_0_, ...), custom_call_target="tpu_custom_call", output_to_operand_aliasing={{0}: (17, {}), {1}: (18, {}), {2}: (19, {}), {3}: (20, {})} | custom-call | tf_op jit(solution)/shard_map/rim/pallas_call | solution.py:505
Async XLA Ops:
  2.2 15.1 %collective-permute-start = (bf16[1424,128]{1,0:T(8,128)(2,1)S(1)}, bf16[1424,128]{1,0:T(8,128)(2,1)S(1)}, u32[]{:S(2)}, u32[]{:S(2)}) collective-permute-start(bf16[1424,128]{1,0:T(8,128)(2,1)S(1)} %get-tuple-element.44), channel_id=1, source_target_pairs={{0,1},{1,0},{2,3},{3,2},{4,5},{5,4},{6,7},{7,6},{8,9},{9,8},{10,11... | collective-permute-start | bytes 1093640 | tf_op jit(solution)/shard_map/ppermute | solution.py:444
  2.3 15.0 %collective-permute-start.1 = (bf16[1424,128]{1,0:T(8,128)(2,1)S(1)}, bf16[1424,128]{1,0:T(8,128)(2,1)S(1)}, u32[]{:S(2)}, u32[]{:S(2)}) collective-permute-start(bf16[1424,128]{1,0:T(8,128)(2,1)S(1)} %get-tuple-element.45), channel_id=1, source_target_pairs={{0,255},{1,2},{2,1},{3,4},{4,3},{5,6},{6,5},{7,8},{8,7},{9,10},{10... | collective-permute-start | bytes 1093640 | tf_op jit(solution)/shard_map/ppermute | solution.py:445
  18.6 9.0 %collective-permute-start.2 = (bf16[640,128]{1,0:T(8,128)(2,1)S(1)}, bf16[640,128]{1,0:T(8,128)(2,1)S(1)}, u32[]{:S(2)}, u32[]{:S(2)}) collective-permute-start(bf16[640,128]{1,0:T(8,128)(2,1)S(1)} %get-tuple-element.61), channel_id=1, source_target_pairs={{0,1},{1,0},{2,3},{3,2},{4,5},{5,4},{6,7},{7,6},{8,9},{9,8},{10,11... | collective-permute-start | bytes 491528 | tf_op jit(solution)/shard_map/ppermute | solution.py:444
  18.7 10.3 %collective-permute-start.3 = (bf16[640,128]{1,0:T(8,128)(2,1)S(1)}, bf16[640,128]{1,0:T(8,128)(2,1)S(1)}, u32[]{:S(2)}, u32[]{:S(2)}) collective-permute-start(bf16[640,128]{1,0:T(8,128)(2,1)S(1)} %get-tuple-element.62), channel_id=1, source_target_pairs={{0,255},{1,2},{2,1},{3,4},{4,3},{5,6},{6,5},{7,8},{8,7},{9,10},{10... | collective-permute-start | bytes 491528 | tf_op jit(solution)/shard_map/ppermute | solution.py:445
  30.3 10.1 %collective-permute-start.4 = (bf16[640,128]{1,0:T(8,128)(2,1)S(1)}, bf16[640,128]{1,0:T(8,128)(2,1)S(1)}, u32[]{:S(2)}, u32[]{:S(2)}) collective-permute-start(bf16[640,128]{1,0:T(8,128)(2,1)S(1)} %get-tuple-element.72), channel_id=1, source_target_pairs={{0,1},{1,0},{2,3},{3,2},{4,5},{5,4},{6,7},{7,6},{8,9},{9,8},{10,11... | collective-permute-start | bytes 491528 | tf_op jit(solution)/shard_map/ppermute | solution.py:444
  30.4 10.4 %collective-permute-start.5 = (bf16[640,128]{1,0:T(8,128)(2,1)S(1)}, bf16[640,128]{1,0:T(8,128)(2,1)S(1)}, u32[]{:S(2)}, u32[]{:S(2)}) collective-permute-start(bf16[640,128]{1,0:T(8,128)(2,1)S(1)} %get-tuple-element.73), channel_id=1, source_target_pairs={{0,255},{1,2},{2,1},{3,4},{4,3},{5,6},{6,5},{7,8},{8,7},{9,10},{10... | collective-permute-start | bytes 491528 | tf_op jit(solution)/shard_map/ppermute | solution.py:445

commit v3 on v2

v3 whole, which is shorter than its diff:
```python
import jax
import jax.numpy as jnp
from jax import lax
from jax.experimental import pallas as pl
from jax.experimental.pallas import tpu as pltpu
from jax.sharding import PartitionSpec as P

buoyancy = 0.2
drag_rate = 0.5
time_step = 0.25
keep_shares = (0.0, 0.75, 1.0 / 3.0)

F32 = jnp.float32
BF16 = jnp.bfloat16
LEV = 80
TILE = 128
SMALL = pl.CostEstimate(flops=1000, bytes_accessed=1000, transcendentals=0)
LARGE = pl.CostEstimate(flops=10**9, bytes_accessed=10**6, transcendentals=0)
NEAR = 3 * LEV
NEXT = NEAR + 2 * LEV
MOVE = NEXT + 3 * LEV
SIDE = MOVE + 16


def lanes(block):
    return slice(block * TILE, (block + 1) * TILE)


def advance(anchor, current, slope, keep_share):
    if keep_share == 0.0:
        return current + time_step * slope
    return keep_share * anchor + (1.0 - keep_share) * (current + time_step * slope)


def block_mask(levels_ref, block):
    depth = lax.broadcasted_iota(jnp.int32, (LEV, TILE), 0)
    return (depth < levels_ref[block : block + 1, :]).astype(F32)


def above_weights():
    row = lax.broadcasted_iota(jnp.int32, (LEV, 3 * LEV), 0)
    column = lax.broadcasted_iota(jnp.int32, (LEV, 3 * LEV), 1)
    column = jnp.where(column >= 2 * LEV, column - 2 * LEV, jnp.where(column >= LEV, column - LEV, column))
    return jnp.where(column < row, 1.0, jnp.where(column == row, 0.5, 0.0)).astype(BF16)


def pressure_of(done, above):
    highs, middles, lows = [], [], []
    for thickness, tracer, mask in done:
        weight = thickness * (1.0 - buoyancy * tracer) * mask
        high = weight.astype(BF16)
        rest = weight - high.astype(F32)
        middle = rest.astype(BF16)
        highs.append(high)
        middles.append(middle)
        lows.append((rest - middle.astype(F32)).astype(BF16))
    parts = jnp.concatenate([jnp.concatenate(p, axis=1) for p in (highs, middles, lows)], axis=0)
    return jnp.dot(above, parts, preferred_element_type=F32) * (1.0 / LEV)


def code_blocks(coded, blocks, done, above):
    pressures = pressure_of(done, above)
    for i, (block, (thickness, tracer, mask)) in enumerate(zip(blocks, done)):
        coded[block, 0:LEV, :] = pressures[:, lanes(i)].astype(BF16)
        coded[block, LEV : 2 * LEV, :] = thickness.astype(BF16)
        coded[block, 2 * LEV : NEAR, :] = tracer.astype(BF16)


def edge_step(levels_mask, first, second, gradient, average, velocity, anchor, keep_share):
    slope = jnp.dot(
        jnp.concatenate([first[:LEV], second[:LEV]], axis=1), gradient, preferred_element_type=F32
    )
    carried = jnp.dot(
        jnp.concatenate([first[LEV:], second[LEV:]], axis=1), average, preferred_element_type=F32
    )
    moving = velocity * levels_mask
    flux = jnp.concatenate([carried[:LEV] * moving, carried[LEV:] * moving], axis=0).astype(BF16)
    change = (-slope - drag_rate * velocity) * levels_mask
    return flux, advance(anchor, velocity, change, keep_share)


def cell_step(block, fluxes_ref, sources_ref, first_block, own, whole, tiles_ref):
    picked = []
    for t in range(6):
        offset = sources_ref[t, block] - 3 * first_block
        offset = jnp.where(offset > 3 * own + 2, offset - 3 * whole, jnp.where(offset < -3, offset + 3 * whole, offset))
        picked.append(fluxes_ref[offset + 3])
    return -jnp.dot(jnp.concatenate(picked, axis=1), tiles_ref[block], preferred_element_type=F32)


def other_block(sources_ref, edge, first_block, own, whole):
    offset = sources_ref[1, edge] - first_block
    return jnp.where(offset > own, offset - whole, jnp.where(offset < -1, offset + whole, offset))


def start_kernel(
    own, thickness, tracer, velocity, levels, average, edge_sources, cell_sources,
    inner, outer, levels_out, edge_sources_out, cell_sources_out,
    h, s, v, flat, sems,
):
    position = lax.axis_index("dom")
    whole = own * lax.axis_size("dom")
    inner_side = 1 - lax.rem(position, 2)
    ends = []
    for p, side in ((0, inner_side), (1, 1 - inner_side)):
        block = side * (own - 1)
        ends.append((p, side, block, block + 1 - 2 * side))

    def columns(block, wide):
        return pl.ds(pl.multiple_of(block * TILE, TILE), wide)

    small = [
        pltpu.make_async_copy(levels, flat, sems.at[0]),
        pltpu.make_async_copy(edge_sources, edge_sources_out, sems.at[1]),
        pltpu.make_async_copy(cell_sources, cell_sources_out, sems.at[2]),
    ]
    fields, tiles = [], []
    for p, side, block, after in ends:
        for k, b in ((0, block), (1, after)):
            fields.append(pltpu.make_async_copy(thickness.at[:, columns(b, TILE)], h.at[p, k], sems.at[3 + 4 * p + 2 * k]))
            fields.append(pltpu.make_async_copy(tracer.at[:, columns(b, TILE)], s.at[p, k], sems.at[4 + 4 * p + 2 * k]))
        fields.append(pltpu.make_async_copy(velocity.at[:, columns(3 * block, 3 * TILE)], v.at[p], sems.at[11 + p]))
        message = (inner, outer)[p]
        rows = pl.ds(pl.multiple_of(block * 6 * TILE, 6 * TILE), 6 * TILE)
        tiles.append(pltpu.make_async_copy(average.at[rows, :], message.at[pl.ds(SIDE, 6 * TILE), :], sems.at[13 + p]))
    for copy in small + fields + tiles:
        copy.start()
    above = above_weights()
    for copy in small:
        copy.wait()
    for block in range(own):
        levels_out[block] = flat[lanes(block)]
    for copy in fields:
        copy.wait()
    done = []
    for p, side, block, after in ends:
        depth = lax.broadcasted_iota(jnp.int32, (LEV, TILE), 0)
        done.append((h[p, 0], s[p, 0], (depth < levels_out[pl.ds(block, 1), :]).astype(F32)))
    pressures = pressure_of(done, above)
    for p, side, block, after in ends:
        message = (inner, outer)[p]
        mask = done[p][2]
        message[0:LEV, :] = pressures[:, lanes(p)].astype(BF16)
        message[LEV : 2 * LEV, :] = h[p, 0].astype(BF16)
        message[2 * LEV : NEAR, :] = s[p, 0].astype(BF16)
        message[NEAR : NEAR + LEV, :] = h[p, 1].astype(BF16)
        message[NEAR + LEV : NEXT, :] = s[p, 1].astype(BF16)
        row = lax.broadcasted_iota(jnp.int32, (16, TILE), 0)
        signs = jnp.zeros((16, TILE), F32)
        for j in range(3):
            message[NEXT + j * LEV : NEXT + (j + 1) * LEV, :] = (v[p, :, lanes(j)] * mask).astype(BF16)
            low = other_block(edge_sources_out, j, position * own, own, whole)
            high = other_block(edge_sources_out, 3 * (own - 1) + j, position * own, own, whole) - (own - 1)
            signs = jnp.where(row == j, jnp.where(side == 0, low, high).astype(F32), signs)
        message[MOVE:SIDE, :] = signs.astype(BF16)
    for copy in tiles:
        copy.wait()


def first_inside(
    own, keep_share, h0, s0, v0, levels, gradient, average, edge_sources, divergence, cell_sources,
    fluxes, new_coded, new_thickness, new_tracer, new_velocity, coded,
):
    done = [(h0[:, lanes(b)], s0[:, lanes(b)], block_mask(levels, b)) for b in range(own)]
    code_blocks(coded, range(own), done, above_weights())
    inside_edges(own, keep_share, coded, v0, v0, levels, gradient, average, edge_sources, fluxes, new_velocity)
    inside_cells(
        own, keep_share, fluxes, h0, s0, h0, s0, levels, divergence, cell_sources,
        new_coded, new_thickness, new_tracer,
    )


def on(odd, work):
    pl.when(lax.rem(lax.axis_index("dom"), 2) == (1 if odd else 0))(work)


def odd_inside(
    own, keep_share, coded, velocity, velocity0, levels, gradient, average, edge_sources,
    thickness, tracer, thickness0, tracer0, divergence, cell_sources,
    fluxes, new_velocity, new_thickness, new_tracer,
):
    def work():
        inside_edges(
            own, keep_share, coded, velocity, velocity0, levels, gradient, average, edge_sources, fluxes, new_velocity
        )
        inside_cells(
            own, keep_share, fluxes, thickness, tracer, thickness0, tracer0, levels, divergence, cell_sources,
            None, new_thickness, new_tracer,
        )

    on(True, work)


def even_edges(own, keep_share, *refs):
    on(False, lambda: inside_edges(own, keep_share, *refs[:7], *refs[9:]))


def even_cells(own, keep_share, *refs):
    on(False, lambda: inside_cells(own, keep_share, *refs[:8], None, *refs[10:]))


def tick(own, keep_share, *refs):
    pass


def inside_edges(
    own, keep_share, coded, velocity, velocity0, levels, gradient, average, edge_sources, fluxes, new_velocity,
    wait=None,
):
    whole = own * lax.axis_size("dom")
    first_block = lax.axis_index("dom") * own
    for block in range(1, own - 1):
        if wait is not None:
            wait(block)
        mask = block_mask(levels, block)
        for edge in range(3 * block, 3 * block + 3):
            other = other_block(edge_sources, edge, first_block, own, whole)
            flux, updated = edge_step(
                mask, coded[block], coded[other], gradient[edge], average[edge],
                velocity[:, lanes(edge)], velocity0[:, lanes(edge)], keep_share,
            )
            fluxes[edge + 3] = flux
            new_velocity[:, lanes(edge)] = updated


def inside_cells(
    own, keep_share, fluxes, thickness, tracer, thickness0, tracer0, levels, divergence, cell_sources,
    new_coded, new_thickness, new_tracer, wait=None,
):
    whole = own * lax.axis_size("dom")
    first_block = lax.axis_index("dom") * own
    done = []
    for block in range(2, own - 2):
        if wait is not None:
            wait(block)
        done.append(
            finish_cell(
                block, own, keep_share, first_block, whole,
                thickness, tracer, thickness0, tracer0, levels, divergence, cell_sources,
                fluxes, new_thickness, new_tracer,
            )
        )
    if new_coded is not None:
        code_blocks(new_coded, range(2, own - 2), done, above_weights())


def finish_cell(
    block, own, keep_share, first_block, whole,
    thickness, tracer, thickness0, tracer0, levels, divergence, cell_sources,
    fluxes, new_thickness, new_tracer,
):
    at = lanes(block)
    mask = block_mask(levels, block)
    change = cell_step(block, fluxes, cell_sources, first_block, own, whole, divergence)
    h = advance(thickness0[:, at], thickness[:, at], change[:LEV] * mask, keep_share)
    s = advance(tracer0[:, at], tracer[:, at], change[LEV:] * mask, keep_share)
    new_thickness[:, at] = h
    new_tracer[:, at] = s
    return h, s, mask


def rim_step(
    odd, own, keep_share, last,
    outer_in, inner_in, tiles_outer, tiles_inner,
    coded, thickness, tracer, velocity, thickness0, tracer0, velocity0, levels,
    gradient, average, edge_sources, divergence, cell_sources,
    fluxes, new_coded, new_thickness, new_tracer, new_velocity, pair,
    inner, outer, send,
):
    above = above_weights()
    first_block = lax.axis_index("dom") * own
    whole = own * lax.axis_size("dom")
    halos = (inner_in, outer_in) if odd else (outer_in, inner_in)
    halo_tiles = (tiles_inner, tiles_outer) if odd else (tiles_outer, tiles_inner)
    messages = (inner, outer) if odd else (outer, inner)
    ends = ((0, 0, 1), (1, own - 1, own - 2))

    for side, block, after in ends:
        mask = block_mask(levels, block)
        outward = 2 * side - 1
        beyond = -1 if side == 0 else own
        halo, tiles = halos[side], halo_tiles[side]
        pair[side, 0] = halo[0:NEAR, :]
        pair[side, 1] = coded[after]
        signs = tiles[MOVE:SIDE, :].astype(F32)
        for j in range(3):
            edge = 3 * block + j
            other = other_block(edge_sources, edge, first_block, own, whole)
            flux, updated = edge_step(
                mask, coded[block], pair[side, (other == after).astype(jnp.int32)], gradient[edge], average[edge],
                velocity[:, lanes(edge)], velocity0[:, lanes(edge)], keep_share,
            )
            fluxes[edge + 3] = flux
            new_velocity[:, lanes(edge)] = updated
            toward = signs[j : j + 1, :] * outward
            second = jnp.where(
                jnp.broadcast_to(toward, (2 * LEV, TILE)) > 0.0,
                halo[NEAR:NEXT, :].astype(F32),
                coded[block, LEV:, :].astype(F32),
            ).astype(BF16)
            carried = jnp.dot(
                jnp.concatenate([halo[LEV:NEAR, :], second], axis=1),
                tiles[SIDE + j * 256 : SIDE + (j + 1) * 256, :],
                preferred_element_type=F32,
            )
            moving = halo[NEXT + j * LEV : NEXT + (j + 1) * LEV, :].astype(F32)
            fluxes[3 * beyond + 3 + j] = jnp.concatenate(
                [carried[:LEV] * moving, carried[LEV:] * moving], axis=0
            ).astype(BF16)
            if not last:
                messages[side][NEXT + j * LEV : NEXT + (j + 1) * LEV, :] = (updated * mask).astype(BF16)
        if last:
            send(2, 3 * block, 3)
    rim = (0, 1, own - 2, own - 1)
    done = []
    for block in rim:
        done.append(
            finish_cell(
                block, own, keep_share, first_block, whole,
                thickness, tracer, thickness0, tracer0, levels, divergence, cell_sources,
                fluxes, new_thickness, new_tracer,
            )
        )
        if last and block in (1, own - 1):
            send(0, block - 1, 2)
            send(1, block - 1, 2)
    if last:
        return
    code_blocks(new_coded, rim, done, above)
    for side, block, after in ends:
        messages[side][0:NEAR, :] = new_coded[block]
        messages[side][NEAR:NEXT, :] = new_coded[after, LEV:, :]


def rim_kernel(odd, second, own, keep_share, *refs):
    common = refs[:17]
    out = refs[17 + 5 + (1 if second else 0) :]
    built, inner, outer, pair = out[:5], out[5], out[6], out[7]

    @pl.when(lax.rem(lax.axis_index("dom"), 2) == (1 if odd else 0))
    def _():
        rim_step(odd, own, keep_share, False, *common, *built, pair, inner, outer, None)


def last_rim_kernel(own, keep_share, *refs):
    inner_in, up_in, down_in, tiles_inner, tiles_up, tiles_down = refs[:6]
    common = refs[6:19]
    fluxes, h, s, v, far_h, far_s, far_v, pair, sems = refs[23:]
    here, far = (h, s, v), (far_h, far_s, far_v)
    odd_here = lax.rem(lax.axis_index("dom"), 2)
    whole = []
    for which in (2, 0, 1):
        lo, wide = (3, 3 * (own - 2)) if which == 2 else (2, own - 4)
        at = (slice(None), pl.ds(lo * TILE, wide * TILE))
        whole.append(pltpu.make_async_copy(here[which].at[at], far[which].at[at], sems.at[which]))
        whole[-1].start()

    for odd in (False, True):

        @pl.when(odd_here == (1 if odd else 0))
        def _(odd=odd):
            sent = []

            def send(which, lo, wide):
                at = (slice(None), pl.ds(lo * TILE, wide * TILE))
                copy = pltpu.make_async_copy(here[which].at[at], far[which].at[at], sems.at[3 + len(sent)])
                copy.start()
                sent.append(copy)

            rim_step(
                odd, own, keep_share, True,
                down_in if odd else up_in, inner_in, tiles_down if odd else tiles_up, tiles_inner,
                *common, fluxes, None, h, s, v, pair, None, None, send,
            )
            for copy in sent:
                copy.wait()

    for copy in whole:
        copy.wait()


def in_vmem(array):
    return pltpu.with_memory_space_constraint(array, pltpu.VMEM)


def in_hbm(array):
    return pltpu.with_memory_space_constraint(array, pltpu.HBM)


def local(
    thickness,
    tracer,
    velocity,
    active_levels,
    gradient_tiles,
    average_tiles,
    edge_sources,
    divergence_tiles,
    cell_sources,
):
    own = cell_sources.shape[0]
    devices = lax.axis_size("dom")
    within = [(i, i ^ 1) for i in range(devices)]
    upward = [(i, (i + 1) % devices) for i in range(devices)]
    filler = {1: 1, 3: -3, 5: -1, 7: -1}
    downward = [(i, (i + filler[i % 8]) % devices if i % 2 else (i - 1) % devices) for i in range(devices)]
    cells, edges = thickness.shape[1], velocity.shape[1]
    vmem = pl.BlockSpec(memory_space=pltpu.VMEM)
    hbm = pl.BlockSpec(memory_space=pltpu.HBM)
    params = pltpu.CompilerParams(vmem_limit_bytes=16 * 1024 * 1024)

    gradient = (gradient_tiles.reshape(3 * own, 2 * TILE, TILE))
    average = (average_tiles.reshape(3 * own, 2 * TILE, TILE))
    average_rows = in_hbm(average_tiles.reshape(3 * own * 2 * TILE, TILE))
    divergence = (divergence_tiles.reshape(own, 6 * TILE, TILE))
    first_rows = SIDE + 6 * TILE

    def message(rows):
        return pltpu.VMEM((rows, TILE), BF16)

    inner, outer, levels, edge_sources, cell_sources = pl.pallas_call(
        lambda *refs: start_kernel(own, *refs),
        out_shape=(
            message(first_rows),
            message(first_rows),
            pltpu.VMEM((own, TILE), jnp.int32),
            pltpu.VMEM((2, 3 * own), jnp.int32),
            pltpu.VMEM((6, own), jnp.int32),
        ),
        in_specs=[hbm] * 7,
        out_specs=[vmem] * 5,
        scratch_shapes=[
            pltpu.VMEM((2, 2, LEV, TILE), F32),
            pltpu.VMEM((2, 2, LEV, TILE), F32),
            pltpu.VMEM((2, LEV, 3 * TILE), F32),
            pltpu.VMEM((cells,), jnp.int32),
            pltpu.SemaphoreType.DMA((15,)),
        ],
        compiler_params=params,
        cost_estimate=pl.CostEstimate(flops=2 * 10**10, bytes_accessed=10**6, transcendentals=0),
        name="start",
    )(in_hbm(thickness), in_hbm(tracer), in_hbm(velocity), in_hbm(active_levels), average_rows, in_hbm(edge_sources.T), in_hbm(cell_sources.T))

    coded_shape = pltpu.VMEM((own, NEAR, TILE), BF16)
    field_shapes = (
        pltpu.VMEM((LEV, cells), F32),
        pltpu.VMEM((LEV, cells), F32),
        pltpu.VMEM((LEV, edges), F32),
    )
    flux_shape = pltpu.VMEM((3 * own + 6, 2 * LEV, TILE), BF16)
    built_shapes = (flux_shape, coded_shape) + field_shapes
    pair_scratch = pltpu.VMEM((2, 2, NEAR, TILE), BF16)

    def send_up(x):
        return lax.ppermute(x, "dom", upward)

    def send_down(x):
        return lax.ppermute(x, "dom", downward)

    def swap_inner(x):
        return lax.ppermute(x, "dom", within)

    def rim(odd, keep_share, inner_in, outer_in, tiles_outer, common, built, inner):
        second = inner is not None
        extra = (inner,) if second else ()
        out = pl.pallas_call(
            lambda *refs: rim_kernel(odd, second, own, keep_share, *refs),
            out_shape=built_shapes + (message(MOVE), message(MOVE)),
            in_specs=[vmem] * (17 + 5 + len(extra)),
            out_specs=[vmem] * 7,
            scratch_shapes=[pair_scratch],
            input_output_aliases={17 + i: i for i in range(5 + len(extra))},
            compiler_params=params,
            cost_estimate=LARGE,
            name="rim_odd" if odd else "rim_even",
        )(outer_in, inner_in, tiles_outer, tiles_inner, *common, *built, *extra)
        return out[:5], out[5], out[6]

    def call(body, keep_share, operands, shapes, specs, scratch, name, after=None, passed=None, filled=()):
        n = len(operands)
        extra = tuple(x for x in (after, passed) if x is not None)
        given = tuple(x for x in (passed,) if x is not None) + filled
        total = n + len(extra) + len(filled)
        first = 0 if passed is None else 1
        return pl.pallas_call(
            lambda *refs: body(own, keep_share, *refs[:n], *refs[n + len(extra) : total], *refs[total + first :]),
            out_shape=tuple(pltpu.VMEM(x.shape, x.dtype) for x in given) + shapes,
            in_specs=[vmem] * total,
            out_specs=[vmem] * len(given) + specs,
            input_output_aliases={total - len(given) + i: i for i in range(len(given))},
            scratch_shapes=scratch,
            compiler_params=params,
            cost_estimate=SMALL,
            name=name,
        )(*operands, *extra, *filled)

    def edges_inside(keep_share, common, passed=None):
        operands = (common[0], common[3], common[6], *common[7:11])
        shapes = (flux_shape, field_shapes[2])
        return call(inside_edges, keep_share, operands, shapes, [vmem] * 2, [], "inside_edges", passed=passed)

    def cell_operands(fluxes, common):
        return (fluxes, common[1], common[2], common[4], common[5], common[7], common[11], common[12])

    up_in, down_in = lax.ppermute(outer, "dom", upward), lax.ppermute(outer, "dom", [(j, i) for i, j in upward])
    anchor = (in_vmem(thickness), in_vmem(tracer), in_vmem(velocity))
    gradient, average, divergence = in_vmem(gradient), in_vmem(average), in_vmem(divergence)
    loaded = call(
        first_inside, keep_shares[0],
        (*anchor, levels, gradient, average, edge_sources, divergence, cell_sources),
        built_shapes + (coded_shape,), [vmem] * 6, [], "inside",
    )
    built, coded = loaded[:5], loaded[5]
    inner_in = swap_inner(inner)
    tiles_up, tiles_down, tiles_inner = up_in, down_in, inner_in

    def operands(coded, state):
        return (coded, *state, *anchor, levels, gradient, average, edge_sources, divergence, cell_sources)

    common = operands(coded, anchor)
    built, inner, outer = rim(False, keep_shares[0], inner_in, up_in, tiles_up, common, built, None)
    next_down = send_down(outer)
    built, inner, outer = rim(True, keep_shares[0], inner_in, down_in, tiles_down, common, built, inner)
    next_up = send_up(outer)
    up_in, down_in, inner_in = next_up, next_down, swap_inner(inner)

    common = operands(built[1], built[2:5])
    fluxes, new_velocity = edges_inside(keep_shares[1], common)
    new_cells = call(
        inside_cells, keep_shares[1], cell_operands(fluxes, common), (coded_shape,) + field_shapes[:2],
        [vmem] * 3, [], "inside_cells", after=down_in,
    )
    built = (fluxes, *new_cells, new_velocity)
    built, inner, outer = rim(True, keep_shares[1], inner_in, down_in, tiles_down, common, built, None)
    next_up = send_up(outer)
    built, inner, outer = rim(False, keep_shares[1], inner_in, up_in, tiles_up, common, built, inner)
    up_in, down_in = next_up, send_down(outer)

    common = operands(built[1], built[2:5])
    far_shapes = (pltpu.HBM((LEV, cells), F32), pltpu.HBM((LEV, cells), F32), pltpu.HBM((LEV, edges), F32))
    edge_operands = (common[0], common[3], common[6], *common[7:11])
    inner, fluxes, new_velocity, h, s = call(
        odd_inside, keep_shares[2],
        edge_operands + (common[1], common[2], common[4], common[5], common[11], common[12]),
        (flux_shape, field_shapes[2]) + field_shapes[:2], [vmem] * 4, [], "odd_inside", passed=inner,
    )
    inner_in = swap_inner(inner)
    fluxes = call(tick, 0.0, (up_in,), (), [], [], "tick", passed=fluxes)[0]
    fluxes, new_velocity = call(
        even_edges, keep_shares[2], edge_operands, (), [], [], "even_edges", filled=(fluxes, new_velocity)
    )
    h, s = call(
        even_cells, keep_shares[2], cell_operands(fluxes, common), (), [], [], "even_cells", filled=(h, s)
    )
    results = pl.pallas_call(
        lambda *refs: last_rim_kernel(own, keep_shares[2], *refs),
        out_shape=(flux_shape,) + field_shapes + far_shapes,
        in_specs=[vmem] * 23,
        out_specs=[vmem] * 4 + [hbm] * 3,
        scratch_shapes=[pair_scratch, pltpu.SemaphoreType.DMA((9,))],
        input_output_aliases={19 + i: i for i in range(4)},
        compiler_params=params,
        cost_estimate=SMALL,
        name="rim",
    )(inner_in, up_in, down_in, tiles_inner, tiles_up, tiles_down, *common, fluxes, h, s, new_velocity)
    return results[4:]


def solution(mesh):
    return jax.shard_map(
        local,
        mesh=mesh,
        in_specs=(
            P(None, "dom"),
            P(None, "dom"),
            P(None, "dom"),
            P("dom"),
            P("dom", None, None, None),
            P("dom", None, None, None),
            P("dom", None),
            P("dom", None, None, None),
            P("dom", None),
        ),
        out_specs=(P(None, "dom"), P(None, "dom"), P(None, "dom")),
        check_vma=False,
    )
```

time: 42.9 us -> 38.7 us (0.902)
  waiting for transfers between devices: 1.88 us -> 10.7 us
  starting transfers between devices: 21.8 us -> 13.2 us
  Pallas kernels: 18.2 us -> 13.6 us
    ppermute x6 -> x9, waiting for transfers between devices: 1.88 us -> 10.7 us  [the longest x2 5.65 us: send_up(): return lax.ppermute(x, 'dom', upward)]
    ppermute x6 -> x9, starting transfers between devices: 21.8 us -> 13.2 us  [the longest x1 8.37 us: local(): lax.ppermute(outer, 'dom', [(j, i) for i, j in upward])]
    pallas_call x6 -> x12, Pallas kernels: 16.6 us -> 11.9 us  [the longest x7 7.68 us: call(): pl.pallas_call(lambda *refs: body(own, keep_share, *refs[:n], *refs[n + l...]
  transfers between devices with their start and end apart: 6 -> 9, of which waited for: 2 -> 4; matrix products, arithmetic and copies ran while one was open for 0% -> 0% of each run, Pallas kernels for 28% -> 26%
where the time goes in v3:
time: 38.7 us; the launch traced here: 38.5 us
  Pallas kernels  13.6 us (35%)
  starting transfers between devices  13.2 us (34%)
  waiting for transfers between devices  10.7 us (28%)
  between operations  0.99 us (3%)
    ppermute x1, starting transfers between devices, local(): lax.ppermute(outer, 'dom', [(j, i) for i, j in upward])  8.37 us
    pallas_call x7, Pallas kernels, call(): pl.pallas_call(lambda *refs: body(own, keep_share, *refs[:n], *refs[n + l...  7.68 us
    ppermute x2, waiting for transfers between devices, send_up(): return lax.ppermute(x, 'dom', upward)  5.65 us
    ppermute x2, waiting for transfers between devices, send_down(): return lax.ppermute(x, 'dom', downward)  2.56 us
    pallas_call x4, Pallas kernels, rim(): pl.pallas_call(lambda *refs: rim_kernel(odd, second, own, keep_share, *re...  2.49 us
    ppermute x1, waiting for transfers between devices, local(): lax.ppermute(outer, 'dom', upward)  2.47 us
    ppermute x2, starting transfers between devices, send_up(): return lax.ppermute(x, 'dom', upward)  2.32 us
    ppermute x2, starting transfers between devices, send_down(): return lax.ppermute(x, 'dom', downward)  1.81 us
  transfers between devices with their start and end apart: 9, of which 4 were waited for; matrix products, arithmetic and copies ran while one was open for 0% of the time, Pallas kernels for 26%

profile of v3, /device:TPU:0, one launch (start us, length us, event | category | flops | bytes accessed | tf_op | source)
XLA Modules:
  0.0 38.5 jit_solution(15609607350445542294)
XLA Ops:
  0.7 1.6 %start.1 = (bf16[1424,128]{1,0:T(8,128)(2,1)S(1)}, bf16[1424,128]{1,0:T(8,128)(2,1)S(1)}, s32[13,128]{1,0:T(8,128)S(1)}, s32[2,39]{1,0:T(2,128)S(1)}, s32[6,13]{1,0:T(8,128)S(1)}) custom-call(f32[80,1664]{1,0:T(8,128)} %refs_10_.11, f32[80,1664]{1,0:T(8,128)} %refs_11_.1, f32[80,4992]{1,0:T(8,128)} %refs_12_.1, s32[1664]{0:T(1024)} %refs_3_.3, ...), custom_call_target="tpu_custom_call" | custom-call | flops 20000000000 | bytes 1000000 | tf_op jit(solution)/shard_map/start/pallas_call | solution.py:421
  2.4 0.1 collective-permute-start.1
  2.5 0.5 %collective-permute-start.2 = (bf16[1424,128]{1,0:T(8,128)(2,1)S(1)}, bf16[1424,128]{1,0:T(8,128)(2,1)S(1)}, u32[]{:S(2)}, u32[]{:S(2)}) collective-permute-start(bf16[1424,128]{1,0:T(8,128)(2,1)S(1)} %get-tuple-element.57), channel_id=1, source_target_pairs={{0,1},{1,2},{2,3},{3,4},{4,5},{5,6},{6,7},{7,8},{8,9},{9,10},{10,1... | collective-permute-start | bytes 1093640 | tf_op jit(solution)/shard_map/ppermute | solution.py:505
  2.9 8.4 %collective-permute-start = (bf16[1424,128]{1,0:T(8,128)(2,1)S(1)}, bf16[1424,128]{1,0:T(8,128)(2,1)S(1)}, u32[]{:S(2)}, u32[]{:S(2)}) collective-permute-start(bf16[1424,128]{1,0:T(8,128)(2,1)S(1)} %get-tuple-element.57), channel_id=1, source_target_pairs={{1,0},{2,1},{3,2},{4,3},{5,4},{6,5},{7,6},{8,7},{9,8},{10,9},{11,1... | collective-permute-start | bytes 1093640 | tf_op jit(solution)/shard_map/ppermute | solution.py:505
  11.4 2.6 %inside.1 = (bf16[45,160,128]{2,1,0:T(8,128)(2,1)S(1)}, bf16[13,240,128]{2,1,0:T(8,128)(2,1)S(1)}, f32[80,1664]{1,0:T(8,128)S(1)}, f32[80,1664]{1,0:T(8,128)S(1)...) custom-call(f32[80,1664]{1,0:T(8,128)S(1)} %copy-done.4, f32[80,1664]{1,0:T(8,128)S(1)} %copy-done.5, ...), custom_call_target="tpu_custom_call" | custom-call | flops 1000 | bytes 1000 | tf_op jit(solution)/shard_map/inside/pallas_call | solution.py:485
  14.0 0.0 collective-permute-done.1.refs_1_.refs_3_
  14.0 2.5 %collective-permute-done.2.refs_0_.refs_2_.refs_4_ = bf16[1424,128]{1,0:T(8,128)(2,1)S(1)} collective-permute-done((bf16[1424,128]{1,0:T(8,128)(2,1)S(1)}, bf16[1424,128]{1,0:T(8,128)(2,1)S(1)}, u32[]{:S(2)}, u32[]{:S(2)}) %collective-permute-start.2) | collective-permute-done | bytes 364576 | tf_op jit(solution)/shard_map/ppermute | solution.py:505
  16.5 1.2 %rim_even.2 = (bf16[45,160,128]{2,1,0:T(8,128)(2,1)S(1)}, bf16[13,240,128]{2,1,0:T(8,128)(2,1)S(1)}, f32[80,1664]{1,0:T(8,128)S(1)}, f32[80,1664]{1,0:T(8,128)S(...) custom-call(bf16[1424,128]{1,0:T(8,128)(2,1)S(1)} %collective-permut, ...), custom_call_target="tpu_custom_call", output_to_operand_aliasing={{0}: (17, {}), {1}: (18, {}), {2}: (19, {}), {3}: (20, {}),... | custom-call | flops 1000000000 | bytes 1000000 | tf_op jit(solution)/shard_map/rim_even/pallas_call | solution.py:466
  17.7 0.1 collective-permute-start.5
  17.8 0.0 collective-permute-done.refs_0_.refs_2_.refs_5_
  17.8 0.1 collective-permute-start.4
  17.9 0.5 %collective-permute-start.3 = (bf16[640,128]{1,0:T(8,128)(2,1)S(1)}, bf16[640,128]{1,0:T(8,128)(2,1)S(1)}, u32[]{:S(2)}, u32[]{:S(2)}) collective-permute-start(bf16[640,128]{1,0:T(8,128)(2,1)S(1)} %get-tuple-element.74), channel_id=1, source_target_pairs={{0,1},{1,2},{2,3},{3,4},{4,5},{5,6},{6,7},{7,8},{8,9},{9,10},{10,1... | collective-permute-start | bytes 491528 | tf_op jit(solution)/shard_map/ppermute | solution.py:455
  18.4 1.5 %inside_edges.1 = (bf16[45,160,128]{2,1,0:T(8,128)(2,1)S(1)}, f32[80,4992]{1,0:T(8,128)S(1)}) custom-call(bf16[13,240,128]{2,1,0:T(8,128)(2,1)S(1)} %get-tuple-element.76.refs_0_.refs_4_, f32[80,4992]{1,0:T(8,128)S(1)} %get-tuple-element.79.refs_1_.refs_7_, f32[80,4992]{1,0:T(8,128)S(1)} %copy-done.3, ...), custom_call_target="tpu_custom_call" | custom-call | flops 1000 | bytes 1000 | tf_op jit(solution)/shard_map/inside_edges/pallas_call | solution.py:485
  19.9 2.6 %collective-permute-done.5.refs_8_.refs_0_ = bf16[640,128]{1,0:T(8,128)(2,1)S(1)} collective-permute-done((bf16[640,128]{1,0:T(8,128)(2,1)S(1)}, bf16[640,128]{1,0:T(8,128)(2,1)S(1)}, u32[]{:S(2)}, u32[]{:S(2)}) %collective-permute-start.5) | collective-permute-done | bytes 163872 | tf_op jit(solution)/shard_map/ppermute | solution.py:458
  22.5 1.1 %inside_cells.1 = (bf16[13,240,128]{2,1,0:T(8,128)(2,1)S(1)}, f32[80,1664]{1,0:T(8,128)S(1)}, f32[80,1664]{1,0:T(8,128)S(1)}) custom-call(bf16[45,160,128]{2,1,0:T(8,128)(2,1)S(1)} %get-tuple-element.81.refs_0_.refs_17_, f32[80,1664]{1,0:T(8,128)S(1)} %get-tuple-element.77.refs_1_.refs_5_, f32[80,1664]{1,0:T(8,128)S(1)} %get-tuple-element.78.refs_2_.refs_6_, ...), custom_call_target="tpu_custom_call" | custom-call | flops 1000 | bytes 1000 | tf_op jit(solution)/shard_map/inside_cells/pallas_call | solution.py:485
  23.7 1.8 %collective-permute-start.7 = (bf16[640,128]{1,0:T(8,128)(2,1)S(1)}, bf16[640,128]{1,0:T(8,128)(2,1)S(1)}, u32[]{:S(2)}, u32[]{:S(2)}) collective-permute-start(bf16[640,128]{1,0:T(8,128)(2,1)S(1)} %get-tuple-element.98), channel_id=1, source_target_pairs={{0,1},{1,2},{2,3},{3,4},{4,5},{5,6},{6,7},{7,8},{8,9},{9,10},{10,1... | collective-permute-start | bytes 491528 | tf_op jit(solution)/shard_map/ppermute | solution.py:455
  25.5 2.7 %collective-permute-done.3.refs_0_ = bf16[640,128]{1,0:T(8,128)(2,1)S(1)} collective-permute-done((bf16[640,128]{1,0:T(8,128)(2,1)S(1)}, bf16[640,128]{1,0:T(8,128)(2,1)S(1)}, u32[]{:S(2)}, u32[]{:S(2)}) %collective-permute-start.3) | collective-permute-done | bytes 163872 | tf_op jit(solution)/shard_map/ppermute | solution.py:455
  28.2 1.2 %rim_even.3 = (bf16[45,160,128]{2,1,0:T(8,128)(2,1)S(1)}, bf16[13,240,128]{2,1,0:T(8,128)(2,1)S(1)}, f32[80,1664]{1,0:T(8,128)S(1)}, f32[80,1664]{1,0:T(8,128)S(...) custom-call(bf16[640,128]{1,0:T(8,128)(2,1)S(1)} %collective-permute, ...), custom_call_target="tpu_custom_call", output_to_operand_aliasing={{0}: (17, {}), {1}: (18, {}), {2}: (19, {}), {3}: (20, {}),... | custom-call | flops 1000000000 | bytes 1000000 | tf_op jit(solution)/shard_map/rim_even/pallas_call | solution.py:466
  29.4 1.7 %collective-permute-start.8 = (bf16[640,128]{1,0:T(8,128)(2,1)S(1)}, bf16[640,128]{1,0:T(8,128)(2,1)S(1)}, u32[]{:S(2)}, u32[]{:S(2)}) collective-permute-start(bf16[640,128]{1,0:T(8,128)(2,1)S(1)} %get-tuple-element.99), channel_id=1, source_target_pairs={{0,255},{1,2},{2,1},{3,0},{4,3},{5,4},{6,5},{7,6},{8,7},{9,10},{10... | collective-permute-start | bytes 491528 | tf_op jit(solution)/shard_map/ppermute | solution.py:458
  31.1 0.0 collective-permute-start.6
  31.1 3.0 %collective-permute-done.7.refs_0_.refs_1_ = bf16[640,128]{1,0:T(8,128)(2,1)S(1)} collective-permute-done((bf16[640,128]{1,0:T(8,128)(2,1)S(1)}, bf16[640,128]{1,0:T(8,128)(2,1)S(1)}, u32[]{:S(2)}, u32[]{:S(2)}) %collective-permute-start.7) | collective-permute-done | bytes 163872 | tf_op jit(solution)/shard_map/ppermute | solution.py:455
  34.1 1.5 %even_edges.1 = (bf16[45,160,128]{2,1,0:T(8,128)(2,1)S(1)}, f32[80,4992]{1,0:T(8,128)S(1)}) custom-call(bf16[13,240,128]{2,1,0:T(8,128)(2,1)S(1)} %get-tuple-element.92.refs_0_.refs_6_, f32[80,4992]{1,0:T(8,128)S(1)} %get-tuple-element.93.refs_1_.refs_9_, f32[80,4992]{1,0:T(8,128)S(1)} %copy-done.3, ...), custom_call_target="tpu_custom_call", output_to_operand_aliasing={{0}: (7, {}), {1}: (8, {})} | custom-call | flops 1000 | bytes 1000 | tf_op jit(solution)/shard_map/even_edges/pallas_call | solution.py:485
  35.6 0.9 %even_cells.1 = (f32[80,1664]{1,0:T(8,128)S(1)}, f32[80,1664]{1,0:T(8,128)S(1)}) custom-call(bf16[45,160,128]{2,1,0:T(8,128)(2,1)S(1)} %get-tuple-element.102.refs_0_.refs_19_, f32[80,1664]{1,0:T(8,128)S(1)} %get-tuple-element.94.refs_7_.refs_1_, f32[80,1664]{1,0:T(8,128)S(1)} %get-tuple-element.95.refs_8_.refs_2_, ...), custom_call_target="tpu_custom_call", output_to_operand_aliasing={{0}: (8, {}), {1}: (9, {})} | custom-call | flops 1000 | bytes 1000 | tf_op jit(solution)/shard_map/even_cells/pallas_call | solution.py:485
  36.6 1.7 %rim.1 = (bf16[45,160,128]{2,1,0:T(8,128)(2,1)S(1)}, f32[80,1664]{1,0:T(8,128)S(1)}, f32[80,1664]{1,0:T(8,128)S(1)}, f32[80,4992]{1,0:T(8,128)S(1)}, f32[80,1664...) custom-call(bf16[640,128]{1,0:T(8,128)(2,1)S(1)} %collective-permute, ...), custom_call_target="tpu_custom_call", output_to_operand_aliasing={{0}: (19, {}), {1}: (20, {}), {2}: (21, {}), {3}: (22, {})} | custom-call | flops 1000 | bytes 1000 | tf_op jit(solution)/shard_map/rim/pallas_call | solution.py:555
  (19 shorter events, 0.1 us)
Async XLA Ops:
  0.6 10.7 %copy-start = (bf16[39,2,128,128]{3,2,1,0:T(8,128)(2,1)S(1)}, bf16[39,2,128,128]{3,2,1,0:T(8,128)(2,1)}, u32[]{:S(2)}) copy-start(bf16[39,2,128,128]{3,2,1,0:T(8,128)(2,1)} %param.14) | copy-start | bytes 7667716
  0.6 10.7 %copy-start.1 = (bf16[39,2,128,128]{3,2,1,0:T(8,128)(2,1)S(1)}, bf16[39,2,128,128]{3,2,1,0:T(8,128)(2,1)}, u32[]{:S(2)}) copy-start(bf16[39,2,128,128]{3,2,1,0:T(8,128)(2,1)} %param.13) | copy-start | bytes 7667716
  0.7 10.7 %copy-start.2 = (bf16[13,6,128,128]{3,2,1,0:T(8,128)(2,1)S(1)}, bf16[13,6,128,128]{3,2,1,0:T(8,128)(2,1)}, u32[]{:S(2)}) copy-start(bf16[13,6,128,128]{3,2,1,0:T(8,128)(2,1)} %param.16) | copy-start | bytes 7667716
  0.7 10.7 %copy-start.3 = (f32[80,4992]{1,0:T(8,128)S(1)}, f32[80,4992]{1,0:T(8,128)}, u32[]{:S(2)}) copy-start(f32[80,4992]{1,0:T(8,128)} %refs_12_.1) | copy-start | bytes 4792324
  0.7 10.7 %copy-start.4 = (f32[80,1664]{1,0:T(8,128)S(1)}, f32[80,1664]{1,0:T(8,128)}, u32[]{:S(2)}) copy-start(f32[80,1664]{1,0:T(8,128)} %refs_10_.11) | copy-start | bytes 1597444
  0.7 10.7 %copy-start.5 = (f32[80,1664]{1,0:T(8,128)S(1)}, f32[80,1664]{1,0:T(8,128)}, u32[]{:S(2)}) copy-start(f32[80,1664]{1,0:T(8,128)} %refs_11_.1) | copy-start | bytes 1597444
  2.4 11.6 %collective-permute-start.1 = (bf16[1424,128]{1,0:T(8,128)(2,1)S(1)}, bf16[1424,128]{1,0:T(8,128)(2,1)S(1)}, u32[]{:S(2)}, u32[]{:S(2)}) collective-permute-start(bf16[1424,128]{1,0:T(8,128)(2,1)S(1)} %get-tuple-element.58), channel_id=1, source_target_pairs={{0,1},{1,0},{2,3},{3,2},{4,5},{5,4},{6,7},{7,6},{8,9},{9,8},{10,11... | collective-permute-start | bytes 1093640 | tf_op jit(solution)/shard_map/ppermute | solution.py:461
  2.5 14.0 %collective-permute-start.2 = (bf16[1424,128]{1,0:T(8,128)(2,1)S(1)}, bf16[1424,128]{1,0:T(8,128)(2,1)S(1)}, u32[]{:S(2)}, u32[]{:S(2)}) collective-permute-start(bf16[1424,128]{1,0:T(8,128)(2,1)S(1)} %get-tuple-element.57), channel_id=1, source_target_pairs={{0,1},{1,2},{2,3},{3,4},{4,5},{5,6},{6,7},{7,8},{8,9},{9,10},{10,1... | collective-permute-start | bytes 1093640 | tf_op jit(solution)/shard_map/ppermute | solution.py:505
  2.9 14.8 %collective-permute-start = (bf16[1424,128]{1,0:T(8,128)(2,1)S(1)}, bf16[1424,128]{1,0:T(8,128)(2,1)S(1)}, u32[]{:S(2)}, u32[]{:S(2)}) collective-permute-start(bf16[1424,128]{1,0:T(8,128)(2,1)S(1)} %get-tuple-element.57), channel_id=1, source_target_pairs={{1,0},{2,1},{3,2},{4,3},{5,4},{6,5},{7,6},{8,7},{9,8},{10,9},{11,1... | collective-permute-start | bytes 1093640 | tf_op jit(solution)/shard_map/ppermute | solution.py:505
  17.7 4.8 %collective-permute-start.5 = (bf16[640,128]{1,0:T(8,128)(2,1)S(1)}, bf16[640,128]{1,0:T(8,128)(2,1)S(1)}, u32[]{:S(2)}, u32[]{:S(2)}) collective-permute-start(bf16[640,128]{1,0:T(8,128)(2,1)S(1)} %get-tuple-element.80), channel_id=1, source_target_pairs={{0,255},{1,2},{2,1},{3,0},{4,3},{5,4},{6,5},{7,6},{8,7},{9,10},{10... | collective-permute-start | bytes 491528 | tf_op jit(solution)/shard_map/ppermute | solution.py:458
  17.8 5.8 %collective-permute-start.4 = (bf16[640,128]{1,0:T(8,128)(2,1)S(1)}, bf16[640,128]{1,0:T(8,128)(2,1)S(1)}, u32[]{:S(2)}, u32[]{:S(2)}) collective-permute-start(bf16[640,128]{1,0:T(8,128)(2,1)S(1)} %get-tuple-element.75), channel_id=1, source_target_pairs={{0,1},{1,0},{2,3},{3,2},{4,5},{5,4},{6,7},{7,6},{8,9},{9,8},{10,11... | collective-permute-start | bytes 491528 | tf_op jit(solution)/shard_map/ppermute | solution.py:461
  17.9 10.3 %collective-permute-start.3 = (bf16[640,128]{1,0:T(8,128)(2,1)S(1)}, bf16[640,128]{1,0:T(8,128)(2,1)S(1)}, u32[]{:S(2)}, u32[]{:S(2)}) collective-permute-start(bf16[640,128]{1,0:T(8,128)(2,1)S(1)} %get-tuple-element.74), channel_id=1, source_target_pairs={{0,1},{1,2},{2,3},{3,4},{4,5},{5,6},{6,7},{7,8},{8,9},{9,10},{10,1... | collective-permute-start | bytes 491528 | tf_op jit(solution)/shard_map/ppermute | solution.py:455
  23.7 10.4 %collective-permute-start.7 = (bf16[640,128]{1,0:T(8,128)(2,1)S(1)}, bf16[640,128]{1,0:T(8,128)(2,1)S(1)}, u32[]{:S(2)}, u32[]{:S(2)}) collective-permute-start(bf16[640,128]{1,0:T(8,128)(2,1)S(1)} %get-tuple-element.98), channel_id=1, source_target_pairs={{0,1},{1,2},{2,3},{3,4},{4,5},{5,6},{6,7},{7,8},{8,9},{9,10},{10,1... | collective-permute-start | bytes 491528 | tf_op jit(solution)/shard_map/ppermute | solution.py:455
  29.4 7.1 %collective-permute-start.8 = (bf16[640,128]{1,0:T(8,128)(2,1)S(1)}, bf16[640,128]{1,0:T(8,128)(2,1)S(1)}, u32[]{:S(2)}, u32[]{:S(2)}) collective-permute-start(bf16[640,128]{1,0:T(8,128)(2,1)S(1)} %get-tuple-element.99), channel_id=1, source_target_pairs={{0,255},{1,2},{2,1},{3,0},{4,3},{5,4},{6,5},{7,6},{8,7},{9,10},{10... | collective-permute-start | bytes 491528 | tf_op jit(solution)/shard_map/ppermute | solution.py:458
  31.1 5.4 %collective-permute-start.6 = (bf16[640,128]{1,0:T(8,128)(2,1)S(1)}, bf16[640,128]{1,0:T(8,128)(2,1)S(1)}, u32[]{:S(2)}, u32[]{:S(2)}) collective-permute-start(bf16[640,128]{1,0:T(8,128)(2,1)S(1)} %get-tuple-element.97), channel_id=1, source_target_pairs={{0,1},{1,0},{2,3},{3,2},{4,5},{5,4},{6,7},{7,6},{8,9},{9,8},{10,11... | collective-permute-start | bytes 491528 | tf_op jit(solution)/shard_map/ppermute | solution.py:461

commit v4 on v3

--- a/solution.py
+++ b/solution.py
@@ -1,3 +1,5 @@
+import functools
+
 import jax
 import jax.numpy as jnp
 from jax import lax
@@ -13,6 +15,7 @@
 F32 = jnp.float32
 BF16 = jnp.bfloat16
 LEV = 80
+EVEN = (0, 2, 4, 6)
 TILE = 128
 SMALL = pl.CostEstimate(flops=1000, bytes_accessed=1000, transcendentals=0)
 LARGE = pl.CostEstimate(flops=10**9, bytes_accessed=10**6, transcendentals=0)
@@ -170,33 +173,46 @@
     )
 
 
-def on(odd, work):
-    pl.when(lax.rem(lax.axis_index("dom"), 2) == (1 if odd else 0))(work)
-
-
-def odd_inside(
+def on(places, work):
+    place = lax.rem(lax.axis_index("dom"), 8)
+    here = place == places[0]
+    for other in places[1:]:
+        here = here | (place == other)
+    pl.when(here)(work)
+
+
+def inside(
+    places, edge_blocks, cell_blocks,
     own, keep_share, coded, velocity, velocity0, levels, gradient, average, edge_sources,
-    thickness, tracer, thickness0, tracer0, divergence, cell_sources,
-    fluxes, new_velocity, new_thickness, new_tracer,
-):
+    thickness, tracer, thickness0, tracer0, divergence, cell_sources, *refs,
+):
+    fluxes, new_velocity, new_thickness, new_tracer = refs[-4:]
+
     def work():
         inside_edges(
-            own, keep_share, coded, velocity, velocity0, levels, gradient, average, edge_sources, fluxes, new_velocity
+            own, keep_share, coded, velocity, velocity0, levels, gradient, average, edge_sources, fluxes, new_velocity,
+            edge_blocks,
         )
         inside_cells(
             own, keep_share, fluxes, thickness, tracer, thickness0, tracer0, levels, divergence, cell_sources,
-            None, new_thickness, new_tracer,
+            None, new_thickness, new_tracer, cell_blocks,
         )
 
-    on(True, work)
-
-
-def even_edges(own, keep_share, *refs):
-    on(False, lambda: inside_edges(own, keep_share, *refs[:7], *refs[9:]))
-
-
-def even_cells(own, keep_share, *refs):
-    on(False, lambda: inside_cells(own, keep_share, *refs[:8], None, *refs[10:]))
+    on(places, work)
+
+
+def whole_inside(
+    own, keep_share, coded, velocity, velocity0, levels, gradient, average, edge_sources,
+    thickness, tracer, thickness0, tracer0, divergence, cell_sources,
+    fluxes, new_coded, new_thickness, new_tracer, new_velocity,
+):
+    inside_edges(
+        own, keep_share, coded, velocity, velocity0, levels, gradient, average, edge_sources, fluxes, new_velocity
+    )
+    inside_cells(
+        own, keep_share, fluxes, thickness, tracer, thickness0, tracer0, levels, divergence, cell_sources,
+        new_coded, new_thickness, new_tracer,
+    )
 
 
 def tick(own, keep_share, *refs):
@@ -205,13 +221,11 @@
 
 def inside_edges(
     own, keep_share, coded, velocity, velocity0, levels, gradient, average, edge_sources, fluxes, new_velocity,
-    wait=None,
+    blocks=None,
 ):
     whole = own * lax.axis_size("dom")
     first_block = lax.axis_index("dom") * own
-    for block in range(1, own - 1):
-        if wait is not None:
-            wait(block)
+    for block in blocks or range(1, own - 1):
         mask = block_mask(levels, block)
         for edge in range(3 * block, 3 * block + 3):
             other = other_block(edge_sources, edge, first_block, own, whole)
@@ -225,14 +239,12 @@
 
 def inside_cells(
     own, keep_share, fluxes, thickness, tracer, thickness0, tracer0, levels, divergence, cell_sources,
-    new_coded, new_thickness, new_tracer, wait=None,
+    new_coded, new_thickness, new_tracer, blocks=None,
 ):
     whole = own * lax.axis_size("dom")
     first_block = lax.axis_index("dom") * own
     done = []
-    for block in range(2, own - 2):
-        if wait is not None:
-            wait(block)
+    for block in blocks or range(2, own - 2):
         done.append(
             finish_cell(
                 block, own, keep_share, first_block, whole,
@@ -494,14 +506,6 @@
             name=name,
         )(*operands, *extra, *filled)
 
-    def edges_inside(keep_share, common, passed=None):
-        operands = (common[0], common[3], common[6], *common[7:11])
-        shapes = (flux_shape, field_shapes[2])
-        return call(inside_edges, keep_share, operands, shapes, [vmem] * 2, [], "inside_edges", passed=passed)
-
-    def cell_operands(fluxes, common):
-        return (fluxes, common[1], common[2], common[4], common[5], common[7], common[11], common[12])
-
     up_in, down_in = lax.ppermute(outer, "dom", upward), lax.ppermute(outer, "dom", [(j, i) for i, j in upward])
     anchor = (in_vmem(thickness), in_vmem(tracer), in_vmem(velocity))
     gradient, average, divergence = in_vmem(gradient), in_vmem(average), in_vmem(divergence)
@@ -524,34 +528,48 @@
     next_up = send_up(outer)
     up_in, down_in, inner_in = next_up, next_down, swap_inner(inner)
 
+    def inside_operands(coded, thickness, tracer, velocity):
+        return (
+            coded, velocity, anchor[2], levels, gradient, average, edge_sources,
+            thickness, tracer, anchor[0], anchor[1], divergence, cell_sources,
+        )
+
     common = operands(built[1], built[2:5])
-    fluxes, new_velocity = edges_inside(keep_shares[1], common)
-    new_cells = call(
-        inside_cells, keep_shares[1], cell_operands(fluxes, common), (coded_shape,) + field_shapes[:2],
-        [vmem] * 3, [], "inside_cells", after=down_in,
-    )
-    built = (fluxes, *new_cells, new_velocity)
+    built = call(
+        whole_inside, keep_shares[1], inside_operands(*common[:4]), built_shapes, [vmem] * 5, [], "inside"
+    )
+    fluxes = call(tick, 0.0, (down_in,), (), [], [], "tick", passed=built[0])[0]
+    built = (fluxes, *built[1:])
     built, inner, outer = rim(True, keep_shares[1], inner_in, down_in, tiles_down, common, built, None)
     next_up = send_up(outer)
+    middle, near_middle = range(3, own - 3), range(4, own - 4)
+    inner, fluxes, new_velocity, h, s = call(
+        functools.partial(inside, EVEN, middle, near_middle), keep_shares[2], inside_operands(*built[1:]),
+        (flux_shape, field_shapes[2]) + field_shapes[:2], [vmem] * 4, [], "even_middle", passed=inner,
+    )
     built, inner, outer = rim(False, keep_shares[1], inner_in, up_in, tiles_up, common, built, inner)
+
+    common = operands(built[1], built[2:5])
+    outer, fluxes, new_velocity, h, s = call(
+        functools.partial(inside, (3,), None, None), keep_shares[2], inside_operands(*common[:4]),
+        (), [], [], "odd_inside", passed=outer, filled=(fluxes, new_velocity, h, s),
+    )
     up_in, down_in = next_up, send_down(outer)
 
-    common = operands(built[1], built[2:5])
     far_shapes = (pltpu.HBM((LEV, cells), F32), pltpu.HBM((LEV, cells), F32), pltpu.HBM((LEV, edges), F32))
-    edge_operands = (common[0], common[3], common[6], *common[7:11])
     inner, fluxes, new_velocity, h, s = call(
-        odd_inside, keep_shares[2],
-        edge_operands + (common[1], common[2], common[4], common[5], common[11], common[12]),
-        (flux_shape, field_shapes[2]) + field_shapes[:2], [vmem] * 4, [], "odd_inside", passed=inner,
+        functools.partial(inside, (1, 5, 7), None, None), keep_shares[2], inside_operands(*common[:4]),
+        (), [], [], "odd_inside", passed=inner, filled=(fluxes, new_velocity, h, s),
     )
     inner_in = swap_inner(inner)
     fluxes = call(tick, 0.0, (up_in,), (), [], [], "tick", passed=fluxes)[0]
-    fluxes, new_velocity = call(
-        even_edges, keep_shares[2], edge_operands, (), [], [], "even_edges", filled=(fluxes, new_velocity)
-    )
-    h, s = call(
-        even_cells, keep_shares[2], cell_operands(fluxes, common), (), [], [], "even_cells", filled=(h, s)
-    )
+    edge_rest = [b for b in range(1, own - 1) if b not in middle]
+    cell_rest = [b for b in range(2, own - 2) if b not in near_middle]
+    fluxes, new_velocity, h, s = call(
+        functools.partial(inside, EVEN, edge_rest, cell_rest), keep_shares[2], inside_operands(*common[:4]),
+        (), [], [], "even_rest", filled=(fluxes, new_velocity, h, s),
+    )
+    h = call(tick, 0.0, (down_in,), (), [], [], "tick", passed=h)[0]
     results = pl.pallas_call(
         lambda *refs: last_rim_kernel(own, keep_shares[2], *refs),
         out_shape=(flux_shape,) + field_shapes + far_shapes,

time: 38.7 us -> 37 us (0.956)
  the two profiles are of different devices: /device:TPU:0 before, /device:TPU:1 now
where the time goes in v4:
time: 37 us; the launch traced here: 36.9 us
  starting transfers between devices  19.8 us (54%)
  Pallas kernels  13.5 us (36%)
  waiting for transfers between devices  2.54 us (7%)
  between operations  1 us (3%)
    ppermute x3, starting transfers between devices, swap_inner(): return lax.ppermute(x, 'dom', within)  9.5 us
    pallas_call x9, Pallas kernels, call(): pl.pallas_call(lambda *refs: body(own, keep_share, *refs[:n], *refs[n + l...  7.65 us
    ppermute x2, starting transfers between devices, send_down(): return lax.ppermute(x, 'dom', downward)  6.67 us
    ppermute x2, starting transfers between devices, send_up(): return lax.ppermute(x, 'dom', upward)  3.15 us
    pallas_call x4, Pallas kernels, rim(): pl.pallas_call(lambda *refs: rim_kernel(odd, second, own, keep_share, *re...  2.5 us
    pallas_call x1, Pallas kernels, local(): pl.pallas_call(lambda *refs: last_rim_kernel(own, keep_shares[2], *refs),...  1.7 us
    pallas_call x1, Pallas kernels, local(): pl.pallas_call(lambda *refs: start_kernel(own, *refs), out_shape=(message...  1.65 us
    ppermute x1, waiting for transfers between devices, local(): lax.ppermute(outer, 'dom', upward)  1.19 us
  transfers between devices with their start and end apart: 9, of which 3 were waited for; matrix products, arithmetic and copies ran while one was open for 0% of the time, Pallas kernels for 27%

profile of v4, /device:TPU:1, one launch (start us, length us, event | category | flops | bytes accessed | tf_op | source)
XLA Modules:
  0.0 36.9 jit_solution(7343637842858950707)
XLA Ops:
  0.7 1.6 %start.1 = (bf16[1424,128]{1,0:T(8,128)(2,1)S(1)}, bf16[1424,128]{1,0:T(8,128)(2,1)S(1)}, s32[13,128]{1,0:T(8,128)S(1)}, s32[2,39]{1,0:T(2,128)S(1)}, s32[6,13]{1,0:T(8,128)S(1)}) custom-call(f32[80,1664]{1,0:T(8,128)} %refs_10_.19, f32[80,1664]{1,0:T(8,128)} %refs_11_.1, f32[80,4992]{1,0:T(8,128)} %refs_12_.1, s32[1664]{0:T(1024)} %refs_3_.1, ...), custom_call_target="tpu_custom_call" | custom-call | flops 20000000000 | bytes 1000000 | tf_op jit(solution)/shard_map/start/pallas_call | solution.py:433
  2.4 3.3 %collective-permute-start.1 = (bf16[1424,128]{1,0:T(8,128)(2,1)S(1)}, bf16[1424,128]{1,0:T(8,128)(2,1)S(1)}, u32[]{:S(2)}, u32[]{:S(2)}) collective-permute-start(bf16[1424,128]{1,0:T(8,128)(2,1)S(1)} %get-tuple-element.68), channel_id=1, source_target_pairs={{0,1},{1,0},{2,3},{3,2},{4,5},{5,4},{6,7},{7,6},{8,9},{9,8},{10,11... | collective-permute-start | bytes 1093640 | tf_op jit(solution)/shard_map/ppermute | solution.py:473
  5.7 0.0 collective-permute-start.2
  5.7 0.5 %collective-permute-start = (bf16[1424,128]{1,0:T(8,128)(2,1)S(1)}, bf16[1424,128]{1,0:T(8,128)(2,1)S(1)}, u32[]{:S(2)}, u32[]{:S(2)}) collective-permute-start(bf16[1424,128]{1,0:T(8,128)(2,1)S(1)} %get-tuple-element.67), channel_id=1, source_target_pairs={{1,0},{2,1},{3,2},{4,3},{5,4},{6,5},{7,6},{8,7},{9,8},{10,9},{11,1... | collective-permute-start | bytes 1093640 | tf_op jit(solution)/shard_map/ppermute | solution.py:509
  6.2 2.7 %inside.2 = (bf16[45,160,128]{2,1,0:T(8,128)(2,1)S(1)}, bf16[13,240,128]{2,1,0:T(8,128)(2,1)S(1)}, f32[80,1664]{1,0:T(8,128)S(1)}, f32[80,1664]{1,0:T(8,128)S(1)...) custom-call(f32[80,1664]{1,0:T(8,128)S(1)} %copy-done.4, f32[80,1664]{1,0:T(8,128)S(1)} %copy-done.5, ...), custom_call_target="tpu_custom_call" | custom-call | flops 1000 | bytes 1000 | tf_op jit(solution)/shard_map/inside/pallas_call | solution.py:497
  8.9 0.0 collective-permute-done.1.refs_1_.refs_3_
  8.9 1.2 %collective-permute-done.2.refs_0_.refs_2_.refs_4_ = bf16[1424,128]{1,0:T(8,128)(2,1)S(1)} collective-permute-done((bf16[1424,128]{1,0:T(8,128)(2,1)S(1)}, bf16[1424,128]{1,0:T(8,128)(2,1)S(1)}, u32[]{:S(2)}, u32[]{:S(2)}) %collective-permute-start.2) | collective-permute-done | bytes 364576 | tf_op jit(solution)/shard_map/ppermute | solution.py:509
  10.1 3.8 %collective-permute-start.5 = (bf16[640,128]{1,0:T(8,128)(2,1)S(1)}, bf16[640,128]{1,0:T(8,128)(2,1)S(1)}, u32[]{:S(2)}, u32[]{:S(2)}) collective-permute-start(bf16[640,128]{1,0:T(8,128)(2,1)S(1)} %get-tuple-element.90), channel_id=1, source_target_pairs={{0,255},{1,2},{2,1},{3,0},{4,3},{5,4},{6,5},{7,6},{8,7},{9,10},{10... | collective-permute-start | bytes 491528 | tf_op jit(solution)/shard_map/ppermute | solution.py:470
  13.9 0.0 collective-permute-done.refs_0_.refs_2_.refs_5_
  13.9 1.2 %rim_odd.2 = (bf16[45,160,128]{2,1,0:T(8,128)(2,1)S(1)}, bf16[13,240,128]{2,1,0:T(8,128)(2,1)S(1)}, f32[80,1664]{1,0:T(8,128)S(1)}, f32[80,1664]{1,0:T(8,128)S(1...) custom-call(bf16[1424,128]{1,0:T(8,128)(2,1)S(1)} %collective-permut, ...), custom_call_target="tpu_custom_call", output_to_operand_aliasing={{0}: (17, {}), {1}: (18, {}), {2}: (19, {}), {3}: (20, {}),... | custom-call | flops 1000000000 | bytes 1000000 | tf_op jit(solution)/shard_map/rim_odd/pallas_call | solution.py:478
  15.1 6.1 %collective-permute-start.4 = (bf16[640,128]{1,0:T(8,128)(2,1)S(1)}, bf16[640,128]{1,0:T(8,128)(2,1)S(1)}, u32[]{:S(2)}, u32[]{:S(2)}) collective-permute-start(bf16[640,128]{1,0:T(8,128)(2,1)S(1)} %get-tuple-element.85), channel_id=1, source_target_pairs={{0,1},{1,0},{2,3},{3,2},{4,5},{5,4},{6,7},{7,6},{8,9},{9,8},{10,11... | collective-permute-start | bytes 491528 | tf_op jit(solution)/shard_map/ppermute | solution.py:473
  21.2 2.9 %collective-permute-start.3 = (bf16[640,128]{1,0:T(8,128)(2,1)S(1)}, bf16[640,128]{1,0:T(8,128)(2,1)S(1)}, u32[]{:S(2)}, u32[]{:S(2)}) collective-permute-start(bf16[640,128]{1,0:T(8,128)(2,1)S(1)} %get-tuple-element.84), channel_id=1, source_target_pairs={{0,1},{1,2},{2,3},{3,4},{4,5},{5,6},{6,7},{7,8},{8,9},{9,10},{10,1... | collective-permute-start | bytes 491528 | tf_op jit(solution)/shard_map/ppermute | solution.py:467
  24.0 2.6 %inside.3 = (bf16[45,160,128]{2,1,0:T(8,128)(2,1)S(1)}, bf16[13,240,128]{2,1,0:T(8,128)(2,1)S(1)}, f32[80,1664]{1,0:T(8,128)S(1)}, f32[80,1664]{1,0:T(8,128)S(1)}, f32[80,4992]{1,0:T(8,128)S(1)}) custom-call(bf16[13,240,128]{2,1,0:T(8,128)(2,1)S(1)} %get-tuple-element.86.refs_0_.refs_4_, f32[80,4992]{1,0:T(8,128)S(1)} %get-tuple-element.89.refs_1_.refs_7_, ...), custom_call_target="tpu_custom_call" | custom-call | flops 1000 | bytes 1000 | tf_op jit(solution)/shard_map/inside/pallas_call | solution.py:497
  26.6 0.0 collective-permute-done.5.refs_0_
  26.6 0.0 collective-permute-done.4.refs_1_
  26.6 1.2 %rim_odd.3 = (bf16[45,160,128]{2,1,0:T(8,128)(2,1)S(1)}, bf16[13,240,128]{2,1,0:T(8,128)(2,1)S(1)}, f32[80,1664]{1,0:T(8,128)S(1)}, f32[80,1664]{1,0:T(8,128)S(1...) custom-call(bf16[640,128]{1,0:T(8,128)(2,1)S(1)} %collective-permute, ...), custom_call_target="tpu_custom_call", output_to_operand_aliasing={{0}: (17, {}), {1}: (18, {}), {2}: (19, {}), {3}: (20, {}),... | custom-call | flops 1000000000 | bytes 1000000 | tf_op jit(solution)/shard_map/rim_odd/pallas_call | solution.py:478
  27.9 0.3 collective-permute-start.7
  28.2 0.0 collective-permute-done.3.refs_0_
  28.3 2.9 %collective-permute-start.8 = (bf16[640,128]{1,0:T(8,128)(2,1)S(1)}, bf16[640,128]{1,0:T(8,128)(2,1)S(1)}, u32[]{:S(2)}, u32[]{:S(2)}) collective-permute-start(bf16[640,128]{1,0:T(8,128)(2,1)S(1)} %get-tuple-element.119), channel_id=1, source_target_pairs={{0,255},{1,2},{2,1},{3,0},{4,3},{5,4},{6,5},{7,6},{8,7},{9,10},{10... | collective-permute-start | bytes 491528 | tf_op jit(solution)/shard_map/ppermute | solution.py:470
  31.2 2.3 %odd_inside.3 = (bf16[640,128]{1,0:T(8,128)(2,1)S(1)}, bf16[45,160,128]{2,1,0:T(8,128)(2,1)S(1)}, f32[80,4992]{1,0:T(8,128)S(1)}, f32[80,1664]{1,0:T(8,128)S(1)}, f32[80,1664]{1,0:T(8,128)S(1)}) custom-call(bf16[13,240,128]{2,1,0:T(8,128)(2,1)S(1)} %get-tuple-element.103.refs_0_.refs_6, ...), custom_call_target="tpu_custom_call", output_to_operand_aliasing={{0}: (13, {}), {1}: (14, {}), {2}: (15, {}), {3}: (16, {}),... | custom-call | flops 1000 | bytes 1000 | tf_op jit(solution)/shard_map/odd_inside/pallas_call | solution.py:497
  33.5 0.1 collective-permute-start.6
  33.7 0.8 %collective-permute-done.8.refs_0_.refs_2_ = bf16[640,128]{1,0:T(8,128)(2,1)S(1)} collective-permute-done((bf16[640,128]{1,0:T(8,128)(2,1)S(1)}, bf16[640,128]{1,0:T(8,128)(2,1)S(1)}, u32[]{:S(2)}, u32[]{:S(2)}) %collective-permute-start.8) | collective-permute-done | bytes 163872 | tf_op jit(solution)/shard_map/ppermute | solution.py:470
  34.5 0.5 %collective-permute-done.6.refs_0_ = bf16[640,128]{1,0:T(8,128)(2,1)S(1)} collective-permute-done((bf16[640,128]{1,0:T(8,128)(2,1)S(1)}, bf16[640,128]{1,0:T(8,128)(2,1)S(1)}, u32[]{:S(2)}, u32[]{:S(2)}) %collective-permute-start.6) | collective-permute-done | bytes 163872 | tf_op jit(solution)/shard_map/ppermute | solution.py:473
  35.0 1.7 %rim.1 = (bf16[45,160,128]{2,1,0:T(8,128)(2,1)S(1)}, f32[80,1664]{1,0:T(8,128)S(1)}, f32[80,1664]{1,0:T(8,128)S(1)}, f32[80,4992]{1,0:T(8,128)S(1)}, f32[80,1664...) custom-call(bf16[640,128]{1,0:T(8,128)(2,1)S(1)} %collective-permute, ...), custom_call_target="tpu_custom_call", output_to_operand_aliasing={{0}: (19, {}), {1}: (20, {}), {2}: (21, {}), {3}: (22, {})} | custom-call | flops 1000 | bytes 1000 | tf_op jit(solution)/shard_map/rim/pallas_call | solution.py:573
  (21 shorter events, 0.1 us)
Async XLA Ops:
  0.6 5.6 %copy-start = (bf16[39,2,128,128]{3,2,1,0:T(8,128)(2,1)S(1)}, bf16[39,2,128,128]{3,2,1,0:T(8,128)(2,1)}, u32[]{:S(2)}) copy-start(bf16[39,2,128,128]{3,2,1,0:T(8,128)(2,1)} %param.14) | copy-start | bytes 7667716
  0.6 5.5 %copy-start.1 = (bf16[39,2,128,128]{3,2,1,0:T(8,128)(2,1)S(1)}, bf16[39,2,128,128]{3,2,1,0:T(8,128)(2,1)}, u32[]{:S(2)}) copy-start(bf16[39,2,128,128]{3,2,1,0:T(8,128)(2,1)} %param.13) | copy-start | bytes 7667716
  0.7 5.5 %copy-start.2 = (bf16[13,6,128,128]{3,2,1,0:T(8,128)(2,1)S(1)}, bf16[13,6,128,128]{3,2,1,0:T(8,128)(2,1)}, u32[]{:S(2)}) copy-start(bf16[13,6,128,128]{3,2,1,0:T(8,128)(2,1)} %param.16) | copy-start | bytes 7667716
  0.7 5.5 %copy-start.3 = (f32[80,4992]{1,0:T(8,128)S(1)}, f32[80,4992]{1,0:T(8,128)}, u32[]{:S(2)}) copy-start(f32[80,4992]{1,0:T(8,128)} %refs_12_.1) | copy-start | bytes 4792324
  0.7 5.5 %copy-start.4 = (f32[80,1664]{1,0:T(8,128)S(1)}, f32[80,1664]{1,0:T(8,128)}, u32[]{:S(2)}) copy-start(f32[80,1664]{1,0:T(8,128)} %refs_10_.19) | copy-start | bytes 1597444
  0.7 5.5 %copy-start.5 = (f32[80,1664]{1,0:T(8,128)S(1)}, f32[80,1664]{1,0:T(8,128)}, u32[]{:S(2)}) copy-start(f32[80,1664]{1,0:T(8,128)} %refs_11_.1) | copy-start | bytes 1597444
  2.4 6.5 %collective-permute-start.1 = (bf16[1424,128]{1,0:T(8,128)(2,1)S(1)}, bf16[1424,128]{1,0:T(8,128)(2,1)S(1)}, u32[]{:S(2)}, u32[]{:S(2)}) collective-permute-start(bf16[1424,128]{1,0:T(8,128)(2,1)S(1)} %get-tuple-element.68), channel_id=1, source_target_pairs={{0,1},{1,0},{2,3},{3,2},{4,5},{5,4},{6,7},{7,6},{8,9},{9,8},{10,11... | collective-permute-start | bytes 1093640 | tf_op jit(solution)/shard_map/ppermute | solution.py:473
  5.7 4.4 %collective-permute-start.2 = (bf16[1424,128]{1,0:T(8,128)(2,1)S(1)}, bf16[1424,128]{1,0:T(8,128)(2,1)S(1)}, u32[]{:S(2)}, u32[]{:S(2)}) collective-permute-start(bf16[1424,128]{1,0:T(8,128)(2,1)S(1)} %get-tuple-element.67), channel_id=1, source_target_pairs={{0,1},{1,2},{2,3},{3,4},{4,5},{5,6},{6,7},{7,8},{8,9},{9,10},{10,1... | collective-permute-start | bytes 1093640 | tf_op jit(solution)/shard_map/ppermute | solution.py:509
  5.7 8.2 %collective-permute-start = (bf16[1424,128]{1,0:T(8,128)(2,1)S(1)}, bf16[1424,128]{1,0:T(8,128)(2,1)S(1)}, u32[]{:S(2)}, u32[]{:S(2)}) collective-permute-start(bf16[1424,128]{1,0:T(8,128)(2,1)S(1)} %get-tuple-element.67), channel_id=1, source_target_pairs={{1,0},{2,1},{3,2},{4,3},{5,4},{6,5},{7,6},{8,7},{9,8},{10,9},{11,1... | collective-permute-start | bytes 1093640 | tf_op jit(solution)/shard_map/ppermute | solution.py:509
  10.1 16.5 %collective-permute-start.5 = (bf16[640,128]{1,0:T(8,128)(2,1)S(1)}, bf16[640,128]{1,0:T(8,128)(2,1)S(1)}, u32[]{:S(2)}, u32[]{:S(2)}) collective-permute-start(bf16[640,128]{1,0:T(8,128)(2,1)S(1)} %get-tuple-element.90), channel_id=1, source_target_pairs={{0,255},{1,2},{2,1},{3,0},{4,3},{5,4},{6,5},{7,6},{8,7},{9,10},{10... | collective-permute-start | bytes 491528 | tf_op jit(solution)/shard_map/ppermute | solution.py:470
  15.1 11.6 %collective-permute-start.4 = (bf16[640,128]{1,0:T(8,128)(2,1)S(1)}, bf16[640,128]{1,0:T(8,128)(2,1)S(1)}, u32[]{:S(2)}, u32[]{:S(2)}) collective-permute-start(bf16[640,128]{1,0:T(8,128)(2,1)S(1)} %get-tuple-element.85), channel_id=1, source_target_pairs={{0,1},{1,0},{2,3},{3,2},{4,5},{5,4},{6,7},{7,6},{8,9},{9,8},{10,11... | collective-permute-start | bytes 491528 | tf_op jit(solution)/shard_map/ppermute | solution.py:473
  21.2 7.0 %collective-permute-start.3 = (bf16[640,128]{1,0:T(8,128)(2,1)S(1)}, bf16[640,128]{1,0:T(8,128)(2,1)S(1)}, u32[]{:S(2)}, u32[]{:S(2)}) collective-permute-start(bf16[640,128]{1,0:T(8,128)(2,1)S(1)} %get-tuple-element.84), channel_id=1, source_target_pairs={{0,1},{1,2},{2,3},{3,4},{4,5},{5,6},{6,7},{7,8},{8,9},{9,10},{10,1... | collective-permute-start | bytes 491528 | tf_op jit(solution)/shard_map/ppermute | solution.py:467
  27.9 5.8 %collective-permute-start.7 = (bf16[640,128]{1,0:T(8,128)(2,1)S(1)}, bf16[640,128]{1,0:T(8,128)(2,1)S(1)}, u32[]{:S(2)}, u32[]{:S(2)}) collective-permute-start(bf16[640,128]{1,0:T(8,128)(2,1)S(1)} %get-tuple-element.118), channel_id=1, source_target_pairs={{0,1},{1,2},{2,3},{3,4},{4,5},{5,6},{6,7},{7,8},{8,9},{9,10},{10,1... | collective-permute-start | bytes 491528 | tf_op jit(solution)/shard_map/ppermute | solution.py:467
  28.3 6.2 %collective-permute-start.8 = (bf16[640,128]{1,0:T(8,128)(2,1)S(1)}, bf16[640,128]{1,0:T(8,128)(2,1)S(1)}, u32[]{:S(2)}, u32[]{:S(2)}) collective-permute-start(bf16[640,128]{1,0:T(8,128)(2,1)S(1)} %get-tuple-element.119), channel_id=1, source_target_pairs={{0,255},{1,2},{2,1},{3,0},{4,3},{5,4},{6,5},{7,6},{8,7},{9,10},{10... | collective-permute-start | bytes 491528 | tf_op jit(solution)/shard_map/ppermute | solution.py:470
  33.5 1.5 %collective-permute-start.6 = (bf16[640,128]{1,0:T(8,128)(2,1)S(1)}, bf16[640,128]{1,0:T(8,128)(2,1)S(1)}, u32[]{:S(2)}, u32[]{:S(2)}) collective-permute-start(bf16[640,128]{1,0:T(8,128)(2,1)S(1)} %get-tuple-element.117), channel_id=1, source_target_pairs={{0,1},{1,0},{2,3},{3,2},{4,5},{5,4},{6,7},{7,6},{8,9},{9,8},{10,11... | collective-permute-start | bytes 491528 | tf_op jit(solution)/shard_map/ppermute | solution.py:473

commit v5 on v4

--- a/solution.py
+++ b/solution.py
@@ -18,6 +18,7 @@
 EVEN = (0, 2, 4, 6)
 TILE = 128
 SMALL = pl.CostEstimate(flops=1000, bytes_accessed=1000, transcendentals=0)
+FIRST = pl.CostEstimate(flops=10**10, bytes_accessed=10**7, transcendentals=0)
 LARGE = pl.CostEstimate(flops=10**9, bytes_accessed=10**6, transcendentals=0)
 NEAR = 3 * LEV
 NEXT = NEAR + 2 * LEV
@@ -502,7 +503,7 @@
             input_output_aliases={total - len(given) + i: i for i in range(len(given))},
             scratch_shapes=scratch,
             compiler_params=params,
-            cost_estimate=SMALL,
+            cost_estimate=FIRST if name == "first_inside" else SMALL,
             name=name,
         )(*operands, *extra, *filled)
 
@@ -512,7 +513,7 @@
     loaded = call(
         first_inside, keep_shares[0],
         (*anchor, levels, gradient, average, edge_sources, divergence, cell_sources),
-        built_shapes + (coded_shape,), [vmem] * 6, [], "inside",
+        built_shapes + (coded_shape,), [vmem] * 6, [], "first_inside",
     )
     built, coded = loaded[:5], loaded[5]
     inner_in = swap_inner(inner)

time: 37 us -> 36.3 us (0.981)
  waiting for transfers between devices: 2.54 us -> 1.35 us
  starting transfers between devices: 19.8 us -> 20.2 us
    ppermute x2, starting transfers between devices: 6.67 us -> 2.98 us  [send_down(): return lax.ppermute(x, 'dom', downward)]
    ppermute x1, starting transfers between devices: 0.01 us -> 2.68 us  [local(): lax.ppermute(outer, 'dom', upward)]
    ppermute x3, starting transfers between devices: 9.5 us -> 10.7 us  [swap_inner(): return lax.ppermute(x, 'dom', within)]
    ppermute x1, waiting for transfers between devices: 1.19 us -> 0.01 us  [local(): lax.ppermute(outer, 'dom', upward)]
  transfers between devices with their start and end apart: 9 -> 9, of which waited for: 3 -> 2; matrix products, arithmetic and copies ran while one was open for 0% -> 0% of each run, Pallas kernels for 27% -> 28%
where the time goes in v5:
time: 36.3 us; the launch traced here: 36.2 us
  starting transfers between devices  20.2 us (56%)
  Pallas kernels  13.6 us (37%)
  waiting for transfers between devices  1.35 us (4%)
  between operations  1.03 us (3%)
    ppermute x3, starting transfers between devices, swap_inner(): return lax.ppermute(x, 'dom', within)  10.7 us
    pallas_call x9, Pallas kernels, call(): pl.pallas_call(lambda *refs: body(own, keep_share, *refs[:n], *refs[n + l...  7.63 us
    ppermute x2, starting transfers between devices, send_up(): return lax.ppermute(x, 'dom', upward)  3.14 us
    ppermute x2, starting transfers between devices, send_down(): return lax.ppermute(x, 'dom', downward)  2.98 us
    ppermute x1, starting transfers between devices, local(): lax.ppermute(outer, 'dom', upward)  2.68 us
    pallas_call x4, Pallas kernels, rim(): pl.pallas_call(lambda *refs: rim_kernel(odd, second, own, keep_share, *re...  2.57 us
    pallas_call x1, Pallas kernels, local(): pl.pallas_call(lambda *refs: last_rim_kernel(own, keep_shares[2], *refs),...  1.7 us
    pallas_call x1, Pallas kernels, local(): pl.pallas_call(lambda *refs: start_kernel(own, *refs), out_shape=(message...  1.65 us
  transfers between devices with their start and end apart: 9, of which 2 were waited for; matrix products, arithmetic and copies ran while one was open for 0% of the time, Pallas kernels for 28%

profile of v5, /device:TPU:1, one launch (start us, length us, event | category | flops | bytes accessed | tf_op | source)
XLA Modules:
  0.0 36.2 jit_solution(15314950192460966)
XLA Ops:
  0.7 1.6 %start.1 = (bf16[1424,128]{1,0:T(8,128)(2,1)S(1)}, bf16[1424,128]{1,0:T(8,128)(2,1)S(1)}, s32[13,128]{1,0:T(8,128)S(1)}, s32[2,39]{1,0:T(2,128)S(1)}, s32[6,13]{1,0:T(8,128)S(1)}) custom-call(f32[80,1664]{1,0:T(8,128)} %refs_10_.19, f32[80,1664]{1,0:T(8,128)} %refs_11_.1, f32[80,4992]{1,0:T(8,128)} %refs_12_.1, s32[1664]{0:T(1024)} %refs_3_.1, ...), custom_call_target="tpu_custom_call" | custom-call | flops 20000000000 | bytes 1000000 | tf_op jit(solution)/shard_map/start/pallas_call | solution.py:434
  2.4 2.7 %collective-permute-start.2 = (bf16[1424,128]{1,0:T(8,128)(2,1)S(1)}, bf16[1424,128]{1,0:T(8,128)(2,1)S(1)}, u32[]{:S(2)}, u32[]{:S(2)}) collective-permute-start(bf16[1424,128]{1,0:T(8,128)(2,1)S(1)} %get-tuple-element.67), channel_id=1, source_target_pairs={{0,1},{1,2},{2,3},{3,4},{4,5},{5,6},{6,7},{7,8},{8,9},{9,10},{10,1... | collective-permute-start | bytes 1093640 | tf_op jit(solution)/shard_map/ppermute | solution.py:510
  5.0 0.7 %collective-permute-start = (bf16[1424,128]{1,0:T(8,128)(2,1)S(1)}, bf16[1424,128]{1,0:T(8,128)(2,1)S(1)}, u32[]{:S(2)}, u32[]{:S(2)}) collective-permute-start(bf16[1424,128]{1,0:T(8,128)(2,1)S(1)} %get-tuple-element.67), channel_id=1, source_target_pairs={{1,0},{2,1},{3,2},{4,3},{5,4},{6,5},{7,6},{8,7},{9,8},{10,9},{11,1... | collective-permute-start | bytes 1093640 | tf_op jit(solution)/shard_map/ppermute | solution.py:510
  5.8 8.2 %collective-permute-start.1 = (bf16[1424,128]{1,0:T(8,128)(2,1)S(1)}, bf16[1424,128]{1,0:T(8,128)(2,1)S(1)}, u32[]{:S(2)}, u32[]{:S(2)}) collective-permute-start(bf16[1424,128]{1,0:T(8,128)(2,1)S(1)} %get-tuple-element.68), channel_id=1, source_target_pairs={{0,1},{1,0},{2,3},{3,2},{4,5},{5,4},{6,7},{7,6},{8,9},{9,8},{10,11... | collective-permute-start | bytes 1093640 | tf_op jit(solution)/shard_map/ppermute | solution.py:474
  14.0 2.7 %first_inside.1 = (bf16[45,160,128]{2,1,0:T(8,128)(2,1)S(1)}, bf16[13,240,128]{2,1,0:T(8,128)(2,1)S(1)}, f32[80,1664]{1,0:T(8,128)S(1)}, f32[80,1664]{1,0:T(8,12...) custom-call(f32[80,1664]{1,0:T(8,128)S(1)} %copy-done.4, f32[80,1664]{1,0:T(8,128)S(1)} %copy-done.5, ...), custom_call_target="tpu_custom_call" | custom-call | flops 10000000000 | bytes 10000000 | tf_op jit(solution)/shard_map/first_inside/pallas_call | solution.py:498
  16.7 0.0 collective-permute-done.1.refs_1_.refs_3_
  16.7 0.1 collective-permute-start.5
  16.8 0.0 collective-permute-done.refs_0_.refs_2_.refs_5_
  16.8 1.2 %rim_odd.2 = (bf16[45,160,128]{2,1,0:T(8,128)(2,1)S(1)}, bf16[13,240,128]{2,1,0:T(8,128)(2,1)S(1)}, f32[80,1664]{1,0:T(8,128)S(1)}, f32[80,1664]{1,0:T(8,128)S(1...) custom-call(bf16[1424,128]{1,0:T(8,128)(2,1)S(1)} %collective-permut, ...), custom_call_target="tpu_custom_call", output_to_operand_aliasing={{0}: (17, {}), {1}: (18, {}), {2}: (19, {}), {3}: (20, {}),... | custom-call | flops 1000000000 | bytes 1000000 | tf_op jit(solution)/shard_map/rim_odd/pallas_call | solution.py:479
  18.1 2.4 %collective-permute-start.4 = (bf16[640,128]{1,0:T(8,128)(2,1)S(1)}, bf16[640,128]{1,0:T(8,128)(2,1)S(1)}, u32[]{:S(2)}, u32[]{:S(2)}) collective-permute-start(bf16[640,128]{1,0:T(8,128)(2,1)S(1)} %get-tuple-element.85), channel_id=1, source_target_pairs={{0,1},{1,0},{2,3},{3,2},{4,5},{5,4},{6,7},{7,6},{8,9},{9,8},{10,11... | collective-permute-start | bytes 491528 | tf_op jit(solution)/shard_map/ppermute | solution.py:474
  20.5 2.9 %collective-permute-start.3 = (bf16[640,128]{1,0:T(8,128)(2,1)S(1)}, bf16[640,128]{1,0:T(8,128)(2,1)S(1)}, u32[]{:S(2)}, u32[]{:S(2)}) collective-permute-start(bf16[640,128]{1,0:T(8,128)(2,1)S(1)} %get-tuple-element.84), channel_id=1, source_target_pairs={{0,1},{1,2},{2,3},{3,4},{4,5},{5,6},{6,7},{7,8},{8,9},{9,10},{10,1... | collective-permute-start | bytes 491528 | tf_op jit(solution)/shard_map/ppermute | solution.py:468
  23.4 2.6 %inside.1 = (bf16[45,160,128]{2,1,0:T(8,128)(2,1)S(1)}, bf16[13,240,128]{2,1,0:T(8,128)(2,1)S(1)}, f32[80,1664]{1,0:T(8,128)S(1)}, f32[80,1664]{1,0:T(8,128)S(1)}, f32[80,4992]{1,0:T(8,128)S(1)}) custom-call(bf16[13,240,128]{2,1,0:T(8,128)(2,1)S(1)} %get-tuple-element.86.refs_0_.refs_4_, f32[80,4992]{1,0:T(8,128)S(1)} %get-tuple-element.89.refs_1_.refs_7_, ...), custom_call_target="tpu_custom_call" | custom-call | flops 1000 | bytes 1000 | tf_op jit(solution)/shard_map/inside/pallas_call | solution.py:498
  25.9 0.0 collective-permute-done.5.refs_0_
  25.9 0.0 collective-permute-done.4.refs_1_
  26.0 1.3 %rim_odd.3 = (bf16[45,160,128]{2,1,0:T(8,128)(2,1)S(1)}, bf16[13,240,128]{2,1,0:T(8,128)(2,1)S(1)}, f32[80,1664]{1,0:T(8,128)S(1)}, f32[80,1664]{1,0:T(8,128)S(1...) custom-call(bf16[640,128]{1,0:T(8,128)(2,1)S(1)} %collective-permute, ...), custom_call_target="tpu_custom_call", output_to_operand_aliasing={{0}: (17, {}), {1}: (18, {}), {2}: (19, {}), {3}: (20, {}),... | custom-call | flops 1000000000 | bytes 1000000 | tf_op jit(solution)/shard_map/rim_odd/pallas_call | solution.py:479
  27.2 0.3 collective-permute-start.7
  27.5 0.0 collective-permute-done.3.refs_0_
  27.6 2.9 %collective-permute-start.8 = (bf16[640,128]{1,0:T(8,128)(2,1)S(1)}, bf16[640,128]{1,0:T(8,128)(2,1)S(1)}, u32[]{:S(2)}, u32[]{:S(2)}) collective-permute-start(bf16[640,128]{1,0:T(8,128)(2,1)S(1)} %get-tuple-element.119), channel_id=1, source_target_pairs={{0,255},{1,2},{2,1},{3,0},{4,3},{5,4},{6,5},{7,6},{8,7},{9,10},{10... | collective-permute-start | bytes 491528 | tf_op jit(solution)/shard_map/ppermute | solution.py:471
  30.5 2.3 %odd_inside.3 = (bf16[640,128]{1,0:T(8,128)(2,1)S(1)}, bf16[45,160,128]{2,1,0:T(8,128)(2,1)S(1)}, f32[80,4992]{1,0:T(8,128)S(1)}, f32[80,1664]{1,0:T(8,128)S(1)}, f32[80,1664]{1,0:T(8,128)S(1)}) custom-call(bf16[13,240,128]{2,1,0:T(8,128)(2,1)S(1)} %get-tuple-element.103.refs_0_.refs_6, ...), custom_call_target="tpu_custom_call", output_to_operand_aliasing={{0}: (13, {}), {1}: (14, {}), {2}: (15, {}), {3}: (16, {}),... | custom-call | flops 1000 | bytes 1000 | tf_op jit(solution)/shard_map/odd_inside/pallas_call | solution.py:498
  32.9 0.1 collective-permute-start.6
  33.0 0.0 collective-permute-done.7.refs_0_.refs_1_
  33.0 0.8 %collective-permute-done.8.refs_0_.refs_2_ = bf16[640,128]{1,0:T(8,128)(2,1)S(1)} collective-permute-done((bf16[640,128]{1,0:T(8,128)(2,1)S(1)}, bf16[640,128]{1,0:T(8,128)(2,1)S(1)}, u32[]{:S(2)}, u32[]{:S(2)}) %collective-permute-start.8) | collective-permute-done | bytes 163872 | tf_op jit(solution)/shard_map/ppermute | solution.py:471
  33.8 0.5 %collective-permute-done.6.refs_0_ = bf16[640,128]{1,0:T(8,128)(2,1)S(1)} collective-permute-done((bf16[640,128]{1,0:T(8,128)(2,1)S(1)}, bf16[640,128]{1,0:T(8,128)(2,1)S(1)}, u32[]{:S(2)}, u32[]{:S(2)}) %collective-permute-start.6) | collective-permute-done | bytes 163872 | tf_op jit(solution)/shard_map/ppermute | solution.py:474
  34.3 1.7 %rim.1 = (bf16[45,160,128]{2,1,0:T(8,128)(2,1)S(1)}, f32[80,1664]{1,0:T(8,128)S(1)}, f32[80,1664]{1,0:T(8,128)S(1)}, f32[80,4992]{1,0:T(8,128)S(1)}, f32[80,1664...) custom-call(bf16[640,128]{1,0:T(8,128)(2,1)S(1)} %collective-permute, ...), custom_call_target="tpu_custom_call", output_to_operand_aliasing={{0}: (19, {}), {1}: (20, {}), {2}: (21, {}), {3}: (22, {})} | custom-call | flops 1000 | bytes 1000 | tf_op jit(solution)/shard_map/rim/pallas_call | solution.py:574
  (21 shorter events, 0.2 us)
Async XLA Ops:
  0.6 13.3 %copy-start = (bf16[39,2,128,128]{3,2,1,0:T(8,128)(2,1)S(1)}, bf16[39,2,128,128]{3,2,1,0:T(8,128)(2,1)}, u32[]{:S(2)}) copy-start(bf16[39,2,128,128]{3,2,1,0:T(8,128)(2,1)} %param.14) | copy-start | bytes 7667716
  0.6 13.3 %copy-start.1 = (bf16[39,2,128,128]{3,2,1,0:T(8,128)(2,1)S(1)}, bf16[39,2,128,128]{3,2,1,0:T(8,128)(2,1)}, u32[]{:S(2)}) copy-start(bf16[39,2,128,128]{3,2,1,0:T(8,128)(2,1)} %param.13) | copy-start | bytes 7667716
  0.7 13.3 %copy-start.2 = (bf16[13,6,128,128]{3,2,1,0:T(8,128)(2,1)S(1)}, bf16[13,6,128,128]{3,2,1,0:T(8,128)(2,1)}, u32[]{:S(2)}) copy-start(bf16[13,6,128,128]{3,2,1,0:T(8,128)(2,1)} %param.16) | copy-start | bytes 7667716
  0.7 13.3 %copy-start.3 = (f32[80,4992]{1,0:T(8,128)S(1)}, f32[80,4992]{1,0:T(8,128)}, u32[]{:S(2)}) copy-start(f32[80,4992]{1,0:T(8,128)} %refs_12_.1) | copy-start | bytes 4792324
  0.7 13.3 %copy-start.4 = (f32[80,1664]{1,0:T(8,128)S(1)}, f32[80,1664]{1,0:T(8,128)}, u32[]{:S(2)}) copy-start(f32[80,1664]{1,0:T(8,128)} %refs_10_.19) | copy-start | bytes 1597444
  0.7 13.3 %copy-start.5 = (f32[80,1664]{1,0:T(8,128)S(1)}, f32[80,1664]{1,0:T(8,128)}, u32[]{:S(2)}) copy-start(f32[80,1664]{1,0:T(8,128)} %refs_11_.1) | copy-start | bytes 1597444
  2.4 14.3 %collective-permute-start.2 = (bf16[1424,128]{1,0:T(8,128)(2,1)S(1)}, bf16[1424,128]{1,0:T(8,128)(2,1)S(1)}, u32[]{:S(2)}, u32[]{:S(2)}) collective-permute-start(bf16[1424,128]{1,0:T(8,128)(2,1)S(1)} %get-tuple-element.67), channel_id=1, source_target_pairs={{0,1},{1,2},{2,3},{3,4},{4,5},{5,6},{6,7},{7,8},{8,9},{9,10},{10,1... | collective-permute-start | bytes 1093640 | tf_op jit(solution)/shard_map/ppermute | solution.py:510
  5.0 11.8 %collective-permute-start = (bf16[1424,128]{1,0:T(8,128)(2,1)S(1)}, bf16[1424,128]{1,0:T(8,128)(2,1)S(1)}, u32[]{:S(2)}, u32[]{:S(2)}) collective-permute-start(bf16[1424,128]{1,0:T(8,128)(2,1)S(1)} %get-tuple-element.67), channel_id=1, source_target_pairs={{1,0},{2,1},{3,2},{4,3},{5,4},{6,5},{7,6},{8,7},{9,8},{10,9},{11,1... | collective-permute-start | bytes 1093640 | tf_op jit(solution)/shard_map/ppermute | solution.py:510
  5.8 10.9 %collective-permute-start.1 = (bf16[1424,128]{1,0:T(8,128)(2,1)S(1)}, bf16[1424,128]{1,0:T(8,128)(2,1)S(1)}, u32[]{:S(2)}, u32[]{:S(2)}) collective-permute-start(bf16[1424,128]{1,0:T(8,128)(2,1)S(1)} %get-tuple-element.68), channel_id=1, source_target_pairs={{0,1},{1,0},{2,3},{3,2},{4,5},{5,4},{6,7},{7,6},{8,9},{9,8},{10,11... | collective-permute-start | bytes 1093640 | tf_op jit(solution)/shard_map/ppermute | solution.py:474
  16.7 9.2 %collective-permute-start.5 = (bf16[640,128]{1,0:T(8,128)(2,1)S(1)}, bf16[640,128]{1,0:T(8,128)(2,1)S(1)}, u32[]{:S(2)}, u32[]{:S(2)}) collective-permute-start(bf16[640,128]{1,0:T(8,128)(2,1)S(1)} %get-tuple-element.90), channel_id=1, source_target_pairs={{0,255},{1,2},{2,1},{3,0},{4,3},{5,4},{6,5},{7,6},{8,7},{9,10},{10... | collective-permute-start | bytes 491528 | tf_op jit(solution)/shard_map/ppermute | solution.py:471
  18.1 7.9 %collective-permute-start.4 = (bf16[640,128]{1,0:T(8,128)(2,1)S(1)}, bf16[640,128]{1,0:T(8,128)(2,1)S(1)}, u32[]{:S(2)}, u32[]{:S(2)}) collective-permute-start(bf16[640,128]{1,0:T(8,128)(2,1)S(1)} %get-tuple-element.85), channel_id=1, source_target_pairs={{0,1},{1,0},{2,3},{3,2},{4,5},{5,4},{6,7},{7,6},{8,9},{9,8},{10,11... | collective-permute-start | bytes 491528 | tf_op jit(solution)/shard_map/ppermute | solution.py:474
  20.5 7.0 %collective-permute-start.3 = (bf16[640,128]{1,0:T(8,128)(2,1)S(1)}, bf16[640,128]{1,0:T(8,128)(2,1)S(1)}, u32[]{:S(2)}, u32[]{:S(2)}) collective-permute-start(bf16[640,128]{1,0:T(8,128)(2,1)S(1)} %get-tuple-element.84), channel_id=1, source_target_pairs={{0,1},{1,2},{2,3},{3,4},{4,5},{5,6},{6,7},{7,8},{8,9},{9,10},{10,1... | collective-permute-start | bytes 491528 | tf_op jit(solution)/shard_map/ppermute | solution.py:468
  27.2 5.8 %collective-permute-start.7 = (bf16[640,128]{1,0:T(8,128)(2,1)S(1)}, bf16[640,128]{1,0:T(8,128)(2,1)S(1)}, u32[]{:S(2)}, u32[]{:S(2)}) collective-permute-start(bf16[640,128]{1,0:T(8,128)(2,1)S(1)} %get-tuple-element.118), channel_id=1, source_target_pairs={{0,1},{1,2},{2,3},{3,4},{4,5},{5,6},{6,7},{7,8},{8,9},{9,10},{10,1... | collective-permute-start | bytes 491528 | tf_op jit(solution)/shard_map/ppermute | solution.py:468
  27.6 6.2 %collective-permute-start.8 = (bf16[640,128]{1,0:T(8,128)(2,1)S(1)}, bf16[640,128]{1,0:T(8,128)(2,1)S(1)}, u32[]{:S(2)}, u32[]{:S(2)}) collective-permute-start(bf16[640,128]{1,0:T(8,128)(2,1)S(1)} %get-tuple-element.119), channel_id=1, source_target_pairs={{0,255},{1,2},{2,1},{3,0},{4,3},{5,4},{6,5},{7,6},{8,7},{9,10},{10... | collective-permute-start | bytes 491528 | tf_op jit(solution)/shard_map/ppermute | solution.py:471
  32.9 1.5 %collective-permute-start.6 = (bf16[640,128]{1,0:T(8,128)(2,1)S(1)}, bf16[640,128]{1,0:T(8,128)(2,1)S(1)}, u32[]{:S(2)}, u32[]{:S(2)}) collective-permute-start(bf16[640,128]{1,0:T(8,128)(2,1)S(1)} %get-tuple-element.117), channel_id=1, source_target_pairs={{0,1},{1,0},{2,3},{3,2},{4,5},{5,4},{6,7},{7,6},{8,9},{9,8},{10,11... | collective-permute-start | bytes 491528 | tf_op jit(solution)/shard_map/ppermute | solution.py:474

commit v6 on v5

--- a/solution.py
+++ b/solution.py
@@ -118,16 +118,16 @@
         pltpu.make_async_copy(edge_sources, edge_sources_out, sems.at[1]),
         pltpu.make_async_copy(cell_sources, cell_sources_out, sems.at[2]),
     ]
-    fields, tiles = [], []
+    fields, speeds, tiles = [], [], []
     for p, side, block, after in ends:
         for k, b in ((0, block), (1, after)):
             fields.append(pltpu.make_async_copy(thickness.at[:, columns(b, TILE)], h.at[p, k], sems.at[3 + 4 * p + 2 * k]))
             fields.append(pltpu.make_async_copy(tracer.at[:, columns(b, TILE)], s.at[p, k], sems.at[4 + 4 * p + 2 * k]))
-        fields.append(pltpu.make_async_copy(velocity.at[:, columns(3 * block, 3 * TILE)], v.at[p], sems.at[11 + p]))
+        speeds.append(pltpu.make_async_copy(velocity.at[:, columns(3 * block, 3 * TILE)], v.at[p], sems.at[11 + p]))
         message = (inner, outer)[p]
         rows = pl.ds(pl.multiple_of(block * 6 * TILE, 6 * TILE), 6 * TILE)
         tiles.append(pltpu.make_async_copy(average.at[rows, :], message.at[pl.ds(SIDE, 6 * TILE), :], sems.at[13 + p]))
-    for copy in small + fields + tiles:
+    for copy in small + fields + speeds + tiles:
         copy.start()
     above = above_weights()
     for copy in small:
@@ -141,6 +141,8 @@
         depth = lax.broadcasted_iota(jnp.int32, (LEV, TILE), 0)
         done.append((h[p, 0], s[p, 0], (depth < levels_out[pl.ds(block, 1), :]).astype(F32)))
     pressures = pressure_of(done, above)
+    for copy in speeds:
+        copy.wait()
     for p, side, block, after in ends:
         message = (inner, outer)[p]
         mask = done[p][2]

time: 36.3 us -> 36.3 us (level)
  no operation moved by 1% of the time
where the time goes in v6:
time: 36.3 us; the launch traced here: 36.2 us
  starting transfers between devices  20.3 us (56%)
  Pallas kernels  13.5 us (37%)
  waiting for transfers between devices  1.35 us (4%)
  between operations  1.03 us (3%)
    ppermute x3, starting transfers between devices, swap_inner(): return lax.ppermute(x, 'dom', within)  10.7 us
    pallas_call x9, Pallas kernels, call(): pl.pallas_call(lambda *refs: body(own, keep_share, *refs[:n], *refs[n + l...  7.64 us
    ppermute x2, starting transfers between devices, send_up(): return lax.ppermute(x, 'dom', upward)  3.15 us
    ppermute x2, starting transfers between devices, send_down(): return lax.ppermute(x, 'dom', downward)  2.99 us
    ppermute x1, starting transfers between devices, local(): lax.ppermute(outer, 'dom', upward)  2.68 us
    pallas_call x4, Pallas kernels, rim(): pl.pallas_call(lambda *refs: rim_kernel(odd, second, own, keep_share, *re...  2.57 us
    pallas_call x1, Pallas kernels, local(): pl.pallas_call(lambda *refs: last_rim_kernel(own, keep_shares[2], *refs),...  1.71 us
    pallas_call x1, Pallas kernels, local(): pl.pallas_call(lambda *refs: start_kernel(own, *refs), out_shape=(message...  1.62 us
  transfers between devices with their start and end apart: 9, of which 2 were waited for; matrix products, arithmetic and copies ran while one was open for 0% of the time, Pallas kernels for 28%

profile of v6, /device:TPU:1, one launch (start us, length us, event | category | flops | bytes accessed | tf_op | source)
XLA Modules:
  0.0 36.2 jit_solution(10509327731852062422)
XLA Ops:
  0.7 1.6 %start.1 = (bf16[1424,128]{1,0:T(8,128)(2,1)S(1)}, bf16[1424,128]{1,0:T(8,128)(2,1)S(1)}, s32[13,128]{1,0:T(8,128)S(1)}, s32[2,39]{1,0:T(2,128)S(1)}, s32[6,13]{1,0:T(8,128)S(1)}) custom-call(f32[80,1664]{1,0:T(8,128)} %refs_10_.19, f32[80,1664]{1,0:T(8,128)} %refs_11_.1, f32[80,4992]{1,0:T(8,128)} %refs_12_.1, s32[1664]{0:T(1024)} %refs_3_.1, ...), custom_call_target="tpu_custom_call" | custom-call | flops 20000000000 | bytes 1000000 | tf_op jit(solution)/shard_map/start/pallas_call | solution.py:436
  2.3 2.7 %collective-permute-start.2 = (bf16[1424,128]{1,0:T(8,128)(2,1)S(1)}, bf16[1424,128]{1,0:T(8,128)(2,1)S(1)}, u32[]{:S(2)}, u32[]{:S(2)}) collective-permute-start(bf16[1424,128]{1,0:T(8,128)(2,1)S(1)} %get-tuple-element.67), channel_id=1, source_target_pairs={{0,1},{1,2},{2,3},{3,4},{4,5},{5,6},{6,7},{7,8},{8,9},{9,10},{10,1... | collective-permute-start | bytes 1093640 | tf_op jit(solution)/shard_map/ppermute | solution.py:512
  5.0 0.7 %collective-permute-start = (bf16[1424,128]{1,0:T(8,128)(2,1)S(1)}, bf16[1424,128]{1,0:T(8,128)(2,1)S(1)}, u32[]{:S(2)}, u32[]{:S(2)}) collective-permute-start(bf16[1424,128]{1,0:T(8,128)(2,1)S(1)} %get-tuple-element.67), channel_id=1, source_target_pairs={{1,0},{2,1},{3,2},{4,3},{5,4},{6,5},{7,6},{8,7},{9,8},{10,9},{11,1... | collective-permute-start | bytes 1093640 | tf_op jit(solution)/shard_map/ppermute | solution.py:512
  5.7 8.2 %collective-permute-start.1 = (bf16[1424,128]{1,0:T(8,128)(2,1)S(1)}, bf16[1424,128]{1,0:T(8,128)(2,1)S(1)}, u32[]{:S(2)}, u32[]{:S(2)}) collective-permute-start(bf16[1424,128]{1,0:T(8,128)(2,1)S(1)} %get-tuple-element.68), channel_id=1, source_target_pairs={{0,1},{1,0},{2,3},{3,2},{4,5},{5,4},{6,7},{7,6},{8,9},{9,8},{10,11... | collective-permute-start | bytes 1093640 | tf_op jit(solution)/shard_map/ppermute | solution.py:476
  14.0 2.7 %first_inside.1 = (bf16[45,160,128]{2,1,0:T(8,128)(2,1)S(1)}, bf16[13,240,128]{2,1,0:T(8,128)(2,1)S(1)}, f32[80,1664]{1,0:T(8,128)S(1)}, f32[80,1664]{1,0:T(8,12...) custom-call(f32[80,1664]{1,0:T(8,128)S(1)} %copy-done.4, f32[80,1664]{1,0:T(8,128)S(1)} %copy-done.5, ...), custom_call_target="tpu_custom_call" | custom-call | flops 10000000000 | bytes 10000000 | tf_op jit(solution)/shard_map/first_inside/pallas_call | solution.py:500
  16.6 0.0 collective-permute-done.1.refs_1_.refs_3_
  16.6 0.0 collective-permute-done.2.refs_0_.refs_2_.refs_4_
  16.7 0.1 collective-permute-start.5
  16.8 0.0 collective-permute-done.refs_0_.refs_2_.refs_5_
  16.8 1.2 %rim_odd.2 = (bf16[45,160,128]{2,1,0:T(8,128)(2,1)S(1)}, bf16[13,240,128]{2,1,0:T(8,128)(2,1)S(1)}, f32[80,1664]{1,0:T(8,128)S(1)}, f32[80,1664]{1,0:T(8,128)S(1...) custom-call(bf16[1424,128]{1,0:T(8,128)(2,1)S(1)} %collective-permut, ...), custom_call_target="tpu_custom_call", output_to_operand_aliasing={{0}: (17, {}), {1}: (18, {}), {2}: (19, {}), {3}: (20, {}),... | custom-call | flops 1000000000 | bytes 1000000 | tf_op jit(solution)/shard_map/rim_odd/pallas_call | solution.py:481
  18.0 2.4 %collective-permute-start.4 = (bf16[640,128]{1,0:T(8,128)(2,1)S(1)}, bf16[640,128]{1,0:T(8,128)(2,1)S(1)}, u32[]{:S(2)}, u32[]{:S(2)}) collective-permute-start(bf16[640,128]{1,0:T(8,128)(2,1)S(1)} %get-tuple-element.85), channel_id=1, source_target_pairs={{0,1},{1,0},{2,3},{3,2},{4,5},{5,4},{6,7},{7,6},{8,9},{9,8},{10,11... | collective-permute-start | bytes 491528 | tf_op jit(solution)/shard_map/ppermute | solution.py:476
  20.4 2.9 %collective-permute-start.3 = (bf16[640,128]{1,0:T(8,128)(2,1)S(1)}, bf16[640,128]{1,0:T(8,128)(2,1)S(1)}, u32[]{:S(2)}, u32[]{:S(2)}) collective-permute-start(bf16[640,128]{1,0:T(8,128)(2,1)S(1)} %get-tuple-element.84), channel_id=1, source_target_pairs={{0,1},{1,2},{2,3},{3,4},{4,5},{5,6},{6,7},{7,8},{8,9},{9,10},{10,1... | collective-permute-start | bytes 491528 | tf_op jit(solution)/shard_map/ppermute | solution.py:470
  23.3 2.6 %inside.1 = (bf16[45,160,128]{2,1,0:T(8,128)(2,1)S(1)}, bf16[13,240,128]{2,1,0:T(8,128)(2,1)S(1)}, f32[80,1664]{1,0:T(8,128)S(1)}, f32[80,1664]{1,0:T(8,128)S(1)}, f32[80,4992]{1,0:T(8,128)S(1)}) custom-call(bf16[13,240,128]{2,1,0:T(8,128)(2,1)S(1)} %get-tuple-element.86.refs_0_.refs_4_, f32[80,4992]{1,0:T(8,128)S(1)} %get-tuple-element.89.refs_1_.refs_7_, ...), custom_call_target="tpu_custom_call" | custom-call | flops 1000 | bytes 1000 | tf_op jit(solution)/shard_map/inside/pallas_call | solution.py:500
  25.9 0.0 collective-permute-done.5.refs_0_
  25.9 1.3 %rim_odd.3 = (bf16[45,160,128]{2,1,0:T(8,128)(2,1)S(1)}, bf16[13,240,128]{2,1,0:T(8,128)(2,1)S(1)}, f32[80,1664]{1,0:T(8,128)S(1)}, f32[80,1664]{1,0:T(8,128)S(1...) custom-call(bf16[640,128]{1,0:T(8,128)(2,1)S(1)} %collective-permute, ...), custom_call_target="tpu_custom_call", output_to_operand_aliasing={{0}: (17, {}), {1}: (18, {}), {2}: (19, {}), {3}: (20, {}),... | custom-call | flops 1000000000 | bytes 1000000 | tf_op jit(solution)/shard_map/rim_odd/pallas_call | solution.py:481
  27.2 0.3 collective-permute-start.7
  27.5 0.0 collective-permute-done.3.refs_0_
  27.6 2.9 %collective-permute-start.8 = (bf16[640,128]{1,0:T(8,128)(2,1)S(1)}, bf16[640,128]{1,0:T(8,128)(2,1)S(1)}, u32[]{:S(2)}, u32[]{:S(2)}) collective-permute-start(bf16[640,128]{1,0:T(8,128)(2,1)S(1)} %get-tuple-element.119), channel_id=1, source_target_pairs={{0,255},{1,2},{2,1},{3,0},{4,3},{5,4},{6,5},{7,6},{8,7},{9,10},{10... | collective-permute-start | bytes 491528 | tf_op jit(solution)/shard_map/ppermute | solution.py:473
  30.5 2.3 %odd_inside.3 = (bf16[640,128]{1,0:T(8,128)(2,1)S(1)}, bf16[45,160,128]{2,1,0:T(8,128)(2,1)S(1)}, f32[80,4992]{1,0:T(8,128)S(1)}, f32[80,1664]{1,0:T(8,128)S(1)}, f32[80,1664]{1,0:T(8,128)S(1)}) custom-call(bf16[13,240,128]{2,1,0:T(8,128)(2,1)S(1)} %get-tuple-element.103.refs_0_.refs_6, ...), custom_call_target="tpu_custom_call", output_to_operand_aliasing={{0}: (13, {}), {1}: (14, {}), {2}: (15, {}), {3}: (16, {}),... | custom-call | flops 1000 | bytes 1000 | tf_op jit(solution)/shard_map/odd_inside/pallas_call | solution.py:500
  32.9 0.1 collective-permute-start.6
  33.0 0.0 collective-permute-done.7.refs_0_.refs_1_
  33.0 0.8 %collective-permute-done.8.refs_0_.refs_2_ = bf16[640,128]{1,0:T(8,128)(2,1)S(1)} collective-permute-done((bf16[640,128]{1,0:T(8,128)(2,1)S(1)}, bf16[640,128]{1,0:T(8,128)(2,1)S(1)}, u32[]{:S(2)}, u32[]{:S(2)}) %collective-permute-start.8) | collective-permute-done | bytes 163872 | tf_op jit(solution)/shard_map/ppermute | solution.py:473
  33.8 0.5 %collective-permute-done.6.refs_0_ = bf16[640,128]{1,0:T(8,128)(2,1)S(1)} collective-permute-done((bf16[640,128]{1,0:T(8,128)(2,1)S(1)}, bf16[640,128]{1,0:T(8,128)(2,1)S(1)}, u32[]{:S(2)}, u32[]{:S(2)}) %collective-permute-start.6) | collective-permute-done | bytes 163872 | tf_op jit(solution)/shard_map/ppermute | solution.py:476
  34.3 1.7 %rim.1 = (bf16[45,160,128]{2,1,0:T(8,128)(2,1)S(1)}, f32[80,1664]{1,0:T(8,128)S(1)}, f32[80,1664]{1,0:T(8,128)S(1)}, f32[80,4992]{1,0:T(8,128)S(1)}, f32[80,1664...) custom-call(bf16[640,128]{1,0:T(8,128)(2,1)S(1)} %collective-permute, ...), custom_call_target="tpu_custom_call", output_to_operand_aliasing={{0}: (19, {}), {1}: (20, {}), {2}: (21, {}), {3}: (22, {})} | custom-call | flops 1000 | bytes 1000 | tf_op jit(solution)/shard_map/rim/pallas_call | solution.py:576
  (21 shorter events, 0.2 us)
Async XLA Ops:
  0.6 13.3 %copy-start = (bf16[39,2,128,128]{3,2,1,0:T(8,128)(2,1)S(1)}, bf16[39,2,128,128]{3,2,1,0:T(8,128)(2,1)}, u32[]{:S(2)}) copy-start(bf16[39,2,128,128]{3,2,1,0:T(8,128)(2,1)} %param.14) | copy-start | bytes 7667716
  0.6 13.3 %copy-start.1 = (bf16[39,2,128,128]{3,2,1,0:T(8,128)(2,1)S(1)}, bf16[39,2,128,128]{3,2,1,0:T(8,128)(2,1)}, u32[]{:S(2)}) copy-start(bf16[39,2,128,128]{3,2,1,0:T(8,128)(2,1)} %param.13) | copy-start | bytes 7667716
  0.7 13.3 %copy-start.2 = (bf16[13,6,128,128]{3,2,1,0:T(8,128)(2,1)S(1)}, bf16[13,6,128,128]{3,2,1,0:T(8,128)(2,1)}, u32[]{:S(2)}) copy-start(bf16[13,6,128,128]{3,2,1,0:T(8,128)(2,1)} %param.16) | copy-start | bytes 7667716
  0.7 13.3 %copy-start.3 = (f32[80,4992]{1,0:T(8,128)S(1)}, f32[80,4992]{1,0:T(8,128)}, u32[]{:S(2)}) copy-start(f32[80,4992]{1,0:T(8,128)} %refs_12_.1) | copy-start | bytes 4792324
  0.7 13.3 %copy-start.4 = (f32[80,1664]{1,0:T(8,128)S(1)}, f32[80,1664]{1,0:T(8,128)}, u32[]{:S(2)}) copy-start(f32[80,1664]{1,0:T(8,128)} %refs_10_.19) | copy-start | bytes 1597444
  0.7 13.3 %copy-start.5 = (f32[80,1664]{1,0:T(8,128)S(1)}, f32[80,1664]{1,0:T(8,128)}, u32[]{:S(2)}) copy-start(f32[80,1664]{1,0:T(8,128)} %refs_11_.1) | copy-start | bytes 1597444
  2.3 14.3 %collective-permute-start.2 = (bf16[1424,128]{1,0:T(8,128)(2,1)S(1)}, bf16[1424,128]{1,0:T(8,128)(2,1)S(1)}, u32[]{:S(2)}, u32[]{:S(2)}) collective-permute-start(bf16[1424,128]{1,0:T(8,128)(2,1)S(1)} %get-tuple-element.67), channel_id=1, source_target_pairs={{0,1},{1,2},{2,3},{3,4},{4,5},{5,6},{6,7},{7,8},{8,9},{9,10},{10,1... | collective-permute-start | bytes 1093640 | tf_op jit(solution)/shard_map/ppermute | solution.py:512
  5.0 11.8 %collective-permute-start = (bf16[1424,128]{1,0:T(8,128)(2,1)S(1)}, bf16[1424,128]{1,0:T(8,128)(2,1)S(1)}, u32[]{:S(2)}, u32[]{:S(2)}) collective-permute-start(bf16[1424,128]{1,0:T(8,128)(2,1)S(1)} %get-tuple-element.67), channel_id=1, source_target_pairs={{1,0},{2,1},{3,2},{4,3},{5,4},{6,5},{7,6},{8,7},{9,8},{10,9},{11,1... | collective-permute-start | bytes 1093640 | tf_op jit(solution)/shard_map/ppermute | solution.py:512
  5.7 10.9 %collective-permute-start.1 = (bf16[1424,128]{1,0:T(8,128)(2,1)S(1)}, bf16[1424,128]{1,0:T(8,128)(2,1)S(1)}, u32[]{:S(2)}, u32[]{:S(2)}) collective-permute-start(bf16[1424,128]{1,0:T(8,128)(2,1)S(1)} %get-tuple-element.68), channel_id=1, source_target_pairs={{0,1},{1,0},{2,3},{3,2},{4,5},{5,4},{6,7},{7,6},{8,9},{9,8},{10,11... | collective-permute-start | bytes 1093640 | tf_op jit(solution)/shard_map/ppermute | solution.py:476
  16.7 9.2 %collective-permute-start.5 = (bf16[640,128]{1,0:T(8,128)(2,1)S(1)}, bf16[640,128]{1,0:T(8,128)(2,1)S(1)}, u32[]{:S(2)}, u32[]{:S(2)}) collective-permute-start(bf16[640,128]{1,0:T(8,128)(2,1)S(1)} %get-tuple-element.90), channel_id=1, source_target_pairs={{0,255},{1,2},{2,1},{3,0},{4,3},{5,4},{6,5},{7,6},{8,7},{9,10},{10... | collective-permute-start | bytes 491528 | tf_op jit(solution)/shard_map/ppermute | solution.py:473
  18.0 7.9 %collective-permute-start.4 = (bf16[640,128]{1,0:T(8,128)(2,1)S(1)}, bf16[640,128]{1,0:T(8,128)(2,1)S(1)}, u32[]{:S(2)}, u32[]{:S(2)}) collective-permute-start(bf16[640,128]{1,0:T(8,128)(2,1)S(1)} %get-tuple-element.85), channel_id=1, source_target_pairs={{0,1},{1,0},{2,3},{3,2},{4,5},{5,4},{6,7},{7,6},{8,9},{9,8},{10,11... | collective-permute-start | bytes 491528 | tf_op jit(solution)/shard_map/ppermute | solution.py:476
  20.4 7.1 %collective-permute-start.3 = (bf16[640,128]{1,0:T(8,128)(2,1)S(1)}, bf16[640,128]{1,0:T(8,128)(2,1)S(1)}, u32[]{:S(2)}, u32[]{:S(2)}) collective-permute-start(bf16[640,128]{1,0:T(8,128)(2,1)S(1)} %get-tuple-element.84), channel_id=1, source_target_pairs={{0,1},{1,2},{2,3},{3,4},{4,5},{5,6},{6,7},{7,8},{8,9},{9,10},{10,1... | collective-permute-start | bytes 491528 | tf_op jit(solution)/shard_map/ppermute | solution.py:470
  27.2 5.8 %collective-permute-start.7 = (bf16[640,128]{1,0:T(8,128)(2,1)S(1)}, bf16[640,128]{1,0:T(8,128)(2,1)S(1)}, u32[]{:S(2)}, u32[]{:S(2)}) collective-permute-start(bf16[640,128]{1,0:T(8,128)(2,1)S(1)} %get-tuple-element.118), channel_id=1, source_target_pairs={{0,1},{1,2},{2,3},{3,4},{4,5},{5,6},{6,7},{7,8},{8,9},{9,10},{10,1... | collective-permute-start | bytes 491528 | tf_op jit(solution)/shard_map/ppermute | solution.py:470
  27.6 6.2 %collective-permute-start.8 = (bf16[640,128]{1,0:T(8,128)(2,1)S(1)}, bf16[640,128]{1,0:T(8,128)(2,1)S(1)}, u32[]{:S(2)}, u32[]{:S(2)}) collective-permute-start(bf16[640,128]{1,0:T(8,128)(2,1)S(1)} %get-tuple-element.119), channel_id=1, source_target_pairs={{0,255},{1,2},{2,1},{3,0},{4,3},{5,4},{6,5},{7,6},{8,7},{9,10},{10... | collective-permute-start | bytes 491528 | tf_op jit(solution)/shard_map/ppermute | solution.py:473
  32.9 1.5 %collective-permute-start.6 = (bf16[640,128]{1,0:T(8,128)(2,1)S(1)}, bf16[640,128]{1,0:T(8,128)(2,1)S(1)}, u32[]{:S(2)}, u32[]{:S(2)}) collective-permute-start(bf16[640,128]{1,0:T(8,128)(2,1)S(1)} %get-tuple-element.117), channel_id=1, source_target_pairs={{0,1},{1,0},{2,3},{3,2},{4,5},{5,4},{6,7},{7,6},{8,9},{9,8},{10,11... | collective-permute-start | bytes 491528 | tf_op jit(solution)/shard_map/ppermute | solution.py:476
